TPU v7x, 128 devices: a whole 4x4x4 slice. The times are simulated.
128 devices in a mesh: tile: 16 (over z_hi, y, core), chan: 8 (over z_lo, x).
Axes of the slice: x: 4, y: 4, z: 4 (z_hi: 2, z_lo: 2; z = z_hi * 2 + z_lo), core: 2. Of those that a mesh axis runs over, the one named last changes fastest.
Arguments:
- features: bfloat16 [2, 96, 144, 2048], P(None, 'tile', 'chan'), may hold values from -6 to 6
- atrous_weight: bfloat16 [3, 3, 3, 2048, 256], P(None, None, None, 'tile', 'chan'), may hold values from -0.046875 to 0.046875
- point_weight: bfloat16 [2048, 256], P('tile', 'chan'), may hold values from -0.125 to 0.125
- branch_shift: float32 [4, 256], P(None, 'chan'), may hold values from -3 to 3
- proj_weight: bfloat16 [1024, 256], replicated, may hold values from -0.25 to 0.25
- class_weight: bfloat16 [256, 3], replicated, may hold values from -0.75 to 0.75
- labels: int32 [2, 96, 144], P(None, 'tile', 'chan'), may hold values from 0 to 2
Outputs:
- projected: bfloat16 [2, 96, 144, 256], P(None, 'tile', 'chan')
- pixel_loss: float32 [2, 96, 144], P(None, 'tile', 'chan')
All inputs are finite; a program needn't handle non-finite values.
Results may differ from a plain program's by a relative error of at most 0.0049.
Values may be sent and summed in bfloat16 or wider, within the bound.
No kernel may reach another device: no remote copies, remote signals or barrier semaphores. Data moves between devices by JAX's collectives and lax.ppermute only.
A program may use at most 320 MiB of HBM per device.

v0:
```python
import jax
import jax.numpy as jnp
from jax import lax
from jax.sharding import PartitionSpec as P


def body(features, atrous_weight, point_weight, branch_shift, proj_weight, class_weight, labels):
    samples = features.shape[0]
    tile_rows = features.shape[1]
    tile_cols = features.shape[2]
    group = branch_shift.shape[1]
    row_strip = lax.all_gather(features, "chan", axis=2, tiled=True)
    whole = lax.all_to_all(row_strip, "tile", split_axis=3, concat_axis=1, tiled=True)
    width = whole.shape[2]
    row_major = whole.transpose(1, 0, 2, 3)
    padded = jnp.pad(row_major, ((36, 36), (0, 0), (36, 36), (0, 0)))
    center = padded[36 : 36 + tile_rows * lax.axis_size("tile"), :, 36 : 36 + width]
    first = jnp.einsum("sg,rbws->grbw", point_weight, center, preferred_element_type=jnp.float32)
    pieces = []
    for index, spacing in enumerate((12, 24, 36)):
        total = jnp.zeros((group, tile_rows * lax.axis_size("tile"), samples, width), jnp.float32)
        for tap_row in range(3):
            for tap_col in range(3):
                row_start = 36 + (tap_row - 1) * spacing
                col_start = 36 + (tap_col - 1) * spacing
                region = padded[
                    row_start : row_start + tile_rows * lax.axis_size("tile"),
                    :,
                    col_start : col_start + width,
                ]
                total = total + jnp.einsum(
                    "sg,rbws->grbw",
                    atrous_weight[index, tap_row, tap_col],
                    region,
                    preferred_element_type=jnp.float32,
                )
        pieces.append(total)
    joined = jnp.concatenate([first] + pieces, axis=0)
    sums = lax.psum_scatter(joined.transpose(1, 2, 3, 0), "tile", scatter_dimension=0, tiled=True)
    pyramid = jax.nn.relu(sums + branch_shift.reshape(-1)).astype(jnp.bfloat16)
    grouped = pyramid.reshape(tile_rows, samples, width, 4, 1, group)
    arrived = lax.all_to_all(grouped, "chan", split_axis=2, concat_axis=4, tiled=True)
    stacked = arrived.transpose(1, 0, 2, 3, 4, 5).reshape(samples * tile_rows * tile_cols, -1)
    mixed = jnp.dot(stacked, proj_weight, preferred_element_type=jnp.float32)
    projected = jax.nn.relu(mixed).astype(jnp.bfloat16)
    logits = jnp.dot(projected, class_weight, preferred_element_type=jnp.float32)
    total = jnp.log(jnp.sum(jnp.exp(logits), axis=-1))
    chosen = jnp.sum(
        jnp.where(labels.reshape(-1, 1) == jnp.arange(3, dtype=jnp.int32), logits, 0.0), axis=-1
    )
    pixel_loss = (total - chosen).reshape(samples, tile_rows, tile_cols)
    return (projected.reshape(samples, tile_rows, tile_cols, -1), pixel_loss)


def solution(mesh):
    return jax.shard_map(
        body,
        mesh=mesh,
        in_specs=(
            P(None, "tile", "chan", None),
            P(None, None, None, "tile", "chan"),
            P("tile", "chan"),
            P(None, "chan"),
            P(),
            P(),
            P(None, "tile", "chan"),
        ),
        out_specs=(P(None, "tile", "chan", None), P(None, "tile", "chan")),
        check_vma=False,
    )
```

profile of v0, /device:TPU:0, one launch (start us, length us, event | category | flops | bytes accessed | tf_op | source)
XLA Modules:
  0.0 691.1 jit_solution(6738896489579111701)
XLA Ops:
  10.3 82.2 %all-gather.2.cloned.1.call-done = bf16[2,6,144,2048]{3,0,1,2:T(2,128)(2,1)} async-done(((bf16[2,6,18,2048]{3,0,1,2:T(2,128)(2,1)}), bf16[2,6,144,2048]{3,0,1,2:T(2,128)(2,1)}) %all-gather.2.cloned.1.call-update) | async-done | bytes 7077904 | tf_op jit(solution)/shard_map/all_gather | solution.py:12
  92.5 27.9 %copy.215 = bf16[2,6,144,2048]{2,1,0,3:T(8,128)(2,1)} copy(bf16[2,6,144,2048]{3,0,1,2:T(2,128)(2,1)} %all-gather.2.cloned.1.call-done) | data formatting | bytes 14155776 | tf_op jit(solution)/shard_map/all_gather | solution.py:12
  120.4 23.7 %reshape.52 = bf16[16,2,110592]{2,1,0:T(2,128)(2,1)} reshape(bf16[2048,2,6,144]{3,2,1,0:T(8,128)(2,1)} %bitcast.309) | data formatting | bytes 14155776
  144.1 89.7 %all_to_all.36 = bf16[16,2,110592]{2,1,0:T(2,128)(2,1)} all-to-all(bf16[16,2,110592]{2,1,0:T(2,128)(2,1)} %reshape.52), channel_id=1, replica_groups=mesh['tile'=16,'chan'=8] {'tile'}, dimensions={0} | all-to-all | bytes 14155776 | tf_op jit(solution)/shard_map/all_to_all | solution.py:13
  233.9 24.0 %reshape.53 = bf16[2048,2,6,144]{3,2,1,0:T(8,128)(2,1)} reshape(bf16[16,2,110592]{2,1,0:T(2,128)(2,1)} %all_to_all.36) | data formatting | bytes 14155776
  257.9 17.4 %copy.217 = bf16[2,16,6,144,128]{4,3,2,1,0:T(8,128)(2,1)} copy(bf16[2,16,6,144,128]{3,2,0,4,1:T(8,128)(2,1)} %bitcast.310) | data formatting | bytes 14155776 | tf_op jit(solution)/shard_map/all_to_all | solution.py:13
  280.2 6.6 fusion
  286.9 6.6 fusion.1
  293.5 6.9 fusion.2
  300.3 6.1 fusion.3
  306.5 6.8 fusion.4
  313.2 7.0 %fusion.5 = f32[96,2,144,32]{0,3,2,1:T(8,128)} fusion(bf16[96,2,144,128]{3,0,2,1:T(8,128)(2,1)S(1)} %bitcast.283, bf16[3,3,3,128,32]{3,4,2,1,0:T(8,128)(2,1)S(1)} %copy-done.2), kind=kOutput, calls=%fused_computation.30 | convolution fusion | flops 226492416 | bytes 10625024 | tf_op jit(solution)/shard_map/sg,rbws->grbw/dot_general | solution.py:31
  320.2 7.2 %fusion.6 = f32[96,2,144,32]{0,3,2,1:T(8,128)} fusion(bf16[96,2,144,128]{3,0,2,1:T(8,128)(2,1)S(1)} %bitcast.284, bf16[3,3,3,128,32]{3,4,2,1,0:T(8,128)(2,1)S(1)} %copy-done.2), kind=kOutput, calls=%fused_computation.31 | convolution fusion | flops 226492416 | bytes 10625024 | tf_op jit(solution)/shard_map/sg,rbws->grbw/dot_general | solution.py:31
  327.5 7.2 %fusion.49 = f32[32,96,2,144]{1,0,3,2:T(8,128)} fusion(bf16[3,3,3,128,32]{3,4,2,1,0:T(8,128)(2,1)S(1)} %copy-done.2, bf16[2,96,144,128]{3,2,1,0:T(8,128)(2,1)S(1)} %bitcast.305), kind=kOutput, calls=%fused_computation.92 | convolution fusion | flops 226492416 | bytes 10625024 | tf_op jit(solution)/shard_map/sg,rbws->grbw/dot_general | solution.py:31
  334.7 6.5 fusion.10
  346.9 6.4 fusion.12
  359.3 6.8 fusion.14
  371.8 6.9 fusion.9
  378.7 7.2 %fusion.39 = f32[32,96,2,144]{1,0,3,2:T(8,128)} fusion(bf16[3,3,3,128,32]{3,4,2,1,0:T(8,128)(2,1)S(1)} %copy-done.2, bf16[2,96,144,128]{3,2,1,0:T(8,128)(2,1)S(1)} %bitcast.306), kind=kOutput, calls=%fused_computation.82 | convolution fusion | flops 226492416 | bytes 10625024 | tf_op jit(solution)/shard_map/sg,rbws->grbw/dot_general | solution.py:31
  385.9 6.6 fusion.16
  392.5 6.7 fusion.17
  399.2 6.2 fusion.18
  422.6 6.7 fusion.22
  429.2 7.2 %fusion.29 = f32[32,96,2,144]{1,0,3,2:T(8,128)} fusion(bf16[3,3,3,128,32]{3,4,2,1,0:T(8,128)(2,1)S(1)} %copy-done.2, bf16[2,96,144,128]{3,2,1,0:T(8,128)(2,1)S(1)} %bitcast.307), kind=kOutput, calls=%fused_computation.72 | convolution fusion | flops 226492416 | bytes 10625024 | tf_op jit(solution)/shard_map/sg,rbws->grbw/dot_general | solution.py:31
  436.5 7.4 %fusion.55 = f32[32,96,2,144]{1,0,3,2:T(8,128)} fusion(bf16[128,32]{0,1:T(8,128)(2,1)S(1)} %copy-done.3, bf16[2,96,144,128]{3,2,1,0:T(8,128)(2,1)S(1)} %bitcast.308), kind=kOutput, calls=%fused_computation.98 | convolution fusion | flops 226492416 | bytes 10625024 | tf_op jit(solution)/shard_map/sg,rbws->grbw/dot_general | solution.py:18
  443.9 20.2 %bitcast_add_fusion.10 = f32[32,96,2,144]{1,0,3,2:T(8,128)} fusion(f32[96,2,144,32]{0,3,2,1:T(8,128)} %fusion.6, f32[96,2,144,32]{0,3,2,1:T(8,128)} %fusion.5, f32[96,2,144,32]{0,3,2,1:T(8,128)} %fusion.4, f32[32,96,2,144]{1,0,3,2:T(8,128)} %fusion.49, f32[96,2,144,32]{0,3,2,1:T(8,128)} %fusion.3, f32[96,2,144,32]{0,3,2,1:T(8,128)} %fusion.2, ...), kind=kOutput, calls=%fused_computation.60 | convolution fusion | flops 233570304 | bytes 38936576 | tf_op jit(solution)/shard_map/sg,rbws->grbw/dot_general | solution.py:31
  464.2 19.4 %bitcast_add_fusion.5 = f32[32,96,2,144]{1,0,3,2:T(8,128)} fusion(f32[96,2,144,32]{0,3,2,1:T(8,128)} %fusion.14, f32[96,2,144,32]{0,3,2,1:T(8,128)} %fusion.13, f32[96,2,144,32]{0,3,2,1:T(8,128)} %fusion.12, f32[32,96,2,144]{1,0,3,2:T(8,128)} %fusion.39, f32[96,2,144,32]{0,3,2,1:T(8,128)} %fusion.11, f32[96,2,144,32]{0,3,2,1:T(8,128)} %fusion.10, ...), kind=kOutput, calls=%fused_computation.55 | convolution fusion | flops 233570304 | bytes 38936576 | tf_op jit(solution)/shard_map/sg,rbws->grbw/dot_general | solution.py:31
  483.6 18.8 %bitcast_add_fusion = f32[32,96,2,144]{1,0,3,2:T(8,128)} fusion(f32[96,2,144,32]{0,3,2,1:T(8,128)} %fusion.22, f32[96,2,144,32]{0,3,2,1:T(8,128)} %fusion.21, f32[96,2,144,32]{0,3,2,1:T(8,128)} %fusion.20, f32[32,96,2,144]{1,0,3,2:T(8,128)} %fusion.29, f32[96,2,144,32]{0,3,2,1:T(8,128)} %fusion.19, f32[96,2,144,32]{0,3,2,1:T(8,128)} %fusion.18, ...), kind=kOutput, calls=%fused_computation.50 | convolution fusion | flops 233570304 | bytes 38936576 | tf_op jit(solution)/shard_map/sg,rbws->grbw/dot_general | solution.py:31
  502.4 13.0 %maximum_bitcast_fusion = f32[96,2,144,128]{0,3,2,1:T(8,128)} fusion(f32[32,96,2,144]{1,0,3,2:T(8,128)} %bitcast_add_fusion, f32[32,96,2,144]{1,0,3,2:T(8,128)} %bitcast_add_fusion.5, f32[32,96,2,144]{1,0,3,2:T(8,128)S(1)} %bitcast.312, f32[32,96,2,144]{1,0,3,2:T(8,128)} %fusion.55), kind=kLoop, calls=%fused_computation.24 | loop fusion | flops 10616832 | bytes 28311552 | tf_op jit(solution)/shard_map/transpose | solution.py:39
  515.4 17.1 %copy.243 = f32[96,2,144,128]{3,2,1,0:T(8,128)} copy(f32[96,2,144,128]{0,3,2,1:T(8,128)} %maximum_bitcast_fusion) | data formatting | bytes 28311552 | tf_op jit(solution)/shard_map/transpose | solution.py:39
  533.2 123.6 %reduce-scatter.2.cloned.1.call-done = f32[6,2,144,128]{3,2,1,0:T(8,128)} async-done(((f32[96,2,144,128]{3,2,1,0:T(8,128)}), f32[6,2,144,128]{3,2,1,0:T(8,128)}) %reduce-scatter.2.cloned.1.call-update) | async-done | bytes 884752 | tf_op jit(solution)/shard_map/reduce_scatter | solution.py:39
  667.0 8.5 %all-to-all-done.1 = bf16[8,2,13824]{2,1,0:T(2,128)(2,1)S(1)} async-done(((bf16[8,2,13824]{2,1,0:T(2,128)(2,1)}), bf16[8,2,13824]{2,1,0:T(2,128)(2,1)S(1)}, u32[]{:S(2)}, u32[]{:S(2)}) %all-to-all-start.1) | async-done | bytes 442400 | tf_op jit(solution)/shard_map/all_to_all | solution.py:42
  (54 shorter events, 62.0 us)
Async XLA Ops:
  7.2 674.8 %copy-start = (bf16[1024,256]{1,0:T(8,128)(2,1)S(1)}, bf16[1024,256]{1,0:T(8,128)(2,1)}, u32[]{:S(2)}) copy-start(bf16[1024,256]{1,0:T(8,128)(2,1)} %param.11) | copy-start | bytes 1572868
  7.2 85.3 %all-gather.2.cloned.1.call-start = ((), (), s32[]{:S(2)}) async-start(), calls=%async_computation.3 | async-start | bytes 7962624 | tf_op jit(solution)/shard_map/all_gather | solution.py:12
  10.2 646.7 %reduce-scatter.2.cloned.1.call-start = ((), (), s32[]{:S(2)}) async-start(), calls=%async_computation.4 | async-start | bytes 15040512 | tf_op jit(solution)/shard_map/reduce_scatter | solution.py:39
  275.3 4.9 copy-start.2
  280.2 142.3 %copy-start.1 = (bf16[2,96,144,128]{3,1,2,0:T(8,128)(2,1)}, bf16[2,96,144,128]{3,1,2,0:T(8,128)(2,1)S(1)}, u32[]{:S(2)}) copy-start(bf16[2,96,144,128]{3,1,2,0:T(8,128)(2,1)S(1)} %copy.311) | copy-start | bytes 21233668
  313.2 14.3 %slice-start = ((s8[7077888]{0:T(1024)(128)(4,1)}), s8[4194304]{0:T(1024)(128)(4,1)S(1)}, s32[]{:S(2)}) async-start(s8[7077888]{0:T(1024)(128)(4,1)} %bitcast.303), calls=%async_computation.5 | async-start | bytes 8388608
  320.2 7.2 %slice-start.1 = ((s8[7077888]{0:T(1024)(128)(4,1)}), s8[2883584]{0:T(1024)(128)(4,1)S(1)}, s32[]{:S(2)}) async-start(s8[7077888]{0:T(1024)(128)(4,1)} %bitcast.303), calls=%async_computation.6 | async-start | bytes 5767168
  429.2 7.2 %copy-start.3 = (bf16[128,32]{0,1:T(8,128)(2,1)S(1)}, bf16[128,32]{0,1:T(8,128)(2,1)}, u32[]{:S(2)}) copy-start(bf16[128,32]{0,1:T(8,128)(2,1)} %param.9) | copy-start | bytes 24580
  464.2 38.2 %slice-start.2 = ((s8[4718592]{0:T(1024)(128)(4,1)}), s8[524288]{0:T(1024)(128)(4,1)S(1)}, s32[]{:S(2)}) async-start(s8[4718592]{0:T(1024)(128)(4,1)} %bitcast.311), calls=%async_computation.7 | async-start | bytes 1048576
  483.6 18.8 %slice-start.3 = ((s8[4718592]{0:T(1024)(128)(4,1)}), s8[4194304]{0:T(1024)(128)(4,1)S(1)}, s32[]{:S(2)}) async-start(s8[4718592]{0:T(1024)(128)(4,1)} %bitcast.311), calls=%async_computation.8 | async-start | bytes 8388608
  532.5 0.7 copy-start.6
  533.2 133.7 %copy-start.4 = (s32[2,6,18]{2,0,1:T(2,128)S(1)}, s32[2,6,18]{2,0,1:T(2,128)}, u32[]{:S(2)}) copy-start(s32[2,6,18]{2,0,1:T(2,128)} %param.13) | copy-start | bytes 2596
  658.8 23.6 %copy-start.5 = (bf16[256,3]{0,1:T(4,128)(2,1)S(1)}, bf16[256,3]{0,1:T(4,128)(2,1)}, u32[]{:S(2)}) copy-start(bf16[256,3]{0,1:T(4,128)(2,1)} %param.12) | copy-start | bytes 4612
  662.5 12.9 %all-to-all-start.1 = ((bf16[8,2,13824]{2,1,0:T(2,128)(2,1)}), bf16[8,2,13824]{2,1,0:T(2,128)(2,1)S(1)}, u32[]{:S(2)}, u32[]{:S(2)}) async-start(bf16[8,2,13824]{2,1,0:T(2,128)(2,1)} %reshape.54), calls=%async_computation.2 | async-start | bytes 884736 | tf_op jit(solution)/shard_map/all_to_all | solution.py:42
Sparse Core Ops, SparseCore 0:
  10.4 82.1 all-gather.1
  532.6 124.2 reduce-scatter.1
where the time goes:
time: 697 us; the launch traced here: 691 us
  matrix products  223 us (32%)
  waiting for transfers between devices  214 us (31%)
  local copies, waits for them, and re-layouts  132 us (19%)
  blocking collectives  89.7 us (13%)
  between operations  14.5 us (2%)
  other arithmetic  13.2 us (2%)
    dot_general x27, matrix products, body(): jnp.einsum('sg,rbws->grbw', atrous_weight[index, tap_row, tap_col], regio...  215 us
    reduce_scatter x1, waiting for transfers between devices, body(): lax.psum_scatter(joined.transpose(1, 2, 3, 0), 'tile', scatter_dimension=...  124 us
    all_to_all x1, blocking collectives, body(): lax.all_to_all(row_strip, 'tile', split_axis=3, concat_axis=1, tiled=True)  89.7 us
    all_gather x1, waiting for transfers between devices, body(): row_strip = lax.all_gather(features, 'chan', axis=2, tiled=True)  82.2 us
    unnamed x30, local copies, waits for them, and re-layouts  56 us
    all_gather x1, local copies, waits for them, and re-layouts, body(): row_strip = lax.all_gather(features, 'chan', axis=2, tiled=True)  27.9 us
    all_to_all x2, local copies, waits for them, and re-layouts, body(): lax.all_to_all(row_strip, 'tile', split_axis=3, concat_axis=1, tiled=True)  22.3 us
    transpose x1, local copies, waits for them, and re-layouts, body(): joined.transpose(1, 2, 3, 0)  17.1 us
  transfers between devices with their start and end apart: 3, of which 3 were waited for; matrix products, arithmetic and copies ran while one was open for 0% of the time, Pallas kernels for 0%

commit v1 on v0

v1 whole, which is shorter than its diff:
```python
import jax
import jax.numpy as jnp
import numpy as np
from jax import lax
from jax.experimental import pallas as pl
from jax.experimental.pallas import tpu as pltpu
from jax.sharding import Mesh, PartitionSpec as P

ROWS = 32
GRID = 224
BF = jnp.bfloat16
F32 = jnp.float32
MIB = 1024 * 1024


def _message_row(i, t, c):
    return i * 9 + t * 3 + c


def _pack_matrix():
    m = np.zeros((256, 216), np.float32)
    for xq in range(4):
        for h in range(2):
            for i in range(3):
                for t in range(3):
                    for c in range(3):
                        row = (xq % 2) * 3 + i
                        col = 3 * (2 * t + h) + c
                        m[(xq * 2 + h) * ROWS + _message_row(i, t, c), (row * 18 + col) * 2 + xq // 2] = 1
    return m


def _unpack_matrices():
    by_cols = np.zeros((216, 256), np.float32)
    by_samples = np.zeros((216, 256), np.float32)
    for h in range(2):
        for xq in range(4):
            for i in range(3):
                for t in range(3):
                    for c in range(3):
                        row = (xq % 2) * 3 + i
                        col = 3 * (2 * t + h) + c
                        b = xq // 2
                        src = (h * 4 + xq) * ROWS + _message_row(i, t, c)
                        by_cols[(row * 18 + col) * 2 + b, src] = 1
                        by_samples[(row * 2 + b) * 18 + col, src] = 1
    return by_cols, by_samples


def _shift_matrices():
    m = np.zeros((7, GRID, 256), np.float32)
    for dc in range(-3, 4):
        for i in range(3):
            for gc in range(12):
                for u in range(6):
                    if 0 <= gc + dc < 12:
                        q = 2 * (gc + dc) + u // 3
                        m[dc + 3, (i * 12 + gc) * 6 + u, (q // 3) * ROWS + _message_row(i, q % 3, u % 3)] = 1
    return m


TAPS = (
    [(3, -1, 0), (2, -1, 0), (1, -1, 0), (0, 0, 0), (1, 0, 0), (2, 0, 0), (3, 0, 0), (1, 1, 0), (2, 1, 0), (3, 1, 0)]
    + [(d, a, c) for c in (-1, 1) for d in (1, 2, 3) for a in (-1, 0, 1)]
)


def _pack_kernel(p_ref, f_ref, out_ref):
    p = p_ref[...]
    for y in range(4):
        for z in range(2):
            part = f_ref[:, z * 1024 + y * 256 : z * 1024 + (y + 1) * 256]
            rows = jnp.dot(p, part, preferred_element_type=F32).astype(BF)
            for xq in range(4):
                for h in range(2):
                    piece = rows[(xq * 2 + h) * ROWS : (xq * 2 + h + 1) * ROWS]
                    for zl in range(2):
                        out_ref[((h * 4 + y) * 2 + zl) * 4 + xq, :, z * 256 : (z + 1) * 256] = piece


def _conv_kernel(where_ref, raw_ref, s_ref, st_ref, own_ref, other_ref, out_ref, xs, wt, sh, acc, sems):
    x, core, zh, first = where_ref[0], where_ref[1], where_ref[2], where_ref[3]
    copies = []
    for k in range(4):
        xo = lax.rem(x + k, 4)
        for z in range(2):
            for o, ref in enumerate((own_ref, other_ref)):
                slab = lax.rem(zh + z, 2) * 2 + lax.rem(core + o, 2)
                copies.append(
                    pltpu.make_async_copy(
                        ref.at[k, z, pl.ds(0, 28)],
                        wt.at[:, xo, :, pl.ds(pl.multiple_of(slab * 128, 128), 128)],
                        sems.at[len(copies)],
                    )
                )
        copies.append(pltpu.make_async_copy(own_ref.at[k, 0, 28], sh.at[xo], sems.at[len(copies)]))
    for copy in copies:
        copy.start()

    def spread(g, _):
        raw = raw_ref[pl.ds(g * 8, 8)].reshape(256, 512)
        for dc in range(7):
            xs[dc, g] = jnp.dot(s_ref[dc], raw, preferred_element_type=F32).astype(BF)
        return 0

    lax.fori_loop(0, 8, spread, 0)
    for copy in copies:
        copy.wait()

    lane = lax.broadcasted_iota(jnp.int32, (1, 128), 1)
    shifts = []
    for b in range(4):
        line = jnp.zeros((1, 128), F32)
        for xo in range(4):
            terms = sh[xo].astype(F32)
            whole = terms[0:1] + terms[1:2] + terms[2:3]
            if xo != b:
                whole = pltpu.roll(whole, ((xo - b) * 32) % 128, 1)
            line = jnp.where((lane >= xo * 32) & (lane < xo * 32 + 32), whole, line)
        shifts.append(jnp.where(first == 0, line, 0.0))
    for b in range(4):
        acc[b] = jnp.broadcast_to(shifts[b].reshape(1, 1, 128), (8, GRID, 128))

    def apply(s, dc, start, stop):
        t = start
        while t < stop:
            n = min(2, stop - t)
            w = wt[t : t + n].reshape(n * 128, 512)
            y = lax.dot_general(xs[dc + 3, s], w, (((1,), (1,)), ((), ())), preferred_element_type=F32)
            for k in range(n):
                d, a, _ = TAPS[t + k]
                acc[d, s - d * a] += y[:, k * 128 : (k + 1) * 128]
            t += n

    for s in range(8):
        apply(s, 0, 3 - min(3, 7 - s), 7 + min(3, s))
        for ci, c in enumerate((-1, 1)):
            for d in (1, 2, 3):
                base = 10 + ci * 9 + (d - 1) * 3
                apply(s, c * d, base + (0 if s + d <= 7 else 1), base + (3 if s - d >= 0 else 2))

    for g in range(8):
        for b in range(4):
            rows = jnp.dot(st_ref[...], acc[b, g].astype(BF), preferred_element_type=F32).astype(BF)
            for j in range(8):
                out_ref[g * 8 + j, :, b * 128 : (b + 1) * 128] = rows[j * ROWS : (j + 1) * ROWS]


def _final_kernel(in_ref, proj_ref, cls_ref, lab_ref, u_ref, v_ref, out_ref, loss_ref, pyr):
    for h in range(2):
        for xq in range(4):
            r = h * 4 + xq
            for zl in range(2):
                total = in_ref[((h * 4 + 0) * 2 + zl) * 4 + xq].astype(F32)
                for y in range(1, 4):
                    total = total + in_ref[((h * 4 + y) * 2 + zl) * 4 + xq].astype(F32)
                total = jnp.maximum(total, 0.0).astype(BF)
                for b in range(4):
                    pyr[r * ROWS : (r + 1) * ROWS, b * 256 + zl * 128 : b * 256 + (zl + 1) * 128] = total[
                        :, b * 128 : (b + 1) * 128
                    ]
    mixed = jnp.dot(pyr[...], proj_ref[...], preferred_element_type=F32)
    projected = jnp.maximum(mixed, 0.0).astype(BF)
    out_ref[...] = jnp.dot(u_ref[...], projected, preferred_element_type=F32).astype(BF)
    rows = jnp.dot(v_ref[...], projected, preferred_element_type=F32).astype(BF)
    logits = lax.dot_general(cls_ref[...], rows, (((1,), (1,)), ((), ())), preferred_element_type=F32)
    total = jnp.zeros((1, 216), F32)
    chosen = jnp.zeros((1, 216), F32)
    for k in range(3):
        total = total + jnp.exp(logits[k : k + 1])
        chosen = chosen + jnp.where(lab_ref[...] == k, logits[k : k + 1], 0.0)
    loss_ref[...] = jnp.log(total) - chosen


def body(features, atrous_weight, point_weight, branch_shift, proj_weight, class_weight, labels):
    x, zh = lax.axis_index("x"), lax.axis_index("zh")
    core, y = lax.axis_index("core"), lax.axis_index("y")
    where = jnp.stack([x, core, zh, y]).astype(jnp.int32)

    wide = atrous_weight.transpose(0, 1, 2, 4, 3)
    taps = [
        point_weight.T if d == 0 else wide[d - 1, a + 1, c + 1]
        for d, a, c in TAPS
    ]
    high = branch_shift.reshape(1, 128).astype(BF)
    rest = branch_shift.reshape(1, 128) - high.astype(F32)
    middle = rest.astype(BF)
    low = (rest - middle.astype(F32)).astype(BF)
    extra = jnp.concatenate([high, middle, low, jnp.zeros((29, 128), BF)])
    weights = jnp.stack(taps + [extra])
    swapped = lax.ppermute(weights, "zh", [(0, 1), (1, 0)])
    pair = jnp.stack([weights, swapped])

    flat = features.transpose(1, 2, 0, 3).reshape(216, 2048)
    messages = pl.pallas_call(
        _pack_kernel,
        out_shape=jax.ShapeDtypeStruct((64, ROWS, 512), BF),
        compiler_params=pltpu.CompilerParams(vmem_limit_bytes=32 * MIB),
        name="pack",
    )(jnp.asarray(_pack_matrix(), BF), flat)

    gathered = [pair] + [
        lax.ppermute(pair, "x", [(i, (i - k) % 4) for i in range(4)]) for k in (1, 2, 3)
    ]
    raw = lax.all_to_all(messages, ("zh", "y", "zl", "x"), 0, 0, tiled=True)
    own = jnp.stack(gathered)
    other = lax.ppermute(own, "core", [(0, 1), (1, 0)])

    shift = _shift_matrices()
    partial = pl.pallas_call(
        _conv_kernel,
        out_shape=jax.ShapeDtypeStruct((64, ROWS, 512), BF),
        in_specs=[
            pl.BlockSpec(memory_space=pltpu.SMEM),
            pl.BlockSpec(memory_space=pltpu.VMEM),
            pl.BlockSpec(memory_space=pltpu.VMEM),
            pl.BlockSpec(memory_space=pltpu.VMEM),
            pl.BlockSpec(memory_space=pl.ANY),
            pl.BlockSpec(memory_space=pl.ANY),
        ],
        scratch_shapes=[
            pltpu.VMEM((7, 8, GRID, 512), BF),
            pltpu.VMEM((28, 4, 32, 512), BF),
            pltpu.VMEM((4, 32, 128), BF),
            pltpu.VMEM((4, 8, GRID, 128), F32),
            pltpu.SemaphoreType.DMA((20,)),
        ],
        compiler_params=pltpu.CompilerParams(vmem_limit_bytes=48 * MIB),
        name="conv",
    )(where, raw, jnp.asarray(shift, BF), jnp.asarray(shift[3].T, BF), own, other)

    arrived = lax.all_to_all(partial, ("zh", "y", "zl", "x"), 0, 0, tiled=True)
    by_cols, by_samples = _unpack_matrices()
    classes = jnp.concatenate([class_weight.T, jnp.zeros((5, 256), BF)])
    projected, loss = pl.pallas_call(
        _final_kernel,
        out_shape=(jax.ShapeDtypeStruct((216, 256), BF), jax.ShapeDtypeStruct((1, 216), F32)),
        scratch_shapes=[pltpu.VMEM((256, 1024), BF)],
        compiler_params=pltpu.CompilerParams(vmem_limit_bytes=32 * MIB),
        name="final",
    )(
        arrived,
        proj_weight,
        classes,
        labels.transpose(1, 0, 2).reshape(1, 216),
        jnp.asarray(by_cols, BF),
        jnp.asarray(by_samples, BF),
    )
    return (
        projected.reshape(6, 18, 2, 256).transpose(2, 0, 1, 3),
        loss.reshape(6, 2, 18).transpose(1, 0, 2),
    )


def solution(mesh):
    fine = Mesh(mesh.devices.reshape(2, 4, 2, 2, 4), ("zh", "y", "core", "zl", "x"))
    tile, chan = ("zh", "y", "core"), ("zl", "x")
    return jax.shard_map(
        body,
        mesh=fine,
        in_specs=(
            P(None, tile, chan, None),
            P(None, None, None, tile, chan),
            P(tile, chan),
            P(None, chan),
            P(),
            P(),
            P(None, tile, chan),
        ),
        out_specs=(P(None, tile, chan, None), P(None, tile, chan)),
        check_vma=False,
    )
```

time: 697 us -> 141 us (0.20)
  matrix products: 223 us -> 0 us
  waiting for transfers between devices: 214 us -> 68.9 us
  local copies, waits for them, and re-layouts: 132 us -> 23 us
  blocking collectives: 89.7 us -> 0 us
  starting transfers between devices: 4.42 us -> 24.7 us
  Pallas kernels: 0 us -> 19.6 us
  between operations: 14.5 us -> 0.82 us
  other arithmetic: 13.2 us -> 2.53 us
    dot_general x30 -> x0, matrix products: 223 us -> none  [the longest x27 215 us: body(): jnp.einsum('sg,rbws->grbw', atrous_weight[index, tap_row, tap_col], regio...]
    reduce_scatter x1 -> x0, waiting for transfers between devices: 124 us -> none  [body(): lax.psum_scatter(joined.transpose(1, 2, 3, 0), 'tile', scatter_dimension=...]
    all_to_all x1 -> x0, blocking collectives: 89.7 us -> none  [body(): lax.all_to_all(row_strip, 'tile', split_axis=3, concat_axis=1, tiled=True)]
    all_gather x1 -> x0, waiting for transfers between devices: 82.2 us -> none  [body(): row_strip = lax.all_gather(features, 'chan', axis=2, tiled=True)]
    all_to_all x1 -> x2, waiting for transfers between devices: 8.47 us -> 53.1 us  [the longest x1 29.6 us: body(): arrived = lax.all_to_all(partial, ('zh', 'y', 'zl', 'x'), 0, 0, tiled=True)]
    unnamed x30 -> x46, local copies, waits for them, and re-layouts: 56 us -> 19.8 us
    all_gather x1 -> x0, local copies, waits for them, and re-layouts: 27.9 us -> none  [body(): row_strip = lax.all_gather(features, 'chan', axis=2, tiled=True)]
    all_to_all x2 -> x0, local copies, waits for them, and re-layouts: 22.3 us -> none  [body(): lax.all_to_all(row_strip, 'tile', split_axis=3, concat_axis=1, tiled=True)]
  transfers between devices with their start and end apart: 3 -> 7, of which waited for: 3 -> 4; matrix products, arithmetic and copies ran while one was open for 0% -> 2% of each run, Pallas kernels for 0% -> 1%
where the time goes in v1:
time: 141 us; the launch traced here: 140 us
  waiting for transfers between devices  68.9 us (49%)
  starting transfers between devices  24.7 us (18%)
  local copies, waits for them, and re-layouts  23 us (16%)
  Pallas kernels  19.6 us (14%)
  other arithmetic  2.53 us (2%)
    all_to_all x1, waiting for transfers between devices, body(): arrived = lax.all_to_all(partial, ('zh', 'y', 'zl', 'x'), 0, 0, tiled=True)  29.6 us
    all_to_all x1, waiting for transfers between devices, body(): raw = lax.all_to_all(messages, ('zh', 'y', 'zl', 'x'), 0, 0, tiled=True)  23.5 us
    unnamed x46, local copies, waits for them, and re-layouts  19.8 us
    pallas_call x1, Pallas kernels, body(): pl.pallas_call(_conv_kernel, out_shape=jax.ShapeDtypeStruct((64, ROWS, 51...  16.9 us
    ppermute x3, waiting for transfers between devices, body(): lax.ppermute(pair, 'x', [(i, (i - k) % 4) for i in range(4)])  9.94 us
    all_to_all x1, starting transfers between devices, body(): raw = lax.all_to_all(messages, ('zh', 'y', 'zl', 'x'), 0, 0, tiled=True)  8.61 us
    all_to_all x1, starting transfers between devices, body(): arrived = lax.all_to_all(partial, ('zh', 'y', 'zl', 'x'), 0, 0, tiled=True)  6.14 us
    ppermute x1, waiting for transfers between devices, body(): swapped = lax.ppermute(weights, 'zh', [(0, 1), (1, 0)])  5.78 us
  transfers between devices with their start and end apart: 7, of which 4 were waited for; matrix products, arithmetic and copies ran while one was open for 2% of the time, Pallas kernels for 1%

profile of v1, /device:TPU:0, one launch (start us, length us, event | category | flops | bytes accessed | tf_op | source)
XLA Modules:
  0.0 139.5 jit_solution(3035805954763254476)
XLA Ops:
  0.7 0.8 constant_dynamic-update-slice_fusion.28
  2.1 0.7 constant_dynamic-update-slice_fusion.26
  2.8 0.7 constant_dynamic-update-slice_fusion.25
  3.5 0.7 constant_dynamic-update-slice_fusion.24
  4.3 0.7 constant_dynamic-update-slice_fusion.23
  5.7 0.7 constant_dynamic-update-slice_fusion.21
  6.4 0.7 constant_dynamic-update-slice_fusion.20
  7.1 0.7 constant_dynamic-update-slice_fusion.19
  7.8 0.7 constant_dynamic-update-slice_fusion.18
  8.5 0.7 constant_dynamic-update-slice_fusion.17
  9.2 0.7 constant_dynamic-update-slice_fusion.16
  9.9 0.7 constant_dynamic-update-slice_fusion.15
  10.6 0.7 constant_dynamic-update-slice_fusion.14
  11.3 0.7 constant_dynamic-update-slice_fusion.13
  12.0 0.7 constant_dynamic-update-slice_fusion.12
  12.7 0.7 constant_dynamic-update-slice_fusion.11
  13.4 0.7 constant_dynamic-update-slice_fusion.10
  20.4 0.8 reshape.77
  21.4 4.0 %collective-permute-start = (bf16[29,32,128]{2,1,0:T(8,128)(2,1)S(1)}, bf16[29,32,128]{2,1,0:T(8,128)(2,1)S(1)}, u32[]{:S(2)}, u32[]{:S(2)}) collective-permute-start(bf16[29,32,128]{2,1,0:T(8,128)(2,1)S(1)} %constant_dynamic-update-slice_fusion), channel_id=1, source_target_pairs={{0,64},{64,0},{1,65},{65,1},{2,66},{66,2},{3,67},{67,3},{4,68},{68... | collective-permute-start | bytes 712712 | tf_op jit(solution)/shard_map/ppermute | solution.py:191
  25.4 5.8 %collective-permute-done = bf16[29,32,128]{2,1,0:T(8,128)(2,1)S(1)} collective-permute-done((bf16[29,32,128]{2,1,0:T(8,128)(2,1)S(1)}, bf16[29,32,128]{2,1,0:T(8,128)(2,1)S(1)}, u32[]{:S(2)}, u32[]{:S(2)}) %collective-permute-start) | collective-permute-done | bytes 237600 | tf_op jit(solution)/shard_map/ppermute | solution.py:191
  31.2 1.6 %collective-permute-start.3 = (bf16[2,29,32,128]{3,2,1,0:T(8,128)(2,1)S(1)}, bf16[2,29,32,128]{3,2,1,0:T(8,128)(2,1)}, u32[]{:S(2)}, u32[]{:S(2)}) collective-permute-start(bf16[2,29,32,128]{3,2,1,0:T(8,128)(2,1)S(1)} %get-tuple-element.7), channel_id=1, source_target_pairs={{0,1},{1,2},{2,3},{3,0},{4,5},{5,6},{6,7},{7,4},{8,9},{9,10},{10,1... | collective-permute-start | bytes 1425416 | tf_op jit(solution)/shard_map/ppermute | solution.py:203
  32.8 2.7 %collective-permute-start.2 = (bf16[2,29,32,128]{3,2,1,0:T(8,128)(2,1)S(1)}, bf16[2,29,32,128]{3,2,1,0:T(8,128)(2,1)}, u32[]{:S(2)}, u32[]{:S(2)}) collective-permute-start(bf16[2,29,32,128]{3,2,1,0:T(8,128)(2,1)S(1)} %get-tuple-element.7), channel_id=1, source_target_pairs={{0,2},{1,3},{2,0},{3,1},{4,6},{5,7},{6,4},{7,5},{8,10},{9,11},{10,... | collective-permute-start | bytes 1425416 | tf_op jit(solution)/shard_map/ppermute | solution.py:203
  35.5 1.4 %collective-permute-start.1 = (bf16[2,29,32,128]{3,2,1,0:T(8,128)(2,1)S(1)}, bf16[2,29,32,128]{3,2,1,0:T(8,128)(2,1)}, u32[]{:S(2)}, u32[]{:S(2)}) collective-permute-start(bf16[2,29,32,128]{3,2,1,0:T(8,128)(2,1)S(1)} %get-tuple-element.7), channel_id=1, source_target_pairs={{0,3},{1,0},{2,1},{3,2},{4,7},{5,4},{6,5},{7,6},{8,11},{9,8},{10,9... | collective-permute-start | bytes 1425416 | tf_op jit(solution)/shard_map/ppermute | solution.py:203
  37.3 1.8 %pack.1 = bf16[64,32,512]{2,1,0:T(8,128)(2,1)} custom-call(bf16[256,216]{1,0:T(8,128)(2,1)S(1)} %copy-done.3, bf16[216,2048]{1,0:T(8,128)(2,1)S(1)} %reshape.76.f_ref), custom_call_target="tpu_custom_call" | custom-call | tf_op jit(solution)/shard_map/pack/pallas_call | solution.py:195
  39.0 8.6 %all-to-all-start = ((bf16[64,32,512]{2,1,0:T(8,128)(2,1)}), bf16[64,32,512]{2,1,0:T(8,128)(2,1)}, u32[]{:S(2)}, u32[]{:S(2)}) async-start(bf16[64,32,512]{2,1,0:T(8,128)(2,1)} %pack.1), calls=%async_computation | async-start | bytes 4194304 | tf_op jit(solution)/shard_map/all_to_all | solution.py:205
  47.7 9.9 %collective-permute-done.2 = bf16[2,29,32,128]{3,2,1,0:T(8,128)(2,1)} collective-permute-done((bf16[2,29,32,128]{3,2,1,0:T(8,128)(2,1)S(1)}, bf16[2,29,32,128]{3,2,1,0:T(8,128)(2,1)}, u32[]{:S(2)}, u32[]{:S(2)}) %collective-permute-start.2) | collective-permute-done | bytes 475168 | tf_op jit(solution)/shard_map/ppermute | solution.py:203
  57.6 1.6 %pad_maximum_fusion.own_ref = bf16[4,2,29,32,128]{4,3,2,1,0:T(8,128)(2,1)S(1)} fusion(bf16[1,2,29,32,128]{4,3,2,1,0:T(8,128)(2,1)} %bitcast.41, bf16[1,2,29,32,128]{4,3,2,1,0:T(8,128)(2,1)} %bitcast.40, bf16[1,2,29,32,128]{4,3,2,1,0:T(8,128)(2,1)} %bitcast.39, bf16[1,2,29,32,128]{4,3,2,1,0:T(8,128)(2,1)S(1)} %get-tuple-element.6), kind=kLoop, calls=%fused_computation | loop fusion | flops 2850816 | bytes 3801088 | tf_op jit(solution)/shard_map/stack | solution.py:206
  59.6 23.5 %all-to-all-done.raw_ref = bf16[64,32,512]{2,1,0:T(8,128)(2,1)} async-done(((bf16[64,32,512]{2,1,0:T(8,128)(2,1)}), bf16[64,32,512]{2,1,0:T(8,128)(2,1)}, u32[]{:S(2)}, u32[]{:S(2)}) %all-to-all-start) | async-done | bytes 2097184 | tf_op jit(solution)/shard_map/all_to_all | solution.py:205
  83.1 16.9 %conv.1 = bf16[64,32,512]{2,1,0:T(8,128)(2,1)} custom-call(s32[4]{0:T(128)S(1)} %pad_add_fusion.where_ref, bf16[64,32,512]{2,1,0:T(8,128)(2,1)} %all-to-all-done.raw_ref, bf16[7,224,256]{2,1,0:T(8,128)(2,1)S(1)} %copy-done, bf16[256,224]{1,0:T(8,128)(2,1)S(1)} %copy-done.2, bf16[4,2,29,32,128]{4,3,2,1,0:T(8,128)(2,1)S(1)} %pad_maximum_fusion.own_ref, ...), custom_call_target="tpu_custom_call" | custom-call | tf_op jit(solution)/shard_map/conv/pallas_call | solution.py:210
  100.1 6.1 %all-to-all-start.1 = ((bf16[64,32,512]{2,1,0:T(8,128)(2,1)}), bf16[64,32,512]{2,1,0:T(8,128)(2,1)S(1)}, u32[]{:S(2)}, u32[]{:S(2)}) async-start(bf16[64,32,512]{2,1,0:T(8,128)(2,1)} %conv.1), calls=%async_computation.1 | async-start | bytes 4194304 | tf_op jit(solution)/shard_map/all_to_all | solution.py:232
  106.4 29.6 %all-to-all-done.1.in_ref = bf16[64,32,512]{2,1,0:T(8,128)(2,1)S(1)} async-done(((bf16[64,32,512]{2,1,0:T(8,128)(2,1)}), bf16[64,32,512]{2,1,0:T(8,128)(2,1)S(1)}, u32[]{:S(2)}, u32[]{:S(2)}) %all-to-all-start.1) | async-done | bytes 2097184 | tf_op jit(solution)/shard_map/all_to_all | solution.py:232
  136.0 0.9 final.1
  (46 shorter events, 11.4 us)
Async XLA Ops:
  0.6 36.6 %copy-start.3 = (bf16[256,216]{1,0:T(8,128)(2,1)S(1)}, bf16[256,216]{1,0:T(8,128)(2,1)}, u32[]{:S(2)}) copy-start(bf16[256,216]{1,0:T(8,128)(2,1)} %constant.30.clone.p_ref) | copy-start | bytes 331780
  0.6 36.3 %copy-start.6 = (bf16[2,6,18,2048]{3,0,2,1:T(2,128)(2,1)S(1)}, bf16[2,6,18,2048]{3,0,2,1:T(2,128)(2,1)}, u32[]{:S(2)}) copy-start(bf16[2,6,18,2048]{3,0,2,1:T(2,128)(2,1)} %param.12) | copy-start | bytes 2654212
  21.4 9.8 %collective-permute-start = (bf16[29,32,128]{2,1,0:T(8,128)(2,1)S(1)}, bf16[29,32,128]{2,1,0:T(8,128)(2,1)S(1)}, u32[]{:S(2)}, u32[]{:S(2)}) collective-permute-start(bf16[29,32,128]{2,1,0:T(8,128)(2,1)S(1)} %constant_dynamic-update-slice_fusion), channel_id=1, source_target_pairs={{0,64},{64,0},{1,65},{65,1},{2,66},{66,2},{3,67},{67,3},{4,68},{68... | collective-permute-start | bytes 712712 | tf_op jit(solution)/shard_map/ppermute | solution.py:191
  31.2 16.5 %collective-permute-start.3 = (bf16[2,29,32,128]{3,2,1,0:T(8,128)(2,1)S(1)}, bf16[2,29,32,128]{3,2,1,0:T(8,128)(2,1)}, u32[]{:S(2)}, u32[]{:S(2)}) collective-permute-start(bf16[2,29,32,128]{3,2,1,0:T(8,128)(2,1)S(1)} %get-tuple-element.7), channel_id=1, source_target_pairs={{0,1},{1,2},{2,3},{3,0},{4,5},{5,6},{6,7},{7,4},{8,9},{9,10},{10,1... | collective-permute-start | bytes 1425416 | tf_op jit(solution)/shard_map/ppermute | solution.py:203
  32.8 24.8 %collective-permute-start.2 = (bf16[2,29,32,128]{3,2,1,0:T(8,128)(2,1)S(1)}, bf16[2,29,32,128]{3,2,1,0:T(8,128)(2,1)}, u32[]{:S(2)}, u32[]{:S(2)}) collective-permute-start(bf16[2,29,32,128]{3,2,1,0:T(8,128)(2,1)S(1)} %get-tuple-element.7), channel_id=1, source_target_pairs={{0,2},{1,3},{2,0},{3,1},{4,6},{5,7},{6,4},{7,5},{8,10},{9,11},{10,... | collective-permute-start | bytes 1425416 | tf_op jit(solution)/shard_map/ppermute | solution.py:203
  35.5 22.1 %collective-permute-start.1 = (bf16[2,29,32,128]{3,2,1,0:T(8,128)(2,1)S(1)}, bf16[2,29,32,128]{3,2,1,0:T(8,128)(2,1)}, u32[]{:S(2)}, u32[]{:S(2)}) collective-permute-start(bf16[2,29,32,128]{3,2,1,0:T(8,128)(2,1)S(1)} %get-tuple-element.7), channel_id=1, source_target_pairs={{0,3},{1,0},{2,1},{3,2},{4,7},{5,4},{6,5},{7,6},{8,11},{9,8},{10,9... | collective-permute-start | bytes 1425416 | tf_op jit(solution)/shard_map/ppermute | solution.py:203
  39.0 44.1 %all-to-all-start = ((bf16[64,32,512]{2,1,0:T(8,128)(2,1)}), bf16[64,32,512]{2,1,0:T(8,128)(2,1)}, u32[]{:S(2)}, u32[]{:S(2)}) async-start(bf16[64,32,512]{2,1,0:T(8,128)(2,1)} %pack.1), calls=%async_computation | async-start | bytes 4194304 | tf_op jit(solution)/shard_map/all_to_all | solution.py:205
  57.6 25.5 %copy-start = (bf16[7,224,256]{2,1,0:T(8,128)(2,1)S(1)}, bf16[7,224,256]{2,1,0:T(8,128)(2,1)}, u32[]{:S(2)}) copy-start(bf16[7,224,256]{2,1,0:T(8,128)(2,1)} %constant.31.clone.s_ref) | copy-start | bytes 2408452
  57.6 25.5 %copy-start.2 = (bf16[256,224]{1,0:T(8,128)(2,1)S(1)}, bf16[256,224]{1,0:T(8,128)(2,1)}, u32[]{:S(2)}) copy-start(bf16[256,224]{1,0:T(8,128)(2,1)} %constant.32.clone.st_ref) | copy-start | bytes 344068
  59.3 23.9 %collective-permute-start.4 = (bf16[4,2,29,32,128]{4,3,2,1,0:T(8,128)(2,1)S(1)}, bf16[4,2,29,32,128]{4,3,2,1,0:T(8,128)(2,1)}, u32[]{:S(2)}, u32[]{:S(2)}) collective-permute-start(bf16[4,2,29,32,128]{4,3,2,1,0:T(8,128)(2,1)S(1)} %pad_maximum_fusion.own_ref), channel_id=1, source_target_pairs={{0,8},{8,0},{1,9},{9,1},{2,10},{10,2},{3,11},{11,3},{4,12},{12,4},... | collective-permute-start | bytes 5701640 | tf_op jit(solution)/shard_map/ppermute | solution.py:207
  100.1 6.2 %copy-start.8 = (bf16[256,3]{0,1:T(4,128)(2,1)S(1)}, bf16[256,3]{0,1:T(4,128)(2,1)}, u32[]{:S(2)}) copy-start(bf16[256,3]{0,1:T(4,128)(2,1)} %param.17) | copy-start | bytes 4612
  100.1 6.2 %copy-start.7 = (s32[2,6,18]{2,0,1:T(2,128)S(1)}, s32[2,6,18]{2,0,1:T(2,128)}, u32[]{:S(2)}) copy-start(s32[2,6,18]{2,0,1:T(2,128)} %param.18) | copy-start | bytes 2596
  100.1 35.9 %copy-start.1 = (bf16[1024,256]{1,0:T(8,128)(2,1)S(1)}, bf16[1024,256]{1,0:T(8,128)(2,1)}, u32[]{:S(2)}) copy-start(bf16[1024,256]{1,0:T(8,128)(2,1)} %proj_ref.1) | copy-start | bytes 1572868
  100.1 35.9 %copy-start.4 = (bf16[216,256]{1,0:T(8,128)(2,1)S(1)}, bf16[216,256]{1,0:T(8,128)(2,1)}, u32[]{:S(2)}) copy-start(bf16[216,256]{1,0:T(8,128)(2,1)} %constant.33.clone.u_ref) | copy-start | bytes 331780
  100.1 35.9 %copy-start.5 = (bf16[216,256]{1,0:T(8,128)(2,1)S(1)}, bf16[216,256]{1,0:T(8,128)(2,1)}, u32[]{:S(2)}) copy-start(bf16[216,256]{1,0:T(8,128)(2,1)} %constant.34.clone.v_ref) | copy-start | bytes 331780
  100.1 35.9 %all-to-all-start.1 = ((bf16[64,32,512]{2,1,0:T(8,128)(2,1)}), bf16[64,32,512]{2,1,0:T(8,128)(2,1)S(1)}, u32[]{:S(2)}, u32[]{:S(2)}) async-start(bf16[64,32,512]{2,1,0:T(8,128)(2,1)} %conv.1), calls=%async_computation.1 | async-start | bytes 4194304 | tf_op jit(solution)/shard_map/all_to_all | solution.py:232

commit v2 on v1

v2 whole, which is shorter than its diff:
```python
import jax
import jax.numpy as jnp
import numpy as np
from jax import lax
from jax.experimental import pallas as pl
from jax.experimental.pallas import tpu as pltpu
from jax.sharding import Mesh, PartitionSpec as P

SPOTS = 27
ROWS = 112
GRID = 224
HALO = 18
BF = jnp.bfloat16
F32 = jnp.float32
MIB = 1024 * 1024
JOIN_FLOPS = 4000000000


def _spot(i, t, c):
    return i * 9 + t * 3 + c


def _pack_matrix():
    m = np.zeros((256, 216), np.float32)
    for xq in range(4):
        for h in range(2):
            for i in range(3):
                for t in range(3):
                    for c in range(3):
                        row = (xq % 2) * 3 + i
                        col = 3 * (2 * t + h) + c
                        m[(xq * 2 + h) * 32 + _spot(i, t, c), (row * 18 + col) * 2 + xq // 2] = 1
    return m


def _unpack_matrices():
    by_cols = np.zeros((216, 256), np.float32)
    by_samples = np.zeros((216, 256), np.float32)
    for h in range(2):
        for xq in range(4):
            for i in range(3):
                for t in range(3):
                    for c in range(3):
                        row = (xq % 2) * 3 + i
                        col = 3 * (2 * t + h) + c
                        b = xq // 2
                        src = (h * 4 + xq) * 32 + _spot(i, t, c)
                        by_cols[(row * 18 + col) * 2 + b, src] = 1
                        by_samples[(row * 2 + b) * 18 + col, src] = 1
    return by_cols, by_samples


GROUPS = [
    [(0, 0, 0), (1, 0, 0), (2, 0, 0), (3, 0, 0)],
    [(3, -1, 0), (2, -1, 0), (1, -1, 0), (1, 1, 0), (2, 1, 0), (3, 1, 0)],
] + [[(d, a, c) for a in (-1, 0, 1)] for d in (1, 2, 3) for c in (-1, 1)]
TAPS = [tap for group in GROUPS for tap in group]


def _weights_kernel(wide_ref, point_ref, shift_ref, out_ref, terms):
    for n, (d, a, c) in enumerate(TAPS):
        out_ref[n] = point_ref[...] if d == 0 else wide_ref[(d - 1) * 9 + (a + 1) * 3 + c + 1]
    whole = shift_ref[...]
    high = whole.astype(BF).astype(F32)
    middle = (whole - high).astype(BF).astype(F32)
    terms[...] = jnp.zeros_like(terms)
    terms[0:4, 0:32] = high
    terms[8:12, 0:32] = middle
    terms[16:20, 0:32] = whole - high - middle
    out_ref[28] = terms[...].astype(BF)


def _join_kernel(a_ref, b_ref, c_ref, out_ref):
    for n, ref in enumerate((a_ref, b_ref, c_ref)):
        out_ref[n] = ref[...]


def _pack_kernel(p_ref, f_ref, out_ref, lines):
    p = p_ref[...]
    lines[...] = jnp.zeros_like(lines)
    for y in range(4):
        for z in range(2):
            part = f_ref[:, z * 1024 + y * 256 : z * 1024 + (y + 1) * 256]
            rows = jnp.dot(p, part, preferred_element_type=F32)
            for n in range(8):
                for o in range(2):
                    start = (z * 2 + o) * SPOTS
                    lines[y * 8 + n, start : start + SPOTS] = rows[n * 32 : n * 32 + SPOTS, o * 128 : (o + 1) * 128]
        for n in range(8):
            message = lines[y * 8 + n].astype(BF)
            for zl in range(2):
                out_ref[(((n % 2) * 4 + y) * 2 + zl) * 4 + n // 2] = message


def _conv_kernel(where_ref, raw_ref, near_own, far_own, near_other, far_other, out_ref, lines, grid, xs, wt, sh, acc, outs, sems):
    x, core, zh, first = where_ref[0], where_ref[1], where_ref[2], where_ref[3]
    copies = []
    own_refs = (near_own.at[0], near_own.at[1], far_own, near_own.at[2])
    other_refs = (near_other.at[0], near_other.at[1], far_other, near_other.at[2])
    for k in range(4):
        xo = lax.rem(x + k, 4)
        for z in range(2):
            for o, ref in enumerate((own_refs[k], other_refs[k])):
                slab = lax.rem(zh + z, 2) * 2 + lax.rem(core + o, 2)
                copies.append(
                    pltpu.make_async_copy(
                        ref.at[z, pl.ds(0, 28)],
                        wt.at[:, xo, :, pl.ds(pl.multiple_of(slab * 128, 128), 128)],
                        sems.at[len(copies)],
                    )
                )
        copies.append(pltpu.make_async_copy(own_refs[k].at[0, 28], sh.at[xo], sems.at[len(copies)]))
    for copy in copies:
        copy.start()

    grid[...] = jnp.zeros_like(grid)
    outs[...] = jnp.zeros_like(outs)

    def gather(s):
        for j in range(8):
            lines[s % 2, j] = raw_ref[s * 8 + j].astype(F32)
            for q in range(4):
                for i in range(3):
                    start = q * SPOTS + i * 9
                    grid[s % 2, q, i, HALO + j * 9 : HALO + j * 9 + 9] = lines[s % 2, j, start : start + 9]
        for dc in range(-3, 4):
            for q in range(4):
                rows = [grid[s % 2, q, i, HALO + dc * 6 : HALO + dc * 6 + 72] for i in range(3)]
                rows.append(jnp.zeros((GRID - 216, 128), F32))
                xs[s % 2, dc + 3, :, q * 128 : (q + 1) * 128] = jnp.concatenate(rows, axis=0).astype(BF)

    def multiply(s):
        base = 0
        for n, group in enumerate(GROUPS):
            valid = [t for t, (d, a, _) in enumerate(group) if 0 <= s - d * a < 8]
            for t in range(valid[0], valid[-1] + 1, 2):
                taps = group[t : min(t + 2, valid[-1] + 1)]
                w = wt[base + t : base + t + len(taps)].reshape(len(taps) * 128, 512)
                y = lax.dot_general(
                    xs[s % 2, taps[0][0] * taps[0][2] + 3], w, (((1,), (1,)), ((), ())), preferred_element_type=F32
                )
                for k, (d, a, _) in enumerate(taps):
                    part = y[:, k * 128 : (k + 1) * 128]
                    g = s - d * a
                    if (d, g) in reached:
                        acc[d, g] += part
                    else:
                        acc[d, g] = part
                        reached.add((d, g))
            base += len(group)

    def send(g):
        for j in range(8):
            for b in range(4):
                for i in range(3):
                    start = b * SPOTS + i * 9
                    outs[j, start : start + 9] = acc[b, g, i * 72 + j * 9 : i * 72 + j * 9 + 9] + shifts[b]
            out_ref[g * 8 + j] = outs[j].astype(BF)

    reached = set()
    gather(0)
    for copy in copies:
        copy.wait()

    lane = lax.broadcasted_iota(jnp.int32, (1, 128), 1)
    shifts = []
    for b in range(4):
        line = jnp.zeros((1, 128), F32)
        for xo in range(4):
            terms = sh[xo].astype(F32)
            whole = (terms[0:8] + terms[8:16] + terms[16:24])[b : b + 1]
            if xo > 0:
                whole = pltpu.roll(whole, xo * 32, 1)
            line = jnp.where((lane >= xo * 32) & (lane < xo * 32 + 32), whole, line)
        shifts.append(jnp.where(first == 0, line, 0.0))

    for s in range(8):
        if s < 7:
            gather(s + 1)
        multiply(s)
        if s >= 3:
            send(s - 3)
    for g in range(5, 8):
        send(g)


CONV_SCRATCH = [
    pltpu.VMEM((2, 8, ROWS, 128), F32),
    pltpu.VMEM((2, 4, 3, HALO + 72 + HALO + 4, 128), F32),
    pltpu.VMEM((2, 7, GRID, 512), BF),
    pltpu.VMEM((28, 4, 32, 512), BF),
    pltpu.VMEM((4, 32, 128), BF),
    pltpu.VMEM((4, 8, GRID, 128), F32),
    pltpu.VMEM((8, ROWS, 128), F32),
    pltpu.SemaphoreType.DMA((20,)),
]


def _final_kernel(in_ref, proj_ref, cls_ref, lab_ref, u_ref, v_ref, out_ref, loss_ref, lines, pyr):
    lines[...] = jnp.zeros_like(lines)
    for h in range(2):
        for xq in range(4):
            r = h * 4 + xq
            for zl in range(2):
                total = in_ref[((h * 4 + 0) * 2 + zl) * 4 + xq].astype(F32)
                for y in range(1, 4):
                    total = total + in_ref[((h * 4 + y) * 2 + zl) * 4 + xq].astype(F32)
                lines[r * 2 + zl, 0:ROWS] = jnp.maximum(total, 0.0)
                for b in range(4):
                    pyr[r * 32 : (r + 1) * 32, b * 256 + zl * 128 : b * 256 + (zl + 1) * 128] = lines[
                        r * 2 + zl, b * SPOTS : b * SPOTS + 32
                    ].astype(BF)
    mixed = jnp.dot(pyr[...], proj_ref[...], preferred_element_type=F32)
    projected = jnp.maximum(mixed, 0.0).astype(BF)
    out_ref[...] = jnp.dot(u_ref[...], projected, preferred_element_type=F32).astype(BF)
    rows = jnp.dot(v_ref[...], projected, preferred_element_type=F32).astype(BF)
    logits = lax.dot_general(cls_ref[...], rows, (((1,), (1,)), ((), ())), preferred_element_type=F32)
    total = jnp.zeros((1, 216), F32)
    chosen = jnp.zeros((1, 216), F32)
    for k in range(3):
        total = total + jnp.exp(logits[k : k + 1])
        chosen = chosen + jnp.where(lab_ref[...] == k, logits[k : k + 1], 0.0)
    loss = jnp.log(total) - chosen
    for r in range(12):
        line = loss if r == 0 else pltpu.roll(loss, 216 - r * 18, 1)
        loss_ref[r // 2, r % 2 : r % 2 + 1, :] = line[:, :18]


def body(features, atrous_weight, point_weight, branch_shift, proj_weight, class_weight, labels):
    x, zh = lax.axis_index("x"), lax.axis_index("zh")
    core, y = lax.axis_index("core"), lax.axis_index("y")
    where = jnp.stack([x, core, zh, y]).astype(jnp.int32)

    weights = pl.pallas_call(
        _weights_kernel,
        out_shape=jax.ShapeDtypeStruct((29, 32, 128), BF),
        scratch_shapes=[pltpu.VMEM((32, 128), F32)],
        name="weights",
    )(atrous_weight.transpose(0, 1, 2, 4, 3).reshape(27, 32, 128), point_weight.T, branch_shift)
    swapped = lax.ppermute(weights, "zh", [(0, 1), (1, 0)])

    flat = features.transpose(1, 2, 0, 3).reshape(216, 2048)
    messages = pl.pallas_call(
        _pack_kernel,
        out_shape=jax.ShapeDtypeStruct((64, ROWS, 128), BF),
        scratch_shapes=[pltpu.VMEM((32, ROWS, 128), F32)],
        compiler_params=pltpu.CompilerParams(vmem_limit_bytes=32 * MIB),
        name="pack",
    )(jnp.asarray(_pack_matrix(), BF), flat)

    messages, swapped = lax.optimization_barrier((messages, swapped))
    pair = jnp.stack([weights, swapped])
    def step(piece, k):
        return lax.ppermute(piece, "x", [(i, (i - k) % 4) for i in range(4)])

    def swap(piece):
        return lax.ppermute(piece, "core", [(0, 1), (1, 0)])

    right, left = step(pair, 1), step(pair, -1)
    near_own = pl.pallas_call(
        _join_kernel,
        out_shape=jax.ShapeDtypeStruct((3, 2, 29, 32, 128), BF),
        cost_estimate=pl.CostEstimate(flops=JOIN_FLOPS, bytes_accessed=2800000, transcendentals=0),
        name="join",
    )(pair, right, left)
    far_own = jnp.stack([step(right[0], 1), step(left[1], -1)])
    near_other, far_other = swap(near_own), swap(far_own)
    raw = lax.all_to_all(messages, ("zh", "y", "zl", "x"), 0, 0, tiled=True)
    partial = pl.pallas_call(
        _conv_kernel,
        out_shape=jax.ShapeDtypeStruct((64, ROWS, 128), BF),
        in_specs=[
            pl.BlockSpec(memory_space=pltpu.SMEM),
            pl.BlockSpec(memory_space=pltpu.VMEM),
        ]
        + [pl.BlockSpec(memory_space=pl.ANY)] * 4,
        scratch_shapes=CONV_SCRATCH,
        compiler_params=pltpu.CompilerParams(vmem_limit_bytes=40 * MIB),
        name="conv",
    )(where, raw, near_own, far_own, near_other, far_other)

    arrived = lax.all_to_all(partial, ("zh", "y", "zl", "x"), 0, 0, tiled=True)
    by_cols, by_samples = _unpack_matrices()
    classes = jnp.concatenate([class_weight.T, jnp.zeros((5, 256), BF)])
    projected, loss = pl.pallas_call(
        _final_kernel,
        out_shape=(jax.ShapeDtypeStruct((216, 256), BF), jax.ShapeDtypeStruct((6, 2, 18), F32)),
        scratch_shapes=[pltpu.VMEM((16, ROWS + 8, 128), F32), pltpu.VMEM((256, 1024), BF)],
        compiler_params=pltpu.CompilerParams(vmem_limit_bytes=32 * MIB),
        name="final",
    )(
        arrived,
        proj_weight,
        classes,
        labels.transpose(1, 0, 2).reshape(1, 216),
        jnp.asarray(by_cols, BF),
        jnp.asarray(by_samples, BF),
    )
    return (
        projected.reshape(6, 18, 2, 256).transpose(2, 0, 1, 3),
        loss.transpose(1, 0, 2),
    )


def solution(mesh):
    fine = Mesh(mesh.devices.reshape(2, 4, 2, 2, 4), ("zh", "y", "core", "zl", "x"))
    tile, chan = ("zh", "y", "core"), ("zl", "x")
    return jax.shard_map(
        body,
        mesh=fine,
        in_specs=(
            P(None, tile, chan, None),
            P(None, None, None, tile, chan),
            P(tile, chan),
            P(None, chan),
            P(),
            P(),
            P(None, tile, chan),
        ),
        out_specs=(P(None, tile, chan, None), P(None, tile, chan)),
        check_vma=False,
    )
```

time: 141 us -> 108 us (0.77)
  waiting for transfers between devices: 68.9 us -> 49.1 us
  local copies, waits for them, and re-layouts: 23 us -> 8.58 us
  starting transfers between devices: 24.7 us -> 29.7 us
  other arithmetic: 2.53 us -> 0.17 us
    all_to_all x1, waiting for transfers between devices: 23.5 us -> 0.01 us  [body(): raw = lax.all_to_all(messages, ('zh', 'y', 'zl', 'x'), 0, 0, tiled=True)]
    unnamed x46 -> x24, local copies, waits for them, and re-layouts: 19.8 us -> 3.48 us
    ppermute x4 -> x6, waiting for transfers between devices: 9.95 us -> 19.8 us  [the longest x4 18.1 us: step(): return lax.ppermute(piece, 'x', [(i, (i - k) % 4) for i in range(4)])]
    ppermute x1, waiting for transfers between devices: 5.78 us -> 1.68 us  [body(): swapped = lax.ppermute(weights, 'zh', [(0, 1), (1, 0)])]
    all_to_all x1, starting transfers between devices: 8.61 us -> 11 us  [body(): raw = lax.all_to_all(messages, ('zh', 'y', 'zl', 'x'), 0, 0, tiled=True)]
    all_to_all x1, starting transfers between devices: 6.14 us -> 8.26 us  [body(): arrived = lax.all_to_all(partial, ('zh', 'y', 'zl', 'x'), 0, 0, tiled=True)]
    reshape x1, local copies, waits for them, and re-layouts: 0.33 us -> 2.4 us  [body(): flat = features.transpose(1, 2, 0, 3).reshape(216, 2048)]
    all_to_all x1, waiting for transfers between devices: 29.6 us -> 27.6 us  [body(): arrived = lax.all_to_all(partial, ('zh', 'y', 'zl', 'x'), 0, 0, tiled=True)]
  transfers between devices with their start and end apart: 7 -> 9, of which waited for: 4 -> 5; matrix products, arithmetic and copies ran while one was open for 2% -> 4% of each run, Pallas kernels for 1% -> 4%
where the time goes in v2:
time: 108 us
  waiting for transfers between devices  49.1 us (45%)
  starting transfers between devices  29.7 us (28%)
  Pallas kernels  19.2 us (18%)
  local copies, waits for them, and re-layouts  8.58 us (8%)
    all_to_all x1, waiting for transfers between devices, body(): arrived = lax.all_to_all(partial, ('zh', 'y', 'zl', 'x'), 0, 0, tiled=True)  27.6 us
    ppermute x4, waiting for transfers between devices, step(): return lax.ppermute(piece, 'x', [(i, (i - k) % 4) for i in range(4)])  18.1 us
    pallas_call x1, Pallas kernels, body(): pl.pallas_call(_conv_kernel, out_shape=jax.ShapeDtypeStruct((64, ROWS, 12...  11.5 us
    all_to_all x1, starting transfers between devices, body(): raw = lax.all_to_all(messages, ('zh', 'y', 'zl', 'x'), 0, 0, tiled=True)  11 us
    all_to_all x1, starting transfers between devices, body(): arrived = lax.all_to_all(partial, ('zh', 'y', 'zl', 'x'), 0, 0, tiled=True)  8.26 us
    ppermute x4, starting transfers between devices, step(): return lax.ppermute(piece, 'x', [(i, (i - k) % 4) for i in range(4)])  6.2 us
    ppermute x1, starting transfers between devices, body(): swapped = lax.ppermute(weights, 'zh', [(0, 1), (1, 0)])  3.96 us
    unnamed x24, local copies, waits for them, and re-layouts  3.48 us
  transfers between devices with their start and end apart: 9, of which 5 were waited for; matrix products, arithmetic and copies ran while one was open for 4% of the time, Pallas kernels for 4%

profile of v2, /device:TPU:0, one launch (start us, length us, event | category | flops | bytes accessed | tf_op | source)
XLA Modules:
  0.0 107.6 jit_solution(15356670390453300473)
XLA Ops:
  0.6 0.0 copy-start.3
  0.6 1.7 %weights.1 = bf16[29,32,128]{2,1,0:T(8,128)(2,1)} custom-call(bf16[27,32,128]{2,1,0:T(8,128)(2,1)} %bitcast.26, bf16[32,128]{1,0:T(8,128)(2,1)} %bitcast.28, f32[4,32]{1,0:T(4,128)} %shift_ref.1), custom_call_target="tpu_custom_call" | custom-call | tf_op jit(solution)/shard_map/weights/pallas_call | solution.py:234
  2.4 4.0 %collective-permute-start = (bf16[29,32,128]{2,1,0:T(8,128)(2,1)}, bf16[29,32,128]{2,1,0:T(8,128)(2,1)S(1)}, u32[]{:S(2)}, u32[]{:S(2)}) collective-permute-start(bf16[29,32,128]{2,1,0:T(8,128)(2,1)} %weights.1), channel_id=1, source_target_pairs={{0,64},{64,0},{1,65},{65,1},{2,66},{66,2},{3,67},{67,3},{4,68},{68... | collective-permute-start | bytes 712712 | tf_op jit(solution)/shard_map/ppermute | solution.py:240
  6.3 2.4 %reshape.16.f_ref = bf16[216,2048]{1,0:T(8,128)(2,1)S(1)} reshape(bf16[6,18,2,2048]{3,2,1,0:T(2,128)(2,1)} %bitcast.22) | data formatting | bytes 1769472 | tf_op jit(solution)/shard_map/reshape | solution.py:242
  8.7 1.9 %pack.1 = bf16[64,112,128]{2,1,0:T(8,128)(2,1)} custom-call(bf16[256,216]{1,0:T(8,128)(2,1)S(1)} %copy-done.3, bf16[216,2048]{1,0:T(8,128)(2,1)S(1)} %reshape.16.f_ref), custom_call_target="tpu_custom_call" | custom-call | tf_op jit(solution)/shard_map/pack/pallas_call | solution.py:243
  10.6 1.7 %collective-permute-done = bf16[29,32,128]{2,1,0:T(8,128)(2,1)S(1)} collective-permute-done((bf16[29,32,128]{2,1,0:T(8,128)(2,1)}, bf16[29,32,128]{2,1,0:T(8,128)(2,1)S(1)}, u32[]{:S(2)}, u32[]{:S(2)}) %collective-permute-start) | collective-permute-done | bytes 237600 | tf_op jit(solution)/shard_map/ppermute | solution.py:240
  12.4 2.8 %collective-permute-start.1 = (bf16[2,29,32,128]{3,2,1,0:T(8,128)(2,1)S(1)}, bf16[2,29,32,128]{3,2,1,0:T(8,128)(2,1)S(1)}, u32[]{:S(2)}, u32[]{:S(2)}) collective-permute-start(bf16[2,29,32,128]{3,2,1,0:T(8,128)(2,1)S(1)} %pad_maximum_fusion.a_ref), channel_id=1, source_target_pairs={{0,3},{1,0},{2,1},{3,2},{4,7},{5,4},{6,5},{7,6},{8,11},{9,8},{10,9... | collective-permute-start | bytes 1425416 | tf_op jit(solution)/shard_map/ppermute | solution.py:254
  15.2 0.0 collective-permute-start.2
  15.2 11.0 %all-to-all-start = ((bf16[64,112,128]{2,1,0:T(8,128)(2,1)}), bf16[64,112,128]{2,1,0:T(8,128)(2,1)S(1)}, u32[]{:S(2)}, u32[]{:S(2)}) async-start(bf16[64,112,128]{2,1,0:T(8,128)(2,1)} %pack.1), calls=%async_computation | async-start | bytes 3670016 | tf_op jit(solution)/shard_map/all_to_all | solution.py:268
  26.2 0.0 collective-permute-done.1.b_ref
  26.2 3.5 %collective-permute-done.2.c_ref = bf16[2,29,32,128]{3,2,1,0:T(8,128)(2,1)S(1)} collective-permute-done((bf16[2,29,32,128]{3,2,1,0:T(8,128)(2,1)S(1)}, bf16[2,29,32,128]{3,2,1,0:T(8,128)(2,1)S(1)}, u32[]{:S(2)}, u32[]{:S(2)}) %collective-permute-start.2) | collective-permute-done | bytes 475168 | tf_op jit(solution)/shard_map/ppermute | solution.py:254
  29.7 0.8 copy-done.9
  30.5 2.5 %join.1.near_own = bf16[3,2,29,32,128]{4,3,2,1,0:T(8,128)(2,1)} custom-call(bf16[2,29,32,128]{3,2,1,0:T(8,128)(2,1)} %copy-done.7, bf16[2,29,32,128]{3,2,1,0:T(8,128)(2,1)} %copy-done.8, bf16[2,29,32,128]{3,2,1,0:T(8,128)(2,1)} %copy-done.9), custom_call_target="tpu_custom_call" | custom-call | flops 4000000000 | bytes 2800000 | tf_op jit(solution)/shard_map/join/pallas_call | solution.py:260
  33.0 1.0 slice_bitcast_fusion
  34.0 0.1 collective-permute-start.4
  34.1 1.0 slice_bitcast_fusion.1
  35.0 3.3 %collective-permute-start.3 = (bf16[29,32,128]{2,1,0:T(8,128)(2,1)S(1)}, bf16[29,32,128]{2,1,0:T(8,128)(2,1)S(1)}, u32[]{:S(2)}, u32[]{:S(2)}) collective-permute-start(bf16[29,32,128]{2,1,0:T(8,128)(2,1)S(1)} %slice_bitcast_fusion.1), channel_id=1, source_target_pairs={{0,3},{1,0},{2,1},{3,2},{4,7},{5,4},{6,5},{7,6},{8,11},{9,8},{10,9... | collective-permute-start | bytes 712712 | tf_op jit(solution)/shard_map/ppermute | solution.py:254
  38.3 14.6 %collective-permute-done.4 = bf16[29,32,128]{2,1,0:T(8,128)(2,1)S(1)} collective-permute-done((bf16[29,32,128]{2,1,0:T(8,128)(2,1)S(1)}, bf16[29,32,128]{2,1,0:T(8,128)(2,1)S(1)}, u32[]{:S(2)}, u32[]{:S(2)}) %collective-permute-start.4) | collective-permute-done | bytes 237600 | tf_op jit(solution)/shard_map/ppermute | solution.py:254
  53.0 0.3 collective-permute-start.6
  53.3 0.1 pad_add_fusion.where_ref
  53.3 1.7 %collective-permute-done.6.far_other = bf16[2,29,32,128]{3,2,1,0:T(8,128)(2,1)S(1)} collective-permute-done((bf16[2,29,32,128]{3,2,1,0:T(8,128)(2,1)S(1)}, bf16[2,29,32,128]{3,2,1,0:T(8,128)(2,1)S(1)}, u32[]{:S(2)}, u32[]{:S(2)}) %collective-permute-start.6) | collective-permute-done | bytes 475168 | tf_op jit(solution)/shard_map/ppermute | solution.py:257
  55.1 0.0 all-to-all-done.raw_ref
  55.1 0.0 collective-permute-done.5.near_other
  55.1 1.4 %copy-done.1 = bf16[3,2,29,32,128]{4,3,2,1,0:T(8,128)(2,1)S(1)} copy-done((bf16[3,2,29,32,128]{4,3,2,1,0:T(8,128)(2,1)S(1)}, bf16[3,2,29,32,128]{4,3,2,1,0:T(8,128)(2,1)}, u32[]{:S(2)}) %copy-start.1) | copy-done | bytes 1425432
  56.5 11.5 %conv.1 = bf16[64,112,128]{2,1,0:T(8,128)(2,1)S(1)} custom-call(s32[4]{0:T(128)S(1)} %pad_add_fusion.where_ref, bf16[64,112,128]{2,1,0:T(8,128)(2,1)S(1)} %all-to-all-done.raw_ref, bf16[3,2,29,32,128]{4,3,2,1,0:T(8,128)(2,1)S(1)} %copy-done.1, bf16[2,29,32,128]{3,2,1,0:T(8,128)(2,1)S(1)} %pad_maximum_fusion.1.far_own, ...), custom_call_target="tpu_custom_call" | custom-call | tf_op jit(solution)/shard_map/conv/pallas_call | solution.py:269
  67.9 1.3 %copy-done = bf16[64,112,128]{2,1,0:T(8,128)(2,1)} copy-done((bf16[64,112,128]{2,1,0:T(8,128)(2,1)}, bf16[64,112,128]{2,1,0:T(8,128)(2,1)S(1)}, u32[]{:S(2)}) %copy-start) | copy-done | bytes 1835032
  69.2 0.0 copy-start.5
  69.2 8.3 %all-to-all-start.1 = ((bf16[64,112,128]{2,1,0:T(8,128)(2,1)}), bf16[64,112,128]{2,1,0:T(8,128)(2,1)S(1)}, u32[]{:S(2)}, u32[]{:S(2)}) async-start(bf16[64,112,128]{2,1,0:T(8,128)(2,1)} %copy-done), calls=%async_computation.1 | async-start | bytes 3670016 | tf_op jit(solution)/shard_map/all_to_all | solution.py:282
  77.5 0.1 reshape.18.lab_ref
  77.6 27.6 %all-to-all-done.1.in_ref = bf16[64,112,128]{2,1,0:T(8,128)(2,1)S(1)} async-done(((bf16[64,112,128]{2,1,0:T(8,128)(2,1)}), bf16[64,112,128]{2,1,0:T(8,128)(2,1)S(1)}, u32[]{:S(2)}, u32[]{:S(2)}) %all-to-all-start.1) | async-done | bytes 1835040 | tf_op jit(solution)/shard_map/all_to_all | solution.py:282
  105.3 1.7 %final.1 = (bf16[216,256]{1,0:T(8,128)(2,1)S(1)}, f32[6,2,18]{2,1,0:T(2,128)}) custom-call(bf16[64,112,128]{2,1,0:T(8,128)(2,1)S(1)} %all-to-all-done.1.in_ref, bf16[1024,256]{1,0:T(8,128)(2,1)S(1)} %copy-done.2, bf16[8,256]{1,0:T(8,128)(2,1)S(1)} %concatenate.3.cls_ref, s32[1,216]{1,0:T(1,128)S(1)} %reshape.18.lab_ref, bf16[216,256]{1,0:T(8,128)(2,1)S(1)} %copy-done.4, ...), custom_call_target="tpu_custom_call" | custom-call | tf_op jit(solution)/shard_map/final/pallas_call | solution.py:285
  106.9 0.7 reshape.19
  (24 shorter events, 0.1 us)
Async XLA Ops:
  0.6 8.1 %copy-start.3 = (bf16[256,216]{1,0:T(8,128)(2,1)S(1)}, bf16[256,216]{1,0:T(8,128)(2,1)}, u32[]{:S(2)}) copy-start(bf16[256,216]{1,0:T(8,128)(2,1)} %constant.25.clone.p_ref) | copy-start | bytes 331780
  2.4 9.9 %collective-permute-start = (bf16[29,32,128]{2,1,0:T(8,128)(2,1)}, bf16[29,32,128]{2,1,0:T(8,128)(2,1)S(1)}, u32[]{:S(2)}, u32[]{:S(2)}) collective-permute-start(bf16[29,32,128]{2,1,0:T(8,128)(2,1)} %weights.1), channel_id=1, source_target_pairs={{0,64},{64,0},{1,65},{65,1},{2,66},{66,2},{3,67},{67,3},{4,68},{68... | collective-permute-start | bytes 712712 | tf_op jit(solution)/shard_map/ppermute | solution.py:240
  8.7 3.6 %copy-start.6 = (bf16[29,32,128]{2,1,0:T(8,128)(2,1)S(1)}, bf16[29,32,128]{2,1,0:T(8,128)(2,1)}, u32[]{:S(2)}) copy-start(bf16[29,32,128]{2,1,0:T(8,128)(2,1)} %weights.1) | copy-start | bytes 712708
  12.4 2.8 %copy-start.7 = (bf16[2,29,32,128]{3,2,1,0:T(8,128)(2,1)}, bf16[2,29,32,128]{3,2,1,0:T(8,128)(2,1)S(1)}, u32[]{:S(2)}) copy-start(bf16[2,29,32,128]{3,2,1,0:T(8,128)(2,1)S(1)} %pad_maximum_fusion.a_ref) | copy-start | bytes 1425412
  12.4 13.8 %collective-permute-start.1 = (bf16[2,29,32,128]{3,2,1,0:T(8,128)(2,1)S(1)}, bf16[2,29,32,128]{3,2,1,0:T(8,128)(2,1)S(1)}, u32[]{:S(2)}, u32[]{:S(2)}) collective-permute-start(bf16[2,29,32,128]{3,2,1,0:T(8,128)(2,1)S(1)} %pad_maximum_fusion.a_ref), channel_id=1, source_target_pairs={{0,3},{1,0},{2,1},{3,2},{4,7},{5,4},{6,5},{7,6},{8,11},{9,8},{10,9... | collective-permute-start | bytes 1425416 | tf_op jit(solution)/shard_map/ppermute | solution.py:254
  15.2 14.5 %collective-permute-start.2 = (bf16[2,29,32,128]{3,2,1,0:T(8,128)(2,1)S(1)}, bf16[2,29,32,128]{3,2,1,0:T(8,128)(2,1)S(1)}, u32[]{:S(2)}, u32[]{:S(2)}) collective-permute-start(bf16[2,29,32,128]{3,2,1,0:T(8,128)(2,1)S(1)} %pad_maximum_fusion.a_ref), channel_id=1, source_target_pairs={{0,1},{1,2},{2,3},{3,0},{4,5},{5,6},{6,7},{7,4},{8,9},{9,10},{10,1... | collective-permute-start | bytes 1425416 | tf_op jit(solution)/shard_map/ppermute | solution.py:254
  15.2 39.9 %all-to-all-start = ((bf16[64,112,128]{2,1,0:T(8,128)(2,1)}), bf16[64,112,128]{2,1,0:T(8,128)(2,1)S(1)}, u32[]{:S(2)}, u32[]{:S(2)}) async-start(bf16[64,112,128]{2,1,0:T(8,128)(2,1)} %pack.1), calls=%async_computation | async-start | bytes 3670016 | tf_op jit(solution)/shard_map/all_to_all | solution.py:268
  26.2 3.5 %copy-start.8 = (bf16[2,29,32,128]{3,2,1,0:T(8,128)(2,1)}, bf16[2,29,32,128]{3,2,1,0:T(8,128)(2,1)S(1)}, u32[]{:S(2)}) copy-start(bf16[2,29,32,128]{3,2,1,0:T(8,128)(2,1)S(1)} %collective-permute-done.1.b_ref) | copy-start | bytes 1425412
  29.7 0.8 copy-start.9
  33.0 22.1 %collective-permute-start.5 = (bf16[3,2,29,32,128]{4,3,2,1,0:T(8,128)(2,1)}, bf16[3,2,29,32,128]{4,3,2,1,0:T(8,128)(2,1)}, u32[]{:S(2)}, u32[]{:S(2)}) collective-permute-start(bf16[3,2,29,32,128]{4,3,2,1,0:T(8,128)(2,1)} %join.1.near_own), channel_id=1, source_target_pairs={{0,8},{8,0},{1,9},{9,1},{2,10},{10,2},{3,11},{11,3},{4,12},{12,4},... | collective-permute-start | bytes 4276232 | tf_op jit(solution)/shard_map/ppermute | solution.py:257
  34.0 19.0 %collective-permute-start.4 = (bf16[29,32,128]{2,1,0:T(8,128)(2,1)S(1)}, bf16[29,32,128]{2,1,0:T(8,128)(2,1)S(1)}, u32[]{:S(2)}, u32[]{:S(2)}) collective-permute-start(bf16[29,32,128]{2,1,0:T(8,128)(2,1)S(1)} %slice_bitcast_fusion), channel_id=1, source_target_pairs={{0,1},{1,2},{2,3},{3,0},{4,5},{5,6},{6,7},{7,4},{8,9},{9,10},{10,1... | collective-permute-start | bytes 712712 | tf_op jit(solution)/shard_map/ppermute | solution.py:254
  35.0 17.9 %collective-permute-start.3 = (bf16[29,32,128]{2,1,0:T(8,128)(2,1)S(1)}, bf16[29,32,128]{2,1,0:T(8,128)(2,1)S(1)}, u32[]{:S(2)}, u32[]{:S(2)}) collective-permute-start(bf16[29,32,128]{2,1,0:T(8,128)(2,1)S(1)} %slice_bitcast_fusion.1), channel_id=1, source_target_pairs={{0,3},{1,0},{2,1},{3,2},{4,7},{5,4},{6,5},{7,6},{8,11},{9,8},{10,9... | collective-permute-start | bytes 712712 | tf_op jit(solution)/shard_map/ppermute | solution.py:254
  53.0 2.1 %collective-permute-start.6 = (bf16[2,29,32,128]{3,2,1,0:T(8,128)(2,1)S(1)}, bf16[2,29,32,128]{3,2,1,0:T(8,128)(2,1)S(1)}, u32[]{:S(2)}, u32[]{:S(2)}) collective-permute-start(bf16[2,29,32,128]{3,2,1,0:T(8,128)(2,1)S(1)} %pad_maximum_fusion.1.far_own), channel_id=1, source_target_pairs={{0,8},{8,0},{1,9},{9,1},{2,10},{10,2},{3,11},{11,3},{4,12},{12,4},... | collective-permute-start | bytes 1425416 | tf_op jit(solution)/shard_map/ppermute | solution.py:257
  55.1 1.4 %copy-start.1 = (bf16[3,2,29,32,128]{4,3,2,1,0:T(8,128)(2,1)S(1)}, bf16[3,2,29,32,128]{4,3,2,1,0:T(8,128)(2,1)}, u32[]{:S(2)}) copy-start(bf16[3,2,29,32,128]{4,3,2,1,0:T(8,128)(2,1)} %join.1.near_own) | copy-start | bytes 4276228
  67.9 1.3 %copy-start = (bf16[64,112,128]{2,1,0:T(8,128)(2,1)}, bf16[64,112,128]{2,1,0:T(8,128)(2,1)S(1)}, u32[]{:S(2)}) copy-start(bf16[64,112,128]{2,1,0:T(8,128)(2,1)S(1)} %conv.1) | copy-start | bytes 5505028
  69.2 8.3 %copy-start.10 = (s32[2,6,18]{2,0,1:T(2,128)S(1)}, s32[2,6,18]{2,0,1:T(2,128)}, u32[]{:S(2)}) copy-start(s32[2,6,18]{2,0,1:T(2,128)} %param.16) | copy-start | bytes 2596
  69.2 8.4 %copy-start.11 = (bf16[256,3]{0,1:T(4,128)(2,1)S(1)}, bf16[256,3]{0,1:T(4,128)(2,1)}, u32[]{:S(2)}) copy-start(bf16[256,3]{0,1:T(4,128)(2,1)} %param.15) | copy-start | bytes 4612
  69.2 36.0 %copy-start.2 = (bf16[1024,256]{1,0:T(8,128)(2,1)S(1)}, bf16[1024,256]{1,0:T(8,128)(2,1)}, u32[]{:S(2)}) copy-start(bf16[1024,256]{1,0:T(8,128)(2,1)} %proj_ref.1) | copy-start | bytes 1572868
  69.2 36.0 %copy-start.4 = (bf16[216,256]{1,0:T(8,128)(2,1)S(1)}, bf16[216,256]{1,0:T(8,128)(2,1)}, u32[]{:S(2)}) copy-start(bf16[216,256]{1,0:T(8,128)(2,1)} %constant.26.clone.u_ref) | copy-start | bytes 331780
  69.2 36.0 %copy-start.5 = (bf16[216,256]{1,0:T(8,128)(2,1)S(1)}, bf16[216,256]{1,0:T(8,128)(2,1)}, u32[]{:S(2)}) copy-start(bf16[216,256]{1,0:T(8,128)(2,1)} %constant.27.clone.v_ref) | copy-start | bytes 331780
  69.2 36.0 %all-to-all-start.1 = ((bf16[64,112,128]{2,1,0:T(8,128)(2,1)}), bf16[64,112,128]{2,1,0:T(8,128)(2,1)S(1)}, u32[]{:S(2)}, u32[]{:S(2)}) async-start(bf16[64,112,128]{2,1,0:T(8,128)(2,1)} %copy-done), calls=%async_computation.1 | async-start | bytes 3670016 | tf_op jit(solution)/shard_map/all_to_all | solution.py:282

commit v3 on v2

--- a/solution.py
+++ b/solution.py
@@ -13,7 +13,7 @@
 BF = jnp.bfloat16
 F32 = jnp.float32
 MIB = 1024 * 1024
-JOIN_FLOPS = 4000000000
+PICK_FLOPS = 20000000000
 
 
 def _spot(i, t, c):
@@ -70,38 +70,39 @@
     out_ref[28] = terms[...].astype(BF)
 
 
-def _join_kernel(a_ref, b_ref, c_ref, out_ref):
-    for n, ref in enumerate((a_ref, b_ref, c_ref)):
-        out_ref[n] = ref[...]
+def _pick_kernel(core_ref, a_ref, b_ref, out_ref):
+    @pl.when(core_ref[0] == 0)
+    def _():
+        out_ref[...] = a_ref[...]
+
+    @pl.when(core_ref[0] == 1)
+    def _():
+        out_ref[...] = b_ref[...]
 
 
 def _pack_kernel(p_ref, f_ref, out_ref, lines):
     p = p_ref[...]
     lines[...] = jnp.zeros_like(lines)
-    for y in range(4):
-        for z in range(2):
-            part = f_ref[:, z * 1024 + y * 256 : z * 1024 + (y + 1) * 256]
-            rows = jnp.dot(p, part, preferred_element_type=F32)
-            for n in range(8):
-                for o in range(2):
-                    start = (z * 2 + o) * SPOTS
-                    lines[y * 8 + n, start : start + SPOTS] = rows[n * 32 : n * 32 + SPOTS, o * 128 : (o + 1) * 128]
+    for q in range(4):
+        rows = jnp.dot(p, f_ref[:, q * 512 : (q + 1) * 512], preferred_element_type=F32)
         for n in range(8):
-            message = lines[y * 8 + n].astype(BF)
+            for o in range(4):
+                lines[q * 8 + n, o * SPOTS : (o + 1) * SPOTS] = rows[n * 32 : n * 32 + SPOTS, o * 128 : (o + 1) * 128]
+            message = lines[q * 8 + n].astype(BF)
             for zl in range(2):
-                out_ref[(((n % 2) * 4 + y) * 2 + zl) * 4 + n // 2] = message
-
-
-def _conv_kernel(where_ref, raw_ref, near_own, far_own, near_other, far_other, out_ref, lines, grid, xs, wt, sh, acc, outs, sems):
-    x, core, zh, first = where_ref[0], where_ref[1], where_ref[2], where_ref[3]
+                out_ref[((q * 2 + n % 2) * 2 + zl) * 4 + n // 2] = message
+
+
+def _conv_kernel(where_ref, raw_ref, *refs):
+    own_refs, other_refs, out_ref = refs[:4], refs[4:8], refs[8]
+    lines, grid, xs, wt, sh, acc, outs, sems = refs[9:]
+    x, core, half, first = where_ref[0], where_ref[1], where_ref[2], where_ref[3]
     copies = []
-    own_refs = (near_own.at[0], near_own.at[1], far_own, near_own.at[2])
-    other_refs = (near_other.at[0], near_other.at[1], far_other, near_other.at[2])
     for k in range(4):
         xo = lax.rem(x + k, 4)
         for z in range(2):
             for o, ref in enumerate((own_refs[k], other_refs[k])):
-                slab = lax.rem(zh + z, 2) * 2 + lax.rem(core + o, 2)
+                slab = lax.rem(half + z, 2) * 2 + lax.rem(core + o, 2)
                 copies.append(
                     pltpu.make_async_copy(
                         ref.at[z, pl.ds(0, 28)],
@@ -202,9 +203,9 @@
         for xq in range(4):
             r = h * 4 + xq
             for zl in range(2):
-                total = in_ref[((h * 4 + 0) * 2 + zl) * 4 + xq].astype(F32)
-                for y in range(1, 4):
-                    total = total + in_ref[((h * 4 + y) * 2 + zl) * 4 + xq].astype(F32)
+                total = in_ref[(h * 2 + zl) * 4 + xq].astype(F32)
+                for q in range(1, 4):
+                    total = total + in_ref[((q * 2 + h) * 2 + zl) * 4 + xq].astype(F32)
                 lines[r * 2 + zl, 0:ROWS] = jnp.maximum(total, 0.0)
                 for b in range(4):
                     pyr[r * 32 : (r + 1) * 32, b * 256 + zl * 128 : b * 256 + (zl + 1) * 128] = lines[
@@ -229,7 +230,7 @@
 def body(features, atrous_weight, point_weight, branch_shift, proj_weight, class_weight, labels):
     x, zh = lax.axis_index("x"), lax.axis_index("zh")
     core, y = lax.axis_index("core"), lax.axis_index("y")
-    where = jnp.stack([x, core, zh, y]).astype(jnp.int32)
+    where = jnp.stack([x, core, y % 2, zh * 2 + y // 2]).astype(jnp.int32)
 
     weights = pl.pallas_call(
         _weights_kernel,
@@ -237,7 +238,7 @@
         scratch_shapes=[pltpu.VMEM((32, 128), F32)],
         name="weights",
     )(atrous_weight.transpose(0, 1, 2, 4, 3).reshape(27, 32, 128), point_weight.T, branch_shift)
-    swapped = lax.ppermute(weights, "zh", [(0, 1), (1, 0)])
+    swapped = lax.ppermute(weights, "y", [(0, 1), (1, 0), (2, 3), (3, 2)])
 
     flat = features.transpose(1, 2, 0, 3).reshape(216, 2048)
     messages = pl.pallas_call(
@@ -250,34 +251,38 @@
 
     messages, swapped = lax.optimization_barrier((messages, swapped))
     pair = jnp.stack([weights, swapped])
-    def step(piece, k):
-        return lax.ppermute(piece, "x", [(i, (i - k) % 4) for i in range(4)])
-
     def swap(piece):
         return lax.ppermute(piece, "core", [(0, 1), (1, 0)])
 
-    right, left = step(pair, 1), step(pair, -1)
-    near_own = pl.pallas_call(
-        _join_kernel,
-        out_shape=jax.ShapeDtypeStruct((3, 2, 29, 32, 128), BF),
-        cost_estimate=pl.CostEstimate(flops=JOIN_FLOPS, bytes_accessed=2800000, transcendentals=0),
-        name="join",
-    )(pair, right, left)
-    far_own = jnp.stack([step(right[0], 1), step(left[1], -1)])
-    near_other, far_other = swap(near_own), swap(far_own)
+    right = lax.ppermute(pair, "x", [(i, (i - 1) % 4) for i in range(4)])
+    left = lax.ppermute(pair, "x", [(i, (i + 1) % 4) for i in range(4)])
+    picked = pl.pallas_call(
+        _pick_kernel,
+        out_shape=jax.ShapeDtypeStruct(pair.shape, BF),
+        in_specs=[
+            pl.BlockSpec(memory_space=pltpu.SMEM),
+            pl.BlockSpec(memory_space=pltpu.VMEM),
+            pl.BlockSpec(memory_space=pltpu.VMEM),
+        ],
+        cost_estimate=pl.CostEstimate(flops=PICK_FLOPS, bytes_accessed=1400000, transcendentals=0),
+        name="pick",
+    )(core.astype(jnp.int32).reshape(1), right, left)
+    far = lax.ppermute(
+        picked, ("core", "x"), [(c * 4 + i, c * 4 + (i - 1 + 2 * c) % 4) for c in range(2) for i in range(4)]
+    )
+    own = [pair, right, far, left]
+    other = [swap(piece) for piece in own]
     raw = lax.all_to_all(messages, ("zh", "y", "zl", "x"), 0, 0, tiled=True)
     partial = pl.pallas_call(
         _conv_kernel,
         out_shape=jax.ShapeDtypeStruct((64, ROWS, 128), BF),
-        in_specs=[
-            pl.BlockSpec(memory_space=pltpu.SMEM),
-            pl.BlockSpec(memory_space=pltpu.VMEM),
-        ]
-        + [pl.BlockSpec(memory_space=pl.ANY)] * 4,
+        in_specs=[pl.BlockSpec(memory_space=pltpu.SMEM), pl.BlockSpec(memory_space=pltpu.VMEM)]
+        + [pl.BlockSpec(memory_space=pl.ANY)] * 8,
+        out_specs=pl.BlockSpec(memory_space=pltpu.VMEM),
         scratch_shapes=CONV_SCRATCH,
-        compiler_params=pltpu.CompilerParams(vmem_limit_bytes=40 * MIB),
+        compiler_params=pltpu.CompilerParams(vmem_limit_bytes=24 * MIB),
         name="conv",
-    )(where, raw, near_own, far_own, near_other, far_other)
+    )(where, raw, *own, *other)
 
     arrived = lax.all_to_all(partial, ("zh", "y", "zl", "x"), 0, 0, tiled=True)
     by_cols, by_samples = _unpack_matrices()

time: 108 us -> 106 us (0.981)
  local copies, waits for them, and re-layouts: 8.58 us -> 5.51 us
  waiting for transfers between devices: 49.1 us -> 51.3 us
    ppermute x5 -> x4, starting transfers between devices: 10.2 us -> 7.1 us  [the longest x1 2.99 us: body(): right = lax.ppermute(pair, 'x', [(i, (i - 1) % 4) for i in range(4)])]
    squeeze x2 -> x0, local copies, waits for them, and re-layouts: 1.92 us -> none  [body(): far_own = jnp.stack([step(right[0], 1), step(left[1], -1)])]
    ppermute x5 -> x4, waiting for transfers between devices: 19.8 us -> 21.6 us  [the longest x1 18.8 us: body(): lax.ppermute(picked, ('core', 'x'), [(c * 4 + i, c * 4 + (i - 1 + 2 * c)...]
    ppermute x2 -> x4, starting transfers between devices: 0.27 us -> 1.84 us  [swap(): return lax.ppermute(piece, 'core', [(0, 1), (1, 0)])]
    unnamed x24 -> x20, local copies, waits for them, and re-layouts: 3.48 us -> 2.33 us
  transfers between devices with their start and end apart: 9 -> 10, of which waited for: 5 -> 6; matrix products, arithmetic and copies ran while one was open for 4% -> 2% of each run, Pallas kernels for 4% -> 4%
where the time goes in v3:
time: 106 us
  waiting for transfers between devices  51.3 us (48%)
  starting transfers between devices  29.2 us (28%)
  Pallas kernels  18.9 us (18%)
  local copies, waits for them, and re-layouts  5.51 us (5%)
    all_to_all x1, waiting for transfers between devices, body(): arrived = lax.all_to_all(partial, ('zh', 'y', 'zl', 'x'), 0, 0, tiled=True)  27.6 us
    ppermute x1, waiting for transfers between devices, body(): lax.ppermute(picked, ('core', 'x'), [(c * 4 + i, c * 4 + (i - 1 + 2 * c)...  18.8 us
    pallas_call x1, Pallas kernels, body(): pl.pallas_call(_conv_kernel, out_shape=jax.ShapeDtypeStruct((64, ROWS, 12...  11.7 us
    all_to_all x1, starting transfers between devices, body(): raw = lax.all_to_all(messages, ('zh', 'y', 'zl', 'x'), 0, 0, tiled=True)  11.6 us
    all_to_all x1, starting transfers between devices, body(): arrived = lax.all_to_all(partial, ('zh', 'y', 'zl', 'x'), 0, 0, tiled=True)  8.59 us
    ppermute x1, starting transfers between devices, body(): right = lax.ppermute(pair, 'x', [(i, (i - 1) % 4) for i in range(4)])  2.99 us
    ppermute x1, starting transfers between devices, body(): lax.ppermute(picked, ('core', 'x'), [(c * 4 + i, c * 4 + (i - 1 + 2 * c)...  2.44 us
    reshape x1, local copies, waits for them, and re-layouts, body(): flat = features.transpose(1, 2, 0, 3).reshape(216, 2048)  2.4 us
  transfers between devices with their start and end apart: 10, of which 6 were waited for; matrix products, arithmetic and copies ran while one was open for 2% of the time, Pallas kernels for 4%

profile of v3, /device:TPU:0, one launch (start us, length us, event | category | flops | bytes accessed | tf_op | source)
XLA Modules:
  0.0 105.8 jit_solution(10566601205318352250)
XLA Ops:
  0.6 0.0 copy-start.4
  0.6 1.7 %weights.1 = bf16[29,32,128]{2,1,0:T(8,128)(2,1)} custom-call(bf16[27,32,128]{2,1,0:T(8,128)(2,1)} %bitcast.18, bf16[32,128]{1,0:T(8,128)(2,1)} %bitcast.20, f32[4,32]{1,0:T(4,128)} %shift_ref.1), custom_call_target="tpu_custom_call" | custom-call | tf_op jit(solution)/shard_map/weights/pallas_call | solution.py:235
  2.3 1.7 %collective-permute-start = (bf16[29,32,128]{2,1,0:T(8,128)(2,1)}, bf16[29,32,128]{2,1,0:T(8,128)(2,1)S(1)}, u32[]{:S(2)}, u32[]{:S(2)}) collective-permute-start(bf16[29,32,128]{2,1,0:T(8,128)(2,1)} %weights.1), channel_id=1, source_target_pairs={{0,16},{16,0},{32,48},{48,32},{1,17},{17,1},{33,49},{49,33},{2,18}... | collective-permute-start | bytes 712712 | tf_op jit(solution)/shard_map/ppermute | solution.py:241
  4.0 2.4 %reshape.17.f_ref = bf16[216,2048]{1,0:T(8,128)(2,1)S(1)} reshape(bf16[6,18,2,2048]{3,2,1,0:T(2,128)(2,1)} %bitcast.16) | data formatting | bytes 1769472 | tf_op jit(solution)/shard_map/reshape | solution.py:243
  6.4 1.9 %pack.1 = bf16[64,112,128]{2,1,0:T(8,128)(2,1)} custom-call(bf16[256,216]{1,0:T(8,128)(2,1)S(1)} %copy-done.4, bf16[216,2048]{1,0:T(8,128)(2,1)S(1)} %reshape.17.f_ref), custom_call_target="tpu_custom_call" | custom-call | tf_op jit(solution)/shard_map/pack/pallas_call | solution.py:244
  8.3 1.7 %collective-permute-done = bf16[29,32,128]{2,1,0:T(8,128)(2,1)S(1)} collective-permute-done((bf16[29,32,128]{2,1,0:T(8,128)(2,1)}, bf16[29,32,128]{2,1,0:T(8,128)(2,1)S(1)}, u32[]{:S(2)}, u32[]{:S(2)}) %collective-permute-start) | collective-permute-done | bytes 237600 | tf_op jit(solution)/shard_map/ppermute | solution.py:241
  10.0 3.0 %collective-permute-start.1 = (bf16[2,29,32,128]{3,2,1,0:T(8,128)(2,1)S(1)}, bf16[2,29,32,128]{3,2,1,0:T(8,128)(2,1)S(1)}, u32[]{:S(2)}, u32[]{:S(2)}) collective-permute-start(bf16[2,29,32,128]{3,2,1,0:T(8,128)(2,1)S(1)} %pad_maximum_fusion.refs_0_), channel_id=1, source_target_pairs={{0,3},{1,0},{2,1},{3,2},{4,7},{5,4},{6,5},{7,6},{8,11},{9,8},{10,9... | collective-permute-start | bytes 1425416 | tf_op jit(solution)/shard_map/ppermute | solution.py:257
  13.0 11.6 %all-to-all-start = ((bf16[64,112,128]{2,1,0:T(8,128)(2,1)}), bf16[64,112,128]{2,1,0:T(8,128)(2,1)S(1)}, u32[]{:S(2)}, u32[]{:S(2)}) async-start(bf16[64,112,128]{2,1,0:T(8,128)(2,1)} %pack.1), calls=%async_computation | async-start | bytes 3670016 | tf_op jit(solution)/shard_map/all_to_all | solution.py:275
  24.7 0.0 collective-permute-done.1.a_ref.refs_1_
  24.7 1.1 %collective-permute-done.2.b_ref.refs_3_ = bf16[2,29,32,128]{3,2,1,0:T(8,128)(2,1)} collective-permute-done((bf16[2,29,32,128]{3,2,1,0:T(8,128)(2,1)S(1)}, bf16[2,29,32,128]{3,2,1,0:T(8,128)(2,1)}, u32[]{:S(2)}, u32[]{:S(2)}) %collective-permute-start.2) | collective-permute-done | bytes 475168 | tf_op jit(solution)/shard_map/ppermute | solution.py:258
  25.8 2.0 %pick.1 = bf16[2,29,32,128]{3,2,1,0:T(8,128)(2,1)} custom-call(s32[1]{0:T(128)} %bitcast.1.core_ref, bf16[2,29,32,128]{3,2,1,0:T(8,128)(2,1)} %copy-done.2, bf16[2,29,32,128]{3,2,1,0:T(8,128)(2,1)} %collective-permute-done.2.b_ref.refs_3_), custom_call_target="tpu_custom_call" | custom-call | flops 20000000000 | bytes 1400000 | tf_op jit(solution)/shard_map/pick/pallas_call | solution.py:259
  27.8 2.4 %collective-permute-start.3 = (bf16[2,29,32,128]{3,2,1,0:T(8,128)(2,1)}, bf16[2,29,32,128]{3,2,1,0:T(8,128)(2,1)S(1)}, u32[]{:S(2)}, u32[]{:S(2)}) collective-permute-start(bf16[2,29,32,128]{3,2,1,0:T(8,128)(2,1)} %pick.1), channel_id=1, source_target_pairs={{0,3},{1,0},{2,1},{3,2},{8,9},{9,10},{10,11},{11,8},{4,7},{5,4},{6... | collective-permute-start | bytes 1425416 | tf_op jit(solution)/shard_map/ppermute | solution.py:270
  30.2 0.0 collective-permute-start.4
  30.2 0.5 collective-permute-start.5
  30.8 0.0 collective-permute-start.7
  30.8 18.8 %collective-permute-done.3.refs_2_ = bf16[2,29,32,128]{3,2,1,0:T(8,128)(2,1)S(1)} collective-permute-done((bf16[2,29,32,128]{3,2,1,0:T(8,128)(2,1)}, bf16[2,29,32,128]{3,2,1,0:T(8,128)(2,1)S(1)}, u32[]{:S(2)}, u32[]{:S(2)}) %collective-permute-start.3) | collective-permute-done | bytes 475168 | tf_op jit(solution)/shard_map/ppermute | solution.py:270
  49.5 1.3 %collective-permute-start.6 = (bf16[2,29,32,128]{3,2,1,0:T(8,128)(2,1)S(1)}, bf16[2,29,32,128]{3,2,1,0:T(8,128)(2,1)}, u32[]{:S(2)}, u32[]{:S(2)}) collective-permute-start(bf16[2,29,32,128]{3,2,1,0:T(8,128)(2,1)S(1)} %collective-permute-done.3.refs_2_), channel_id=1, source_target_pairs={{0,8},{8,0},{1,9},{9,1},{2,10},{10,2},{3,11},{11,3},{4,12},{12,4},... | collective-permute-start | bytes 1425416 | tf_op jit(solution)/shard_map/ppermute | solution.py:255
  50.9 0.1 pad_add_fusion.where_ref
  50.9 0.0 collective-permute-done.4.refs_4_
  50.9 0.0 collective-permute-done.5.refs_5_
  50.9 0.0 collective-permute-done.7.refs_7_
  51.0 1.5 %collective-permute-done.6.refs_6_ = bf16[2,29,32,128]{3,2,1,0:T(8,128)(2,1)} collective-permute-done((bf16[2,29,32,128]{3,2,1,0:T(8,128)(2,1)S(1)}, bf16[2,29,32,128]{3,2,1,0:T(8,128)(2,1)}, u32[]{:S(2)}, u32[]{:S(2)}) %collective-permute-start.6) | collective-permute-done | bytes 475168 | tf_op jit(solution)/shard_map/ppermute | solution.py:255
  52.5 0.6 all-to-all-done.raw_ref
  53.0 1.0 copy-done.3
  54.1 11.7 %conv.1 = bf16[64,112,128]{2,1,0:T(8,128)(2,1)S(1)} custom-call(s32[4]{0:T(128)S(1)} %pad_add_fusion.where_ref, bf16[64,112,128]{2,1,0:T(8,128)(2,1)S(1)} %all-to-all-done.raw_ref, bf16[2,29,32,128]{3,2,1,0:T(8,128)(2,1)S(1)} %pad_maximum_fusion.refs_0_, bf16[2,29,32,128]{3,2,1,0:T(8,128)(2,1)S(1)} %copy-done.3, ...), custom_call_target="tpu_custom_call" | custom-call | tf_op jit(solution)/shard_map/conv/pallas_call | solution.py:276
  65.8 1.3 %copy-done = bf16[64,112,128]{2,1,0:T(8,128)(2,1)} copy-done((bf16[64,112,128]{2,1,0:T(8,128)(2,1)}, bf16[64,112,128]{2,1,0:T(8,128)(2,1)S(1)}, u32[]{:S(2)}) %copy-start) | copy-done | bytes 1835032
  67.1 0.0 copy-start.6
  67.1 8.6 %all-to-all-start.1 = ((bf16[64,112,128]{2,1,0:T(8,128)(2,1)}), bf16[64,112,128]{2,1,0:T(8,128)(2,1)S(1)}, u32[]{:S(2)}, u32[]{:S(2)}) async-start(bf16[64,112,128]{2,1,0:T(8,128)(2,1)} %copy-done), calls=%async_computation.1 | async-start | bytes 3670016 | tf_op jit(solution)/shard_map/all_to_all | solution.py:287
  75.7 0.1 reshape.19.lab_ref
  75.8 27.6 %all-to-all-done.1.in_ref = bf16[64,112,128]{2,1,0:T(8,128)(2,1)S(1)} async-done(((bf16[64,112,128]{2,1,0:T(8,128)(2,1)}), bf16[64,112,128]{2,1,0:T(8,128)(2,1)S(1)}, u32[]{:S(2)}, u32[]{:S(2)}) %all-to-all-start.1) | async-done | bytes 1835040 | tf_op jit(solution)/shard_map/all_to_all | solution.py:287
  103.5 1.6 %final.1 = (bf16[216,256]{1,0:T(8,128)(2,1)S(1)}, f32[6,2,18]{2,1,0:T(2,128)}) custom-call(bf16[64,112,128]{2,1,0:T(8,128)(2,1)S(1)} %all-to-all-done.1.in_ref, bf16[1024,256]{1,0:T(8,128)(2,1)S(1)} %copy-done.1, bf16[8,256]{1,0:T(8,128)(2,1)S(1)} %concatenate.3.cls_ref, s32[1,216]{1,0:T(1,128)S(1)} %reshape.19.lab_ref, bf16[216,256]{1,0:T(8,128)(2,1)S(1)} %copy-done.5, ...), custom_call_target="tpu_custom_call" | custom-call | tf_op jit(solution)/shard_map/final/pallas_call | solution.py:290
  105.1 0.7 reshape.20
  (19 shorter events, 0.1 us)
Async XLA Ops:
  0.6 5.8 %copy-start.4 = (bf16[256,216]{1,0:T(8,128)(2,1)S(1)}, bf16[256,216]{1,0:T(8,128)(2,1)}, u32[]{:S(2)}) copy-start(bf16[256,216]{1,0:T(8,128)(2,1)} %constant.49.clone.p_ref) | copy-start | bytes 331780
  2.3 7.6 %collective-permute-start = (bf16[29,32,128]{2,1,0:T(8,128)(2,1)}, bf16[29,32,128]{2,1,0:T(8,128)(2,1)S(1)}, u32[]{:S(2)}, u32[]{:S(2)}) collective-permute-start(bf16[29,32,128]{2,1,0:T(8,128)(2,1)} %weights.1), channel_id=1, source_target_pairs={{0,16},{16,0},{32,48},{48,32},{1,17},{17,1},{33,49},{49,33},{2,18}... | collective-permute-start | bytes 712712 | tf_op jit(solution)/shard_map/ppermute | solution.py:241
  6.4 3.6 %copy-start.7 = (bf16[29,32,128]{2,1,0:T(8,128)(2,1)S(1)}, bf16[29,32,128]{2,1,0:T(8,128)(2,1)}, u32[]{:S(2)}) copy-start(bf16[29,32,128]{2,1,0:T(8,128)(2,1)} %weights.1) | copy-start | bytes 712708
  10.0 14.6 %collective-permute-start.1 = (bf16[2,29,32,128]{3,2,1,0:T(8,128)(2,1)S(1)}, bf16[2,29,32,128]{3,2,1,0:T(8,128)(2,1)S(1)}, u32[]{:S(2)}, u32[]{:S(2)}) collective-permute-start(bf16[2,29,32,128]{3,2,1,0:T(8,128)(2,1)S(1)} %pad_maximum_fusion.refs_0_), channel_id=1, source_target_pairs={{0,3},{1,0},{2,1},{3,2},{4,7},{5,4},{6,5},{7,6},{8,11},{9,8},{10,9... | collective-permute-start | bytes 1425416 | tf_op jit(solution)/shard_map/ppermute | solution.py:257
  13.0 12.8 %collective-permute-start.2 = (bf16[2,29,32,128]{3,2,1,0:T(8,128)(2,1)S(1)}, bf16[2,29,32,128]{3,2,1,0:T(8,128)(2,1)}, u32[]{:S(2)}, u32[]{:S(2)}) collective-permute-start(bf16[2,29,32,128]{3,2,1,0:T(8,128)(2,1)S(1)} %pad_maximum_fusion.refs_0_), channel_id=1, source_target_pairs={{0,1},{1,2},{2,3},{3,0},{4,5},{5,6},{6,7},{7,4},{8,9},{9,10},{10,1... | collective-permute-start | bytes 1425416 | tf_op jit(solution)/shard_map/ppermute | solution.py:258
  13.0 40.0 %all-to-all-start = ((bf16[64,112,128]{2,1,0:T(8,128)(2,1)}), bf16[64,112,128]{2,1,0:T(8,128)(2,1)S(1)}, u32[]{:S(2)}, u32[]{:S(2)}) async-start(bf16[64,112,128]{2,1,0:T(8,128)(2,1)} %pack.1), calls=%async_computation | async-start | bytes 3670016 | tf_op jit(solution)/shard_map/all_to_all | solution.py:275
  24.7 1.1 %copy-start.2 = (bf16[2,29,32,128]{3,2,1,0:T(8,128)(2,1)}, bf16[2,29,32,128]{3,2,1,0:T(8,128)(2,1)S(1)}, u32[]{:S(2)}) copy-start(bf16[2,29,32,128]{3,2,1,0:T(8,128)(2,1)S(1)} %collective-permute-done.1.a_ref.refs_1_) | copy-start | bytes 1425412
  27.8 21.7 %collective-permute-start.3 = (bf16[2,29,32,128]{3,2,1,0:T(8,128)(2,1)}, bf16[2,29,32,128]{3,2,1,0:T(8,128)(2,1)S(1)}, u32[]{:S(2)}, u32[]{:S(2)}) collective-permute-start(bf16[2,29,32,128]{3,2,1,0:T(8,128)(2,1)} %pick.1), channel_id=1, source_target_pairs={{0,3},{1,0},{2,1},{3,2},{8,9},{9,10},{10,11},{11,8},{4,7},{5,4},{6... | collective-permute-start | bytes 1425416 | tf_op jit(solution)/shard_map/ppermute | solution.py:270
  30.2 20.7 %collective-permute-start.4 = (bf16[2,29,32,128]{3,2,1,0:T(8,128)(2,1)S(1)}, bf16[2,29,32,128]{3,2,1,0:T(8,128)(2,1)S(1)}, u32[]{:S(2)}, u32[]{:S(2)}) collective-permute-start(bf16[2,29,32,128]{3,2,1,0:T(8,128)(2,1)S(1)} %pad_maximum_fusion.refs_0_), channel_id=1, source_target_pairs={{0,8},{8,0},{1,9},{9,1},{2,10},{10,2},{3,11},{11,3},{4,12},{12,4},... | collective-permute-start | bytes 1425416 | tf_op jit(solution)/shard_map/ppermute | solution.py:255
  30.2 20.7 %collective-permute-start.5 = (bf16[2,29,32,128]{3,2,1,0:T(8,128)(2,1)}, bf16[2,29,32,128]{3,2,1,0:T(8,128)(2,1)}, u32[]{:S(2)}, u32[]{:S(2)}) collective-permute-start(bf16[2,29,32,128]{3,2,1,0:T(8,128)(2,1)} %copy-done.2), channel_id=1, source_target_pairs={{0,8},{8,0},{1,9},{9,1},{2,10},{10,2},{3,11},{11,3},{4,12},{12,4},... | collective-permute-start | bytes 1425416 | tf_op jit(solution)/shard_map/ppermute | solution.py:255
  30.8 20.2 %collective-permute-start.7 = (bf16[2,29,32,128]{3,2,1,0:T(8,128)(2,1)}, bf16[2,29,32,128]{3,2,1,0:T(8,128)(2,1)}, u32[]{:S(2)}, u32[]{:S(2)}) collective-permute-start(bf16[2,29,32,128]{3,2,1,0:T(8,128)(2,1)} %collective-permute-done.2.b_ref.refs_3_), channel_id=1, source_target_pairs={{0,8},{8,0},{1,9},{9,1},{2,10},{10,2},{3,11},{11,3},{4,12},{12,4},... | collective-permute-start | bytes 1425416 | tf_op jit(solution)/shard_map/ppermute | solution.py:255
  49.5 2.9 %collective-permute-start.6 = (bf16[2,29,32,128]{3,2,1,0:T(8,128)(2,1)S(1)}, bf16[2,29,32,128]{3,2,1,0:T(8,128)(2,1)}, u32[]{:S(2)}, u32[]{:S(2)}) collective-permute-start(bf16[2,29,32,128]{3,2,1,0:T(8,128)(2,1)S(1)} %collective-permute-done.3.refs_2_), channel_id=1, source_target_pairs={{0,8},{8,0},{1,9},{9,1},{2,10},{10,2},{3,11},{11,3},{4,12},{12,4},... | collective-permute-start | bytes 1425416 | tf_op jit(solution)/shard_map/ppermute | solution.py:255
  53.0 1.0 copy-start.3
  65.8 1.3 %copy-start = (bf16[64,112,128]{2,1,0:T(8,128)(2,1)}, bf16[64,112,128]{2,1,0:T(8,128)(2,1)S(1)}, u32[]{:S(2)}) copy-start(bf16[64,112,128]{2,1,0:T(8,128)(2,1)S(1)} %conv.1) | copy-start | bytes 5505028
  67.1 8.6 %copy-start.8 = (s32[2,6,18]{2,0,1:T(2,128)S(1)}, s32[2,6,18]{2,0,1:T(2,128)}, u32[]{:S(2)}) copy-start(s32[2,6,18]{2,0,1:T(2,128)} %param.16) | copy-start | bytes 2596
  67.1 8.7 %copy-start.9 = (bf16[256,3]{0,1:T(4,128)(2,1)S(1)}, bf16[256,3]{0,1:T(4,128)(2,1)}, u32[]{:S(2)}) copy-start(bf16[256,3]{0,1:T(4,128)(2,1)} %param.15) | copy-start | bytes 4612
  67.1 36.4 %copy-start.1 = (bf16[1024,256]{1,0:T(8,128)(2,1)S(1)}, bf16[1024,256]{1,0:T(8,128)(2,1)}, u32[]{:S(2)}) copy-start(bf16[1024,256]{1,0:T(8,128)(2,1)} %proj_ref.1) | copy-start | bytes 1572868
  67.1 36.4 %copy-start.5 = (bf16[216,256]{1,0:T(8,128)(2,1)S(1)}, bf16[216,256]{1,0:T(8,128)(2,1)}, u32[]{:S(2)}) copy-start(bf16[216,256]{1,0:T(8,128)(2,1)} %constant.50.clone.u_ref) | copy-start | bytes 331780
  67.1 36.4 %copy-start.6 = (bf16[216,256]{1,0:T(8,128)(2,1)S(1)}, bf16[216,256]{1,0:T(8,128)(2,1)}, u32[]{:S(2)}) copy-start(bf16[216,256]{1,0:T(8,128)(2,1)} %constant.51.clone.v_ref) | copy-start | bytes 331780
  67.1 36.4 %all-to-all-start.1 = ((bf16[64,112,128]{2,1,0:T(8,128)(2,1)}), bf16[64,112,128]{2,1,0:T(8,128)(2,1)S(1)}, u32[]{:S(2)}, u32[]{:S(2)}) async-start(bf16[64,112,128]{2,1,0:T(8,128)(2,1)} %copy-done), calls=%async_computation.1 | async-start | bytes 3670016 | tf_op jit(solution)/shard_map/all_to_all | solution.py:287

commit v4 on v3

--- a/solution.py
+++ b/solution.py
@@ -1,3 +1,5 @@
+import itertools
+
 import jax
 import jax.numpy as jnp
 import numpy as np
@@ -34,7 +36,7 @@
 
 
 def _unpack_matrices():
-    by_cols = np.zeros((216, 256), np.float32)
+    by_cols = np.zeros((2, 108, 256), np.float32)
     by_samples = np.zeros((216, 256), np.float32)
     for h in range(2):
         for xq in range(4):
@@ -45,7 +47,7 @@
                         col = 3 * (2 * t + h) + c
                         b = xq // 2
                         src = (h * 4 + xq) * 32 + _spot(i, t, c)
-                        by_cols[(row * 18 + col) * 2 + b, src] = 1
+                        by_cols[b, row * 18 + col, src] = 1
                         by_samples[(row * 2 + b) * 18 + col, src] = 1
     return by_cols, by_samples
 
@@ -117,6 +119,11 @@
     grid[...] = jnp.zeros_like(grid)
     outs[...] = jnp.zeros_like(outs)
 
+    def window(dc):
+        low = max(0, -dc * 6) // 8 * 8
+        high = -(-min(72, 72 - dc * 6) // 8) * 8
+        return low, high - low, -(-3 * (high - low) // 16) * 16
+
     def gather(s):
         for j in range(8):
             lines[s % 2, j] = raw_ref[s * 8 + j].astype(F32)
@@ -124,30 +131,45 @@
                 for i in range(3):
                     start = q * SPOTS + i * 9
                     grid[s % 2, q, i, HALO + j * 9 : HALO + j * 9 + 9] = lines[s % 2, j, start : start + 9]
+            yield
         for dc in range(-3, 4):
             for q in range(4):
-                rows = [grid[s % 2, q, i, HALO + dc * 6 : HALO + dc * 6 + 72] for i in range(3)]
-                rows.append(jnp.zeros((GRID - 216, 128), F32))
-                xs[s % 2, dc + 3, :, q * 128 : (q + 1) * 128] = jnp.concatenate(rows, axis=0).astype(BF)
-
-    def multiply(s):
+                low, size, full = window(dc)
+                start = HALO + dc * 6 + low
+                rows = [grid[s % 2, q, i, start : start + size] for i in range(3)]
+                if full > 3 * size:
+                    rows.append(jnp.zeros((full - 3 * size, 128), F32))
+                rows = jnp.concatenate(rows, axis=0).astype(BF)
+                xs[s // 2 % 2, dc + 3, s % 2 * full : (s % 2 + 1) * full, q * 128 : (q + 1) * 128] = rows
+                yield
+
+    def multiply(m):
         base = 0
-        for n, group in enumerate(GROUPS):
-            valid = [t for t, (d, a, _) in enumerate(group) if 0 <= s - d * a < 8]
+        for group in GROUPS:
+            valid = [t for t, (d, a, _) in enumerate(group) if _meets(m, d, a)]
             for t in range(valid[0], valid[-1] + 1, 2):
                 taps = group[t : min(t + 2, valid[-1] + 1)]
                 w = wt[base + t : base + t + len(taps)].reshape(len(taps) * 128, 512)
+                dc = taps[0][0] * taps[0][2]
+                low, size, full = window(dc)
                 y = lax.dot_general(
-                    xs[s % 2, taps[0][0] * taps[0][2] + 3], w, (((1,), (1,)), ((), ())), preferred_element_type=F32
+                    xs[m % 2, dc + 3, : 2 * full], w, (((1,), (1,)), ((), ())), preferred_element_type=F32
                 )
                 for k, (d, a, _) in enumerate(taps):
-                    part = y[:, k * 128 : (k + 1) * 128]
-                    g = s - d * a
-                    if (d, g) in reached:
-                        acc[d, g] += part
-                    else:
-                        acc[d, g] = part
-                        reached.add((d, g))
+                    for n in range(2):
+                        g = 2 * m + n - d * a
+                        if not 0 <= g < 8:
+                            continue
+                        part = y[n * full : (n + 1) * full, k * 128 : (k + 1) * 128]
+                        if (d, g) not in reached:
+                            acc[d, g] = part
+                            reached.add((d, g))
+                        elif size == 72:
+                            acc[d, g] += part
+                        else:
+                            for i in range(3):
+                                acc[d, g, i * 72 + low : i * 72 + low + size] += part[i * size : (i + 1) * size]
+                yield
             base += len(group)
 
     def send(g):
@@ -157,9 +179,11 @@
                     start = b * SPOTS + i * 9
                     outs[j, start : start + 9] = acc[b, g, i * 72 + j * 9 : i * 72 + j * 9 + 9] + shifts[b]
             out_ref[g * 8 + j] = outs[j].astype(BF)
+            yield
 
     reached = set()
-    gather(0)
+    for _ in itertools.chain(gather(0), gather(1)):
+        pass
     for copy in copies:
         copy.wait()
 
@@ -175,20 +199,39 @@
             line = jnp.where((lane >= xo * 32) & (lane < xo * 32 + 32), whole, line)
         shifts.append(jnp.where(first == 0, line, 0.0))
 
-    for s in range(8):
-        if s < 7:
-            gather(s + 1)
-        multiply(s)
-        if s >= 3:
-            send(s - 3)
-    for g in range(5, 8):
-        send(g)
+    for m in range(4):
+        beside = []
+        if m == 3:
+            beside.extend((send(g), 8) for g in range(3))
+        else:
+            beside.extend((gather(s), 36) for s in (2 * m + 2, 2 * m + 3))
+        left = sum(n for _, n in beside)
+        steps = itertools.chain(*(step for step, _ in beside))
+        tiles = _tiles(m)
+        for n, _ in enumerate(multiply(m)):
+            share = -(-left // max(tiles - n, 1))
+            for _ in range(share):
+                next(steps, None)
+            left -= share
+        for _ in steps:
+            pass
+    for g in range(3, 8):
+        for _ in send(g):
+            pass
+
+
+def _meets(m, d, a):
+    return any(0 <= s - d * a < 8 for s in (2 * m, 2 * m + 1))
+
+
+def _tiles(m):
+    return sum(-(-sum(_meets(m, d, a) for d, a, _ in group) // 2) for group in GROUPS)
 
 
 CONV_SCRATCH = [
     pltpu.VMEM((2, 8, ROWS, 128), F32),
     pltpu.VMEM((2, 4, 3, HALO + 72 + HALO + 4, 128), F32),
-    pltpu.VMEM((2, 7, GRID, 512), BF),
+    pltpu.VMEM((2, 7, 2 * GRID, 512), BF),
     pltpu.VMEM((28, 4, 32, 512), BF),
     pltpu.VMEM((4, 32, 128), BF),
     pltpu.VMEM((4, 8, GRID, 128), F32),
@@ -213,7 +256,8 @@
                     ].astype(BF)
     mixed = jnp.dot(pyr[...], proj_ref[...], preferred_element_type=F32)
     projected = jnp.maximum(mixed, 0.0).astype(BF)
-    out_ref[...] = jnp.dot(u_ref[...], projected, preferred_element_type=F32).astype(BF)
+    for b in range(2):
+        out_ref[:, b, :] = jnp.dot(u_ref[b], projected, preferred_element_type=F32).astype(BF)
     rows = jnp.dot(v_ref[...], projected, preferred_element_type=F32).astype(BF)
     logits = lax.dot_general(cls_ref[...], rows, (((1,), (1,)), ((), ())), preferred_element_type=F32)
     total = jnp.zeros((1, 216), F32)
@@ -259,11 +303,7 @@
     picked = pl.pallas_call(
         _pick_kernel,
         out_shape=jax.ShapeDtypeStruct(pair.shape, BF),
-        in_specs=[
-            pl.BlockSpec(memory_space=pltpu.SMEM),
-            pl.BlockSpec(memory_space=pltpu.VMEM),
-            pl.BlockSpec(memory_space=pltpu.VMEM),
-        ],
+        in_specs=[pl.BlockSpec(memory_space=pltpu.SMEM)] + [pl.BlockSpec(memory_space=pltpu.VMEM)] * 2,
         cost_estimate=pl.CostEstimate(flops=PICK_FLOPS, bytes_accessed=1400000, transcendentals=0),
         name="pick",
     )(core.astype(jnp.int32).reshape(1), right, left)
@@ -289,7 +329,7 @@
     classes = jnp.concatenate([class_weight.T, jnp.zeros((5, 256), BF)])
     projected, loss = pl.pallas_call(
         _final_kernel,
-        out_shape=(jax.ShapeDtypeStruct((216, 256), BF), jax.ShapeDtypeStruct((6, 2, 18), F32)),
+        out_shape=(jax.ShapeDtypeStruct((108, 2, 256), BF), jax.ShapeDtypeStruct((6, 2, 18), F32)),
         scratch_shapes=[pltpu.VMEM((16, ROWS + 8, 128), F32), pltpu.VMEM((256, 1024), BF)],
         compiler_params=pltpu.CompilerParams(vmem_limit_bytes=32 * MIB),
         name="final",

time: 106 us -> 105 us (level)
    pallas_call x1, Pallas kernels: 11.7 us -> 10.6 us  [body(): pl.pallas_call(_conv_kernel, out_shape=jax.ShapeDtypeStruct((64, ROWS, 12...]
where the time goes in v4:
time: 105 us; the launch traced here: 104 us
  waiting for transfers between devices  51.3 us (49%)
  starting transfers between devices  29.2 us (28%)
  Pallas kernels  17.9 us (17%)
  local copies, waits for them, and re-layouts  4.82 us (5%)
    all_to_all x1, waiting for transfers between devices, body(): arrived = lax.all_to_all(partial, ('zh', 'y', 'zl', 'x'), 0, 0, tiled=True)  27.6 us
    ppermute x1, waiting for transfers between devices, body(): lax.ppermute(picked, ('core', 'x'), [(c * 4 + i, c * 4 + (i - 1 + 2 * c)...  18.8 us
    all_to_all x1, starting transfers between devices, body(): raw = lax.all_to_all(messages, ('zh', 'y', 'zl', 'x'), 0, 0, tiled=True)  11.6 us
    pallas_call x1, Pallas kernels, body(): pl.pallas_call(_conv_kernel, out_shape=jax.ShapeDtypeStruct((64, ROWS, 12...  10.6 us
    all_to_all x1, starting transfers between devices, body(): arrived = lax.all_to_all(partial, ('zh', 'y', 'zl', 'x'), 0, 0, tiled=True)  8.62 us
    ppermute x1, starting transfers between devices, body(): right = lax.ppermute(pair, 'x', [(i, (i - 1) % 4) for i in range(4)])  2.99 us
    ppermute x1, starting transfers between devices, body(): lax.ppermute(picked, ('core', 'x'), [(c * 4 + i, c * 4 + (i - 1 + 2 * c)...  2.44 us
    reshape x1, local copies, waits for them, and re-layouts, body(): flat = features.transpose(1, 2, 0, 3).reshape(216, 2048)  2.4 us
  transfers between devices with their start and end apart: 10, of which 6 were waited for; matrix products, arithmetic and copies ran while one was open for 2% of the time, Pallas kernels for 4%

profile of v4, /device:TPU:0, one launch (start us, length us, event | category | flops | bytes accessed | tf_op | source)
XLA Modules:
  0.0 104.1 jit_solution(5952987840195627413)
XLA Ops:
  0.6 0.0 copy-start.4
  0.6 1.7 %weights.1 = bf16[29,32,128]{2,1,0:T(8,128)(2,1)} custom-call(bf16[27,32,128]{2,1,0:T(8,128)(2,1)} %bitcast.20, bf16[32,128]{1,0:T(8,128)(2,1)} %bitcast.21, f32[4,32]{1,0:T(4,128)} %shift_ref.1), custom_call_target="tpu_custom_call" | custom-call | tf_op jit(solution)/shard_map/weights/pallas_call | solution.py:279
  2.3 1.7 %collective-permute-start = (bf16[29,32,128]{2,1,0:T(8,128)(2,1)}, bf16[29,32,128]{2,1,0:T(8,128)(2,1)S(1)}, u32[]{:S(2)}, u32[]{:S(2)}) collective-permute-start(bf16[29,32,128]{2,1,0:T(8,128)(2,1)} %weights.1), channel_id=1, source_target_pairs={{0,16},{16,0},{32,48},{48,32},{1,17},{17,1},{33,49},{49,33},{2,18}... | collective-permute-start | bytes 712712 | tf_op jit(solution)/shard_map/ppermute | solution.py:285
  4.0 2.4 %reshape.17.f_ref = bf16[216,2048]{1,0:T(8,128)(2,1)S(1)} reshape(bf16[6,18,2,2048]{3,2,1,0:T(2,128)(2,1)} %bitcast.18) | data formatting | bytes 1769472 | tf_op jit(solution)/shard_map/reshape | solution.py:287
  6.4 1.9 %pack.1 = bf16[64,112,128]{2,1,0:T(8,128)(2,1)} custom-call(bf16[256,216]{1,0:T(8,128)(2,1)S(1)} %copy-done.4, bf16[216,2048]{1,0:T(8,128)(2,1)S(1)} %reshape.17.f_ref), custom_call_target="tpu_custom_call" | custom-call | tf_op jit(solution)/shard_map/pack/pallas_call | solution.py:288
  8.3 1.7 %collective-permute-done = bf16[29,32,128]{2,1,0:T(8,128)(2,1)S(1)} collective-permute-done((bf16[29,32,128]{2,1,0:T(8,128)(2,1)}, bf16[29,32,128]{2,1,0:T(8,128)(2,1)S(1)}, u32[]{:S(2)}, u32[]{:S(2)}) %collective-permute-start) | collective-permute-done | bytes 237600 | tf_op jit(solution)/shard_map/ppermute | solution.py:285
  10.0 3.0 %collective-permute-start.1 = (bf16[2,29,32,128]{3,2,1,0:T(8,128)(2,1)S(1)}, bf16[2,29,32,128]{3,2,1,0:T(8,128)(2,1)S(1)}, u32[]{:S(2)}, u32[]{:S(2)}) collective-permute-start(bf16[2,29,32,128]{3,2,1,0:T(8,128)(2,1)S(1)} %pad_maximum_fusion.refs_0_), channel_id=1, source_target_pairs={{0,3},{1,0},{2,1},{3,2},{4,7},{5,4},{6,5},{7,6},{8,11},{9,8},{10,9... | collective-permute-start | bytes 1425416 | tf_op jit(solution)/shard_map/ppermute | solution.py:301
  13.0 0.0 collective-permute-start.2
  13.0 11.6 %all-to-all-start = ((bf16[64,112,128]{2,1,0:T(8,128)(2,1)}), bf16[64,112,128]{2,1,0:T(8,128)(2,1)S(1)}, u32[]{:S(2)}, u32[]{:S(2)}) async-start(bf16[64,112,128]{2,1,0:T(8,128)(2,1)} %pack.1), calls=%async_computation | async-start | bytes 3670016 | tf_op jit(solution)/shard_map/all_to_all | solution.py:315
  24.7 0.0 collective-permute-done.1.a_ref.refs_1_
  24.7 1.1 %collective-permute-done.2.b_ref.refs_3_ = bf16[2,29,32,128]{3,2,1,0:T(8,128)(2,1)} collective-permute-done((bf16[2,29,32,128]{3,2,1,0:T(8,128)(2,1)S(1)}, bf16[2,29,32,128]{3,2,1,0:T(8,128)(2,1)}, u32[]{:S(2)}, u32[]{:S(2)}) %collective-permute-start.2) | collective-permute-done | bytes 475168 | tf_op jit(solution)/shard_map/ppermute | solution.py:302
  25.8 2.0 %pick.1 = bf16[2,29,32,128]{3,2,1,0:T(8,128)(2,1)} custom-call(s32[1]{0:T(128)} %bitcast.1.core_ref, bf16[2,29,32,128]{3,2,1,0:T(8,128)(2,1)} %copy-done.2, bf16[2,29,32,128]{3,2,1,0:T(8,128)(2,1)} %collective-permute-done.2.b_ref.refs_3_), custom_call_target="tpu_custom_call" | custom-call | flops 20000000000 | bytes 1400000 | tf_op jit(solution)/shard_map/pick/pallas_call | solution.py:303
  27.8 2.4 %collective-permute-start.3 = (bf16[2,29,32,128]{3,2,1,0:T(8,128)(2,1)}, bf16[2,29,32,128]{3,2,1,0:T(8,128)(2,1)S(1)}, u32[]{:S(2)}, u32[]{:S(2)}) collective-permute-start(bf16[2,29,32,128]{3,2,1,0:T(8,128)(2,1)} %pick.1), channel_id=1, source_target_pairs={{0,3},{1,0},{2,1},{3,2},{8,9},{9,10},{10,11},{11,8},{4,7},{5,4},{6... | collective-permute-start | bytes 1425416 | tf_op jit(solution)/shard_map/ppermute | solution.py:310
  30.2 0.0 collective-permute-start.4
  30.2 0.5 collective-permute-start.5
  30.8 0.0 collective-permute-start.7
  30.8 18.8 %collective-permute-done.3.refs_2_ = bf16[2,29,32,128]{3,2,1,0:T(8,128)(2,1)S(1)} collective-permute-done((bf16[2,29,32,128]{3,2,1,0:T(8,128)(2,1)}, bf16[2,29,32,128]{3,2,1,0:T(8,128)(2,1)S(1)}, u32[]{:S(2)}, u32[]{:S(2)}) %collective-permute-start.3) | collective-permute-done | bytes 475168 | tf_op jit(solution)/shard_map/ppermute | solution.py:310
  49.5 1.3 %collective-permute-start.6 = (bf16[2,29,32,128]{3,2,1,0:T(8,128)(2,1)S(1)}, bf16[2,29,32,128]{3,2,1,0:T(8,128)(2,1)}, u32[]{:S(2)}, u32[]{:S(2)}) collective-permute-start(bf16[2,29,32,128]{3,2,1,0:T(8,128)(2,1)S(1)} %collective-permute-done.3.refs_2_), channel_id=1, source_target_pairs={{0,8},{8,0},{1,9},{9,1},{2,10},{10,2},{3,11},{11,3},{4,12},{12,4},... | collective-permute-start | bytes 1425416 | tf_op jit(solution)/shard_map/ppermute | solution.py:299
  50.9 0.1 pad_add_fusion.where_ref
  50.9 0.0 collective-permute-done.4.refs_4_
  50.9 0.0 collective-permute-done.5.refs_5_
  50.9 0.0 collective-permute-done.7.refs_7_
  51.0 1.5 %collective-permute-done.6.refs_6_ = bf16[2,29,32,128]{3,2,1,0:T(8,128)(2,1)} collective-permute-done((bf16[2,29,32,128]{3,2,1,0:T(8,128)(2,1)S(1)}, bf16[2,29,32,128]{3,2,1,0:T(8,128)(2,1)}, u32[]{:S(2)}, u32[]{:S(2)}) %collective-permute-start.6) | collective-permute-done | bytes 475168 | tf_op jit(solution)/shard_map/ppermute | solution.py:299
  52.5 0.6 all-to-all-done.raw_ref
  53.0 1.0 copy-done.3
  54.1 10.6 %conv.1 = bf16[64,112,128]{2,1,0:T(8,128)(2,1)S(1)} custom-call(s32[4]{0:T(128)S(1)} %pad_add_fusion.where_ref, bf16[64,112,128]{2,1,0:T(8,128)(2,1)S(1)} %all-to-all-done.raw_ref, bf16[2,29,32,128]{3,2,1,0:T(8,128)(2,1)S(1)} %pad_maximum_fusion.refs_0_, bf16[2,29,32,128]{3,2,1,0:T(8,128)(2,1)S(1)} %copy-done.3, ...), custom_call_target="tpu_custom_call" | custom-call | tf_op jit(solution)/shard_map/conv/pallas_call | solution.py:316
  64.7 1.3 %copy-done = bf16[64,112,128]{2,1,0:T(8,128)(2,1)} copy-done((bf16[64,112,128]{2,1,0:T(8,128)(2,1)}, bf16[64,112,128]{2,1,0:T(8,128)(2,1)S(1)}, u32[]{:S(2)}) %copy-start) | copy-done | bytes 1835032
  66.0 0.0 copy-start.6
  66.0 8.6 %all-to-all-start.1 = ((bf16[64,112,128]{2,1,0:T(8,128)(2,1)}), bf16[64,112,128]{2,1,0:T(8,128)(2,1)S(1)}, u32[]{:S(2)}, u32[]{:S(2)}) async-start(bf16[64,112,128]{2,1,0:T(8,128)(2,1)} %copy-done), calls=%async_computation.1 | async-start | bytes 3670016 | tf_op jit(solution)/shard_map/all_to_all | solution.py:327
  74.6 0.1 reshape.19.lab_ref
  74.8 27.6 %all-to-all-done.1.in_ref = bf16[64,112,128]{2,1,0:T(8,128)(2,1)S(1)} async-done(((bf16[64,112,128]{2,1,0:T(8,128)(2,1)}), bf16[64,112,128]{2,1,0:T(8,128)(2,1)S(1)}, u32[]{:S(2)}, u32[]{:S(2)}) %all-to-all-start.1) | async-done | bytes 1835040 | tf_op jit(solution)/shard_map/all_to_all | solution.py:327
  102.4 1.7 %final.1 = (bf16[108,2,256]{2,1,0:T(2,128)(2,1)}, f32[6,2,18]{2,1,0:T(2,128)}) custom-call(bf16[64,112,128]{2,1,0:T(8,128)(2,1)S(1)} %all-to-all-done.1.in_ref, bf16[1024,256]{1,0:T(8,128)(2,1)S(1)} %copy-done.1, bf16[8,256]{1,0:T(8,128)(2,1)S(1)} %concatenate.3.cls_ref, s32[1,216]{1,0:T(1,128)S(1)} %reshape.19.lab_ref, bf16[2,108,256]{2,1,0:T(8,128)(2,1)S(1)} %copy-done.5, ...), custom_call_target="tpu_custom_call" | custom-call | tf_op jit(solution)/shard_map/final/pallas_call | solution.py:330
  (18 shorter events, 0.1 us)
Async XLA Ops:
  0.6 5.8 %copy-start.4 = (bf16[256,216]{1,0:T(8,128)(2,1)S(1)}, bf16[256,216]{1,0:T(8,128)(2,1)}, u32[]{:S(2)}) copy-start(bf16[256,216]{1,0:T(8,128)(2,1)} %constant.49.clone.p_ref) | copy-start | bytes 331780
  2.3 7.6 %collective-permute-start = (bf16[29,32,128]{2,1,0:T(8,128)(2,1)}, bf16[29,32,128]{2,1,0:T(8,128)(2,1)S(1)}, u32[]{:S(2)}, u32[]{:S(2)}) collective-permute-start(bf16[29,32,128]{2,1,0:T(8,128)(2,1)} %weights.1), channel_id=1, source_target_pairs={{0,16},{16,0},{32,48},{48,32},{1,17},{17,1},{33,49},{49,33},{2,18}... | collective-permute-start | bytes 712712 | tf_op jit(solution)/shard_map/ppermute | solution.py:285
  6.4 3.6 %copy-start.7 = (bf16[29,32,128]{2,1,0:T(8,128)(2,1)S(1)}, bf16[29,32,128]{2,1,0:T(8,128)(2,1)}, u32[]{:S(2)}) copy-start(bf16[29,32,128]{2,1,0:T(8,128)(2,1)} %weights.1) | copy-start | bytes 712708
  10.0 14.6 %collective-permute-start.1 = (bf16[2,29,32,128]{3,2,1,0:T(8,128)(2,1)S(1)}, bf16[2,29,32,128]{3,2,1,0:T(8,128)(2,1)S(1)}, u32[]{:S(2)}, u32[]{:S(2)}) collective-permute-start(bf16[2,29,32,128]{3,2,1,0:T(8,128)(2,1)S(1)} %pad_maximum_fusion.refs_0_), channel_id=1, source_target_pairs={{0,3},{1,0},{2,1},{3,2},{4,7},{5,4},{6,5},{7,6},{8,11},{9,8},{10,9... | collective-permute-start | bytes 1425416 | tf_op jit(solution)/shard_map/ppermute | solution.py:301
  13.0 12.8 %collective-permute-start.2 = (bf16[2,29,32,128]{3,2,1,0:T(8,128)(2,1)S(1)}, bf16[2,29,32,128]{3,2,1,0:T(8,128)(2,1)}, u32[]{:S(2)}, u32[]{:S(2)}) collective-permute-start(bf16[2,29,32,128]{3,2,1,0:T(8,128)(2,1)S(1)} %pad_maximum_fusion.refs_0_), channel_id=1, source_target_pairs={{0,1},{1,2},{2,3},{3,0},{4,5},{5,6},{6,7},{7,4},{8,9},{9,10},{10,1... | collective-permute-start | bytes 1425416 | tf_op jit(solution)/shard_map/ppermute | solution.py:302
  13.0 40.0 %all-to-all-start = ((bf16[64,112,128]{2,1,0:T(8,128)(2,1)}), bf16[64,112,128]{2,1,0:T(8,128)(2,1)S(1)}, u32[]{:S(2)}, u32[]{:S(2)}) async-start(bf16[64,112,128]{2,1,0:T(8,128)(2,1)} %pack.1), calls=%async_computation | async-start | bytes 3670016 | tf_op jit(solution)/shard_map/all_to_all | solution.py:315
  24.7 1.1 %copy-start.2 = (bf16[2,29,32,128]{3,2,1,0:T(8,128)(2,1)}, bf16[2,29,32,128]{3,2,1,0:T(8,128)(2,1)S(1)}, u32[]{:S(2)}) copy-start(bf16[2,29,32,128]{3,2,1,0:T(8,128)(2,1)S(1)} %collective-permute-done.1.a_ref.refs_1_) | copy-start | bytes 1425412
  27.8 21.7 %collective-permute-start.3 = (bf16[2,29,32,128]{3,2,1,0:T(8,128)(2,1)}, bf16[2,29,32,128]{3,2,1,0:T(8,128)(2,1)S(1)}, u32[]{:S(2)}, u32[]{:S(2)}) collective-permute-start(bf16[2,29,32,128]{3,2,1,0:T(8,128)(2,1)} %pick.1), channel_id=1, source_target_pairs={{0,3},{1,0},{2,1},{3,2},{8,9},{9,10},{10,11},{11,8},{4,7},{5,4},{6... | collective-permute-start | bytes 1425416 | tf_op jit(solution)/shard_map/ppermute | solution.py:310
  30.2 20.7 %collective-permute-start.4 = (bf16[2,29,32,128]{3,2,1,0:T(8,128)(2,1)S(1)}, bf16[2,29,32,128]{3,2,1,0:T(8,128)(2,1)S(1)}, u32[]{:S(2)}, u32[]{:S(2)}) collective-permute-start(bf16[2,29,32,128]{3,2,1,0:T(8,128)(2,1)S(1)} %pad_maximum_fusion.refs_0_), channel_id=1, source_target_pairs={{0,8},{8,0},{1,9},{9,1},{2,10},{10,2},{3,11},{11,3},{4,12},{12,4},... | collective-permute-start | bytes 1425416 | tf_op jit(solution)/shard_map/ppermute | solution.py:299
  30.2 20.7 %collective-permute-start.5 = (bf16[2,29,32,128]{3,2,1,0:T(8,128)(2,1)}, bf16[2,29,32,128]{3,2,1,0:T(8,128)(2,1)}, u32[]{:S(2)}, u32[]{:S(2)}) collective-permute-start(bf16[2,29,32,128]{3,2,1,0:T(8,128)(2,1)} %copy-done.2), channel_id=1, source_target_pairs={{0,8},{8,0},{1,9},{9,1},{2,10},{10,2},{3,11},{11,3},{4,12},{12,4},... | collective-permute-start | bytes 1425416 | tf_op jit(solution)/shard_map/ppermute | solution.py:299
  30.8 20.2 %collective-permute-start.7 = (bf16[2,29,32,128]{3,2,1,0:T(8,128)(2,1)}, bf16[2,29,32,128]{3,2,1,0:T(8,128)(2,1)}, u32[]{:S(2)}, u32[]{:S(2)}) collective-permute-start(bf16[2,29,32,128]{3,2,1,0:T(8,128)(2,1)} %collective-permute-done.2.b_ref.refs_3_), channel_id=1, source_target_pairs={{0,8},{8,0},{1,9},{9,1},{2,10},{10,2},{3,11},{11,3},{4,12},{12,4},... | collective-permute-start | bytes 1425416 | tf_op jit(solution)/shard_map/ppermute | solution.py:299
  49.5 2.9 %collective-permute-start.6 = (bf16[2,29,32,128]{3,2,1,0:T(8,128)(2,1)S(1)}, bf16[2,29,32,128]{3,2,1,0:T(8,128)(2,1)}, u32[]{:S(2)}, u32[]{:S(2)}) collective-permute-start(bf16[2,29,32,128]{3,2,1,0:T(8,128)(2,1)S(1)} %collective-permute-done.3.refs_2_), channel_id=1, source_target_pairs={{0,8},{8,0},{1,9},{9,1},{2,10},{10,2},{3,11},{11,3},{4,12},{12,4},... | collective-permute-start | bytes 1425416 | tf_op jit(solution)/shard_map/ppermute | solution.py:299
  53.0 1.0 copy-start.3
  64.7 1.3 %copy-start = (bf16[64,112,128]{2,1,0:T(8,128)(2,1)}, bf16[64,112,128]{2,1,0:T(8,128)(2,1)S(1)}, u32[]{:S(2)}) copy-start(bf16[64,112,128]{2,1,0:T(8,128)(2,1)S(1)} %conv.1) | copy-start | bytes 5505028
  66.0 8.7 %copy-start.8 = (s32[2,6,18]{2,0,1:T(2,128)S(1)}, s32[2,6,18]{2,0,1:T(2,128)}, u32[]{:S(2)}) copy-start(s32[2,6,18]{2,0,1:T(2,128)} %param.16) | copy-start | bytes 2596
  66.0 8.8 %copy-start.9 = (bf16[256,3]{0,1:T(4,128)(2,1)S(1)}, bf16[256,3]{0,1:T(4,128)(2,1)}, u32[]{:S(2)}) copy-start(bf16[256,3]{0,1:T(4,128)(2,1)} %param.15) | copy-start | bytes 4612
  66.0 36.4 %copy-start.1 = (bf16[1024,256]{1,0:T(8,128)(2,1)S(1)}, bf16[1024,256]{1,0:T(8,128)(2,1)}, u32[]{:S(2)}) copy-start(bf16[1024,256]{1,0:T(8,128)(2,1)} %proj_ref.1) | copy-start | bytes 1572868
  66.0 36.4 %copy-start.5 = (bf16[2,108,256]{2,1,0:T(8,128)(2,1)S(1)}, bf16[2,108,256]{2,1,0:T(8,128)(2,1)}, u32[]{:S(2)}) copy-start(bf16[2,108,256]{2,1,0:T(8,128)(2,1)} %constant.50.clone.u_ref) | copy-start | bytes 331780
  66.0 36.4 %copy-start.6 = (bf16[216,256]{1,0:T(8,128)(2,1)S(1)}, bf16[216,256]{1,0:T(8,128)(2,1)}, u32[]{:S(2)}) copy-start(bf16[216,256]{1,0:T(8,128)(2,1)} %constant.51.clone.v_ref) | copy-start | bytes 331780
  66.0 36.4 %all-to-all-start.1 = ((bf16[64,112,128]{2,1,0:T(8,128)(2,1)}), bf16[64,112,128]{2,1,0:T(8,128)(2,1)S(1)}, u32[]{:S(2)}, u32[]{:S(2)}) async-start(bf16[64,112,128]{2,1,0:T(8,128)(2,1)} %copy-done), calls=%async_computation.1 | async-start | bytes 3670016 | tf_op jit(solution)/shard_map/all_to_all | solution.py:327

commit v5 on v4

--- a/solution.py
+++ b/solution.py
@@ -96,9 +96,12 @@
 
 
 def _conv_kernel(where_ref, raw_ref, *refs):
-    own_refs, other_refs, out_ref = refs[:4], refs[4:8], refs[8]
-    lines, grid, xs, wt, sh, acc, outs, sems = refs[9:]
+    own_refs, other_refs, out_ref = refs[:3], refs[3:6], refs[6]
+    lines, grid, xs, wt, sh, acc, outs, sems = refs[7:]
     x, core, half, first = where_ref[0], where_ref[1], where_ref[2], where_ref[3]
+    own_refs, other_refs = (
+        (near, sides.at[0], far, sides.at[1]) for near, sides, far in (own_refs, other_refs)
+    )
     copies = []
     for k in range(4):
         xo = lax.rem(x + k, 4)
@@ -310,14 +313,15 @@
     far = lax.ppermute(
         picked, ("core", "x"), [(c * 4 + i, c * 4 + (i - 1 + 2 * c) % 4) for c in range(2) for i in range(4)]
     )
-    own = [pair, right, far, left]
+    sides = jnp.stack([right, left])
+    own = [pair, sides, far]
     other = [swap(piece) for piece in own]
     raw = lax.all_to_all(messages, ("zh", "y", "zl", "x"), 0, 0, tiled=True)
     partial = pl.pallas_call(
         _conv_kernel,
         out_shape=jax.ShapeDtypeStruct((64, ROWS, 128), BF),
         in_specs=[pl.BlockSpec(memory_space=pltpu.SMEM), pl.BlockSpec(memory_space=pltpu.VMEM)]
-        + [pl.BlockSpec(memory_space=pl.ANY)] * 8,
+        + [pl.BlockSpec(memory_space=pl.ANY)] * 6,
         out_specs=pl.BlockSpec(memory_space=pltpu.VMEM),
         scratch_shapes=CONV_SCRATCH,
         compiler_params=pltpu.CompilerParams(vmem_limit_bytes=24 * MIB),

time: 105 us -> 104 us (level)
  waiting for transfers between devices: 51.3 us -> 49.8 us
  other arithmetic: 0.12 us -> 1.38 us
  local copies, waits for them, and re-layouts: 4.82 us -> 3.77 us
    ppermute x1, starting transfers between devices: 0.01 us -> 1.73 us  [body(): left = lax.ppermute(pair, 'x', [(i, (i + 1) % 4) for i in range(4)])]
    ppermute x1, starting transfers between devices: 2.99 us -> 1.58 us  [body(): right = lax.ppermute(pair, 'x', [(i, (i - 1) % 4) for i in range(4)])]
    another operation x0 -> x1, other arithmetic: none -> 1.26 us  [body(): sides = jnp.stack([right, left])]
    all_to_all x1, starting transfers between devices: 11.6 us -> 10.4 us  [body(): raw = lax.all_to_all(messages, ('zh', 'y', 'zl', 'x'), 0, 0, tiled=True)]
    ppermute x1, waiting for transfers between devices: 1.12 us -> 0.01 us  [body(): left = lax.ppermute(pair, 'x', [(i, (i + 1) % 4) for i in range(4)])]
    all_to_all x1, starting transfers between devices: 8.62 us -> 9.67 us  [body(): arrived = lax.all_to_all(partial, ('zh', 'y', 'zl', 'x'), 0, 0, tiled=True)]
    unnamed x20 -> x16, local copies, waits for them, and re-layouts: 2.33 us -> 1.28 us
  transfers between devices with their start and end apart: 10 -> 9, of which waited for: 6 -> 5; matrix products, arithmetic and copies ran while one was open for 2% -> 4% of each run, Pallas kernels for 4% -> 4%
where the time goes in v5:
time: 104 us; the launch traced here: 103 us
  waiting for transfers between devices  49.8 us (48%)
  starting transfers between devices  29.6 us (28%)
  Pallas kernels  17.9 us (17%)
  local copies, waits for them, and re-layouts  3.77 us (4%)
  other arithmetic  1.38 us (1%)
    all_to_all x1, waiting for transfers between devices, body(): arrived = lax.all_to_all(partial, ('zh', 'y', 'zl', 'x'), 0, 0, tiled=True)  27.6 us
    ppermute x1, waiting for transfers between devices, body(): lax.ppermute(picked, ('core', 'x'), [(c * 4 + i, c * 4 + (i - 1 + 2 * c)...  18.3 us
    pallas_call x1, Pallas kernels, body(): pl.pallas_call(_conv_kernel, out_shape=jax.ShapeDtypeStruct((64, ROWS, 12...  10.6 us
    all_to_all x1, starting transfers between devices, body(): raw = lax.all_to_all(messages, ('zh', 'y', 'zl', 'x'), 0, 0, tiled=True)  10.4 us
    all_to_all x1, starting transfers between devices, body(): arrived = lax.all_to_all(partial, ('zh', 'y', 'zl', 'x'), 0, 0, tiled=True)  9.67 us
    ppermute x1, starting transfers between devices, body(): lax.ppermute(picked, ('core', 'x'), [(c * 4 + i, c * 4 + (i - 1 + 2 * c)...  2.78 us
    reshape x1, local copies, waits for them, and re-layouts, body(): flat = features.transpose(1, 2, 0, 3).reshape(216, 2048)  2.4 us
  transfers between devices with their start and end apart: 9, of which 5 were waited for; matrix products, arithmetic and copies ran while one was open for 4% of the time, Pallas kernels for 4%

profile of v5, /device:TPU:0, one launch (start us, length us, event | category | flops | bytes accessed | tf_op | source)
XLA Modules:
  0.0 103.2 jit_solution(1762497337678572508)
XLA Ops:
  0.6 0.0 copy-start.2
  0.6 1.7 %weights.1 = bf16[29,32,128]{2,1,0:T(8,128)(2,1)} custom-call(bf16[27,32,128]{2,1,0:T(8,128)(2,1)} %bitcast.22, bf16[32,128]{1,0:T(8,128)(2,1)} %bitcast.23, f32[4,32]{1,0:T(4,128)} %shift_ref.1), custom_call_target="tpu_custom_call" | custom-call | tf_op jit(solution)/shard_map/weights/pallas_call | solution.py:282
  2.4 1.7 %collective-permute-start = (bf16[29,32,128]{2,1,0:T(8,128)(2,1)}, bf16[29,32,128]{2,1,0:T(8,128)(2,1)S(1)}, u32[]{:S(2)}, u32[]{:S(2)}) collective-permute-start(bf16[29,32,128]{2,1,0:T(8,128)(2,1)} %weights.1), channel_id=1, source_target_pairs={{0,16},{16,0},{32,48},{48,32},{1,17},{17,1},{33,49},{49,33},{2,18}... | collective-permute-start | bytes 712712 | tf_op jit(solution)/shard_map/ppermute | solution.py:288
  4.0 2.4 %reshape.17.f_ref = bf16[216,2048]{1,0:T(8,128)(2,1)S(1)} reshape(bf16[6,18,2,2048]{3,2,1,0:T(2,128)(2,1)} %bitcast.20) | data formatting | bytes 1769472 | tf_op jit(solution)/shard_map/reshape | solution.py:290
  6.4 0.0 copy-done.2
  6.5 1.9 %pack.1 = bf16[64,112,128]{2,1,0:T(8,128)(2,1)} custom-call(bf16[256,216]{1,0:T(8,128)(2,1)S(1)} %copy-done.2, bf16[216,2048]{1,0:T(8,128)(2,1)S(1)} %reshape.17.f_ref), custom_call_target="tpu_custom_call" | custom-call | tf_op jit(solution)/shard_map/pack/pallas_call | solution.py:291
  8.3 1.7 %collective-permute-done = bf16[29,32,128]{2,1,0:T(8,128)(2,1)S(1)} collective-permute-done((bf16[29,32,128]{2,1,0:T(8,128)(2,1)}, bf16[29,32,128]{2,1,0:T(8,128)(2,1)S(1)}, u32[]{:S(2)}, u32[]{:S(2)}) %collective-permute-start) | collective-permute-done | bytes 237600 | tf_op jit(solution)/shard_map/ppermute | solution.py:288
  10.1 1.7 %collective-permute-start.2 = (bf16[2,29,32,128]{3,2,1,0:T(8,128)(2,1)S(1)}, bf16[2,29,32,128]{3,2,1,0:T(8,128)(2,1)}, u32[]{:S(2)}, u32[]{:S(2)}) collective-permute-start(bf16[2,29,32,128]{3,2,1,0:T(8,128)(2,1)S(1)} %pad_maximum_fusion.1.refs_0_), channel_id=1, source_target_pairs={{0,1},{1,2},{2,3},{3,0},{4,5},{5,6},{6,7},{7,4},{8,9},{9,10},{10,1... | collective-permute-start | bytes 1425416 | tf_op jit(solution)/shard_map/ppermute | solution.py:305
  11.8 1.6 %collective-permute-start.1 = (bf16[2,29,32,128]{3,2,1,0:T(8,128)(2,1)S(1)}, bf16[2,29,32,128]{3,2,1,0:T(8,128)(2,1)}, u32[]{:S(2)}, u32[]{:S(2)}) collective-permute-start(bf16[2,29,32,128]{3,2,1,0:T(8,128)(2,1)S(1)} %pad_maximum_fusion.1.refs_0_), channel_id=1, source_target_pairs={{0,3},{1,0},{2,1},{3,2},{4,7},{5,4},{6,5},{7,6},{8,11},{9,8},{10,9... | collective-permute-start | bytes 1425416 | tf_op jit(solution)/shard_map/ppermute | solution.py:304
  13.4 10.4 %all-to-all-start = ((bf16[64,112,128]{2,1,0:T(8,128)(2,1)}), bf16[64,112,128]{2,1,0:T(8,128)(2,1)S(1)}, u32[]{:S(2)}, u32[]{:S(2)}) async-start(bf16[64,112,128]{2,1,0:T(8,128)(2,1)} %pack.1), calls=%async_computation | async-start | bytes 3670016 | tf_op jit(solution)/shard_map/all_to_all | solution.py:319
  23.7 0.0 collective-permute-done.2.b_ref
  23.8 0.0 collective-permute-done.1.a_ref
  23.8 2.0 %pick.1 = bf16[2,29,32,128]{3,2,1,0:T(8,128)(2,1)} custom-call(s32[1]{0:T(128)} %bitcast.1.core_ref, bf16[2,29,32,128]{3,2,1,0:T(8,128)(2,1)} %collective-permute-done.1.a_ref, bf16[2,29,32,128]{3,2,1,0:T(8,128)(2,1)} %collective-permute-done.2.b_ref), custom_call_target="tpu_custom_call" | custom-call | flops 20000000000 | bytes 1400000 | tf_op jit(solution)/shard_map/pick/pallas_call | solution.py:306
  25.8 2.8 %collective-permute-start.3 = (bf16[2,29,32,128]{3,2,1,0:T(8,128)(2,1)}, bf16[2,29,32,128]{3,2,1,0:T(8,128)(2,1)}, u32[]{:S(2)}, u32[]{:S(2)}) collective-permute-start(bf16[2,29,32,128]{3,2,1,0:T(8,128)(2,1)} %pick.1), channel_id=1, source_target_pairs={{0,3},{1,0},{2,1},{3,2},{8,9},{9,10},{10,11},{11,8},{4,7},{5,4},{6... | collective-permute-start | bytes 1425416 | tf_op jit(solution)/shard_map/ppermute | solution.py:313
  28.5 1.3 %pad_maximum_fusion.refs_1_ = bf16[2,2,29,32,128]{4,3,2,1,0:T(8,128)(2,1)S(1)} fusion(bf16[1,2,29,32,128]{4,3,2,1,0:T(8,128)(2,1)} %bitcast.11, bf16[1,2,29,32,128]{4,3,2,1,0:T(8,128)(2,1)} %bitcast.10), kind=kLoop, calls=%fused_computation | loop fusion | flops 475136 | bytes 1900544 | tf_op jit(solution)/shard_map/stack | solution.py:316
  29.8 0.1 collective-permute-start.5
  29.9 0.5 collective-permute-start.4
  30.4 18.3 %collective-permute-done.3.refs_2_ = bf16[2,29,32,128]{3,2,1,0:T(8,128)(2,1)} collective-permute-done((bf16[2,29,32,128]{3,2,1,0:T(8,128)(2,1)}, bf16[2,29,32,128]{3,2,1,0:T(8,128)(2,1)}, u32[]{:S(2)}, u32[]{:S(2)}) %collective-permute-start.3) | collective-permute-done | bytes 475168 | tf_op jit(solution)/shard_map/ppermute | solution.py:313
  48.7 1.2 %collective-permute-start.6 = (bf16[2,29,32,128]{3,2,1,0:T(8,128)(2,1)}, bf16[2,29,32,128]{3,2,1,0:T(8,128)(2,1)}, u32[]{:S(2)}, u32[]{:S(2)}) collective-permute-start(bf16[2,29,32,128]{3,2,1,0:T(8,128)(2,1)} %collective-permute-done.3.refs_2_), channel_id=1, source_target_pairs={{0,8},{8,0},{1,9},{9,1},{2,10},{10,2},{3,11},{11,3},{4,12},{12,4},... | collective-permute-start | bytes 1425416 | tf_op jit(solution)/shard_map/ppermute | solution.py:302
  49.9 0.1 pad_add_fusion.where_ref
  50.0 0.0 collective-permute-done.4.refs_3_
  50.0 0.0 collective-permute-done.5.refs_4_
  50.0 1.7 %collective-permute-done.6.refs_5_ = bf16[2,29,32,128]{3,2,1,0:T(8,128)(2,1)} collective-permute-done((bf16[2,29,32,128]{3,2,1,0:T(8,128)(2,1)}, bf16[2,29,32,128]{3,2,1,0:T(8,128)(2,1)}, u32[]{:S(2)}, u32[]{:S(2)}) %collective-permute-start.6) | collective-permute-done | bytes 475168 | tf_op jit(solution)/shard_map/ppermute | solution.py:302
  51.7 0.4 all-to-all-done.raw_ref
  52.1 10.6 %conv.1 = bf16[64,112,128]{2,1,0:T(8,128)(2,1)S(1)} custom-call(s32[4]{0:T(128)S(1)} %pad_add_fusion.where_ref, bf16[64,112,128]{2,1,0:T(8,128)(2,1)S(1)} %all-to-all-done.raw_ref, bf16[2,29,32,128]{3,2,1,0:T(8,128)(2,1)S(1)} %pad_maximum_fusion.1.refs_0_, bf16[2,2,29,32,128]{4,3,2,1,0:T(8,128)(2,1)S(1)} %pad_maximum_fusion.refs_1_, ...), custom_call_target="tpu_custom_call" | custom-call | tf_op jit(solution)/shard_map/conv/pallas_call | solution.py:320
  62.8 1.2 %copy-done = bf16[64,112,128]{2,1,0:T(8,128)(2,1)} copy-done((bf16[64,112,128]{2,1,0:T(8,128)(2,1)}, bf16[64,112,128]{2,1,0:T(8,128)(2,1)S(1)}, u32[]{:S(2)}) %copy-start) | copy-done | bytes 1835032
  64.0 0.0 copy-start.4
  64.0 9.7 %all-to-all-start.1 = ((bf16[64,112,128]{2,1,0:T(8,128)(2,1)}), bf16[64,112,128]{2,1,0:T(8,128)(2,1)S(1)}, u32[]{:S(2)}, u32[]{:S(2)}) async-start(bf16[64,112,128]{2,1,0:T(8,128)(2,1)} %copy-done), calls=%async_computation.1 | async-start | bytes 3670016 | tf_op jit(solution)/shard_map/all_to_all | solution.py:331
  73.7 0.1 reshape.19.lab_ref
  73.8 27.6 %all-to-all-done.1.in_ref = bf16[64,112,128]{2,1,0:T(8,128)(2,1)S(1)} async-done(((bf16[64,112,128]{2,1,0:T(8,128)(2,1)}), bf16[64,112,128]{2,1,0:T(8,128)(2,1)S(1)}, u32[]{:S(2)}, u32[]{:S(2)}) %all-to-all-start.1) | async-done | bytes 1835040 | tf_op jit(solution)/shard_map/all_to_all | solution.py:331
  101.5 0.0 copy-done.3
  101.5 1.7 %final.1 = (bf16[108,2,256]{2,1,0:T(2,128)(2,1)}, f32[6,2,18]{2,1,0:T(2,128)}) custom-call(bf16[64,112,128]{2,1,0:T(8,128)(2,1)S(1)} %all-to-all-done.1.in_ref, bf16[1024,256]{1,0:T(8,128)(2,1)S(1)} %copy-done.1, bf16[8,256]{1,0:T(8,128)(2,1)S(1)} %concatenate.3.cls_ref, s32[1,216]{1,0:T(1,128)S(1)} %reshape.19.lab_ref, bf16[2,108,256]{2,1,0:T(8,128)(2,1)S(1)} %copy-done.3, ...), custom_call_target="tpu_custom_call" | custom-call | tf_op jit(solution)/shard_map/final/pallas_call | solution.py:334
  (13 shorter events, 0.1 us)
Async XLA Ops:
  0.6 5.8 %copy-start.2 = (bf16[256,216]{1,0:T(8,128)(2,1)S(1)}, bf16[256,216]{1,0:T(8,128)(2,1)}, u32[]{:S(2)}) copy-start(bf16[256,216]{1,0:T(8,128)(2,1)} %constant.49.clone.p_ref) | copy-start | bytes 331780
  2.4 7.6 %collective-permute-start = (bf16[29,32,128]{2,1,0:T(8,128)(2,1)}, bf16[29,32,128]{2,1,0:T(8,128)(2,1)S(1)}, u32[]{:S(2)}, u32[]{:S(2)}) collective-permute-start(bf16[29,32,128]{2,1,0:T(8,128)(2,1)} %weights.1), channel_id=1, source_target_pairs={{0,16},{16,0},{32,48},{48,32},{1,17},{17,1},{33,49},{49,33},{2,18}... | collective-permute-start | bytes 712712 | tf_op jit(solution)/shard_map/ppermute | solution.py:288
  6.4 3.6 %copy-start.5 = (bf16[29,32,128]{2,1,0:T(8,128)(2,1)S(1)}, bf16[29,32,128]{2,1,0:T(8,128)(2,1)}, u32[]{:S(2)}) copy-start(bf16[29,32,128]{2,1,0:T(8,128)(2,1)} %weights.1) | copy-start | bytes 712708
  10.1 13.7 %collective-permute-start.2 = (bf16[2,29,32,128]{3,2,1,0:T(8,128)(2,1)S(1)}, bf16[2,29,32,128]{3,2,1,0:T(8,128)(2,1)}, u32[]{:S(2)}, u32[]{:S(2)}) collective-permute-start(bf16[2,29,32,128]{3,2,1,0:T(8,128)(2,1)S(1)} %pad_maximum_fusion.1.refs_0_), channel_id=1, source_target_pairs={{0,1},{1,2},{2,3},{3,0},{4,5},{5,6},{6,7},{7,4},{8,9},{9,10},{10,1... | collective-permute-start | bytes 1425416 | tf_op jit(solution)/shard_map/ppermute | solution.py:305
  11.8 12.0 %collective-permute-start.1 = (bf16[2,29,32,128]{3,2,1,0:T(8,128)(2,1)S(1)}, bf16[2,29,32,128]{3,2,1,0:T(8,128)(2,1)}, u32[]{:S(2)}, u32[]{:S(2)}) collective-permute-start(bf16[2,29,32,128]{3,2,1,0:T(8,128)(2,1)S(1)} %pad_maximum_fusion.1.refs_0_), channel_id=1, source_target_pairs={{0,3},{1,0},{2,1},{3,2},{4,7},{5,4},{6,5},{7,6},{8,11},{9,8},{10,9... | collective-permute-start | bytes 1425416 | tf_op jit(solution)/shard_map/ppermute | solution.py:304
  13.4 38.7 %all-to-all-start = ((bf16[64,112,128]{2,1,0:T(8,128)(2,1)}), bf16[64,112,128]{2,1,0:T(8,128)(2,1)S(1)}, u32[]{:S(2)}, u32[]{:S(2)}) async-start(bf16[64,112,128]{2,1,0:T(8,128)(2,1)} %pack.1), calls=%async_computation | async-start | bytes 3670016 | tf_op jit(solution)/shard_map/all_to_all | solution.py:319
  25.8 23.0 %collective-permute-start.3 = (bf16[2,29,32,128]{3,2,1,0:T(8,128)(2,1)}, bf16[2,29,32,128]{3,2,1,0:T(8,128)(2,1)}, u32[]{:S(2)}, u32[]{:S(2)}) collective-permute-start(bf16[2,29,32,128]{3,2,1,0:T(8,128)(2,1)} %pick.1), channel_id=1, source_target_pairs={{0,3},{1,0},{2,1},{3,2},{8,9},{9,10},{10,11},{11,8},{4,7},{5,4},{6... | collective-permute-start | bytes 1425416 | tf_op jit(solution)/shard_map/ppermute | solution.py:313
  29.8 20.2 %collective-permute-start.5 = (bf16[2,2,29,32,128]{4,3,2,1,0:T(8,128)(2,1)S(1)}, bf16[2,2,29,32,128]{4,3,2,1,0:T(8,128)(2,1)}, u32[]{:S(2)}, u32[]{:S(2)}) collective-permute-start(bf16[2,2,29,32,128]{4,3,2,1,0:T(8,128)(2,1)S(1)} %pad_maximum_fusion.refs_1_), channel_id=1, source_target_pairs={{0,8},{8,0},{1,9},{9,1},{2,10},{10,2},{3,11},{11,3},{4,12},{12,4},... | collective-permute-start | bytes 2850824 | tf_op jit(solution)/shard_map/ppermute | solution.py:302
  29.9 20.1 %collective-permute-start.4 = (bf16[2,29,32,128]{3,2,1,0:T(8,128)(2,1)S(1)}, bf16[2,29,32,128]{3,2,1,0:T(8,128)(2,1)}, u32[]{:S(2)}, u32[]{:S(2)}) collective-permute-start(bf16[2,29,32,128]{3,2,1,0:T(8,128)(2,1)S(1)} %pad_maximum_fusion.1.refs_0_), channel_id=1, source_target_pairs={{0,8},{8,0},{1,9},{9,1},{2,10},{10,2},{3,11},{11,3},{4,12},{12,4},... | collective-permute-start | bytes 1425416 | tf_op jit(solution)/shard_map/ppermute | solution.py:302
  48.7 3.0 %collective-permute-start.6 = (bf16[2,29,32,128]{3,2,1,0:T(8,128)(2,1)}, bf16[2,29,32,128]{3,2,1,0:T(8,128)(2,1)}, u32[]{:S(2)}, u32[]{:S(2)}) collective-permute-start(bf16[2,29,32,128]{3,2,1,0:T(8,128)(2,1)} %collective-permute-done.3.refs_2_), channel_id=1, source_target_pairs={{0,8},{8,0},{1,9},{9,1},{2,10},{10,2},{3,11},{11,3},{4,12},{12,4},... | collective-permute-start | bytes 1425416 | tf_op jit(solution)/shard_map/ppermute | solution.py:302
  62.8 1.3 %copy-start = (bf16[64,112,128]{2,1,0:T(8,128)(2,1)}, bf16[64,112,128]{2,1,0:T(8,128)(2,1)S(1)}, u32[]{:S(2)}) copy-start(bf16[64,112,128]{2,1,0:T(8,128)(2,1)S(1)} %conv.1) | copy-start | bytes 5505028
  64.0 9.7 %copy-start.6 = (s32[2,6,18]{2,0,1:T(2,128)S(1)}, s32[2,6,18]{2,0,1:T(2,128)}, u32[]{:S(2)}) copy-start(s32[2,6,18]{2,0,1:T(2,128)} %param.16) | copy-start | bytes 2596
  64.0 9.8 %copy-start.7 = (bf16[256,3]{0,1:T(4,128)(2,1)S(1)}, bf16[256,3]{0,1:T(4,128)(2,1)}, u32[]{:S(2)}) copy-start(bf16[256,3]{0,1:T(4,128)(2,1)} %param.15) | copy-start | bytes 4612
  64.0 37.5 %copy-start.1 = (bf16[1024,256]{1,0:T(8,128)(2,1)S(1)}, bf16[1024,256]{1,0:T(8,128)(2,1)}, u32[]{:S(2)}) copy-start(bf16[1024,256]{1,0:T(8,128)(2,1)} %proj_ref.1) | copy-start | bytes 1572868
  64.0 37.5 %copy-start.3 = (bf16[2,108,256]{2,1,0:T(8,128)(2,1)S(1)}, bf16[2,108,256]{2,1,0:T(8,128)(2,1)}, u32[]{:S(2)}) copy-start(bf16[2,108,256]{2,1,0:T(8,128)(2,1)} %constant.50.clone.u_ref) | copy-start | bytes 331780
  64.0 37.5 %copy-start.4 = (bf16[216,256]{1,0:T(8,128)(2,1)S(1)}, bf16[216,256]{1,0:T(8,128)(2,1)}, u32[]{:S(2)}) copy-start(bf16[216,256]{1,0:T(8,128)(2,1)} %constant.51.clone.v_ref) | copy-start | bytes 331780
  64.0 37.4 %all-to-all-start.1 = ((bf16[64,112,128]{2,1,0:T(8,128)(2,1)}), bf16[64,112,128]{2,1,0:T(8,128)(2,1)S(1)}, u32[]{:S(2)}, u32[]{:S(2)}) async-start(bf16[64,112,128]{2,1,0:T(8,128)(2,1)} %copy-done), calls=%async_computation.1 | async-start | bytes 3670016 | tf_op jit(solution)/shard_map/all_to_all | solution.py:331

commit v6 on v5

--- a/solution.py
+++ b/solution.py
@@ -59,17 +59,9 @@
 TAPS = [tap for group in GROUPS for tap in group]
 
 
-def _weights_kernel(wide_ref, point_ref, shift_ref, out_ref, terms):
+def _weights_kernel(wide_ref, point_ref, out_ref):
     for n, (d, a, c) in enumerate(TAPS):
         out_ref[n] = point_ref[...] if d == 0 else wide_ref[(d - 1) * 9 + (a + 1) * 3 + c + 1]
-    whole = shift_ref[...]
-    high = whole.astype(BF).astype(F32)
-    middle = (whole - high).astype(BF).astype(F32)
-    terms[...] = jnp.zeros_like(terms)
-    terms[0:4, 0:32] = high
-    terms[8:12, 0:32] = middle
-    terms[16:20, 0:32] = whole - high - middle
-    out_ref[28] = terms[...].astype(BF)
 
 
 def _pick_kernel(core_ref, a_ref, b_ref, out_ref):
@@ -95,10 +87,10 @@
                 out_ref[((q * 2 + n % 2) * 2 + zl) * 4 + n // 2] = message
 
 
-def _conv_kernel(where_ref, raw_ref, *refs):
+def _conv_kernel(where_ref, raw_ref, shift_ref, *refs):
     own_refs, other_refs, out_ref = refs[:3], refs[3:6], refs[6]
-    lines, grid, xs, wt, sh, acc, outs, sems = refs[7:]
-    x, core, half, first = where_ref[0], where_ref[1], where_ref[2], where_ref[3]
+    lines, grid, xs, wt, acc, outs, sems = refs[7:]
+    x, core, half = where_ref[0], where_ref[1], where_ref[2]
     own_refs, other_refs = (
         (near, sides.at[0], far, sides.at[1]) for near, sides, far in (own_refs, other_refs)
     )
@@ -110,17 +102,22 @@
                 slab = lax.rem(half + z, 2) * 2 + lax.rem(core + o, 2)
                 copies.append(
                     pltpu.make_async_copy(
-                        ref.at[z, pl.ds(0, 28)],
+                        ref.at[z],
                         wt.at[:, xo, :, pl.ds(pl.multiple_of(slab * 128, 128), 128)],
                         sems.at[len(copies)],
                     )
                 )
-        copies.append(pltpu.make_async_copy(own_refs[k].at[0, 28], sh.at[xo], sems.at[len(copies)]))
     for copy in copies:
         copy.start()
 
     grid[...] = jnp.zeros_like(grid)
     outs[...] = jnp.zeros_like(outs)
+    whole = shift_ref[...]
+    high = whole.astype(BF).astype(F32)
+    middle = (whole - high).astype(BF).astype(F32)
+    for j in range(8):
+        for n, term in enumerate((high, middle, whole - high - middle)):
+            outs[j, 4 * SPOTS + n : 4 * SPOTS + n + 1] = term
 
     def window(dc):
         low = max(0, -dc * 6) // 8 * 8
@@ -180,7 +177,7 @@
             for b in range(4):
                 for i in range(3):
                     start = b * SPOTS + i * 9
-                    outs[j, start : start + 9] = acc[b, g, i * 72 + j * 9 : i * 72 + j * 9 + 9] + shifts[b]
+                    outs[j, start : start + 9] = acc[b, g, i * 72 + j * 9 : i * 72 + j * 9 + 9]
             out_ref[g * 8 + j] = outs[j].astype(BF)
             yield
 
@@ -189,18 +186,6 @@
         pass
     for copy in copies:
         copy.wait()
-
-    lane = lax.broadcasted_iota(jnp.int32, (1, 128), 1)
-    shifts = []
-    for b in range(4):
-        line = jnp.zeros((1, 128), F32)
-        for xo in range(4):
-            terms = sh[xo].astype(F32)
-            whole = (terms[0:8] + terms[8:16] + terms[16:24])[b : b + 1]
-            if xo > 0:
-                whole = pltpu.roll(whole, xo * 32, 1)
-            line = jnp.where((lane >= xo * 32) & (lane < xo * 32 + 32), whole, line)
-        shifts.append(jnp.where(first == 0, line, 0.0))
 
     for m in range(4):
         beside = []
@@ -236,15 +221,27 @@
     pltpu.VMEM((2, 4, 3, HALO + 72 + HALO + 4, 128), F32),
     pltpu.VMEM((2, 7, 2 * GRID, 512), BF),
     pltpu.VMEM((28, 4, 32, 512), BF),
-    pltpu.VMEM((4, 32, 128), BF),
     pltpu.VMEM((4, 8, GRID, 128), F32),
     pltpu.VMEM((8, ROWS, 128), F32),
-    pltpu.SemaphoreType.DMA((20,)),
+    pltpu.SemaphoreType.DMA((16,)),
 ]
 
 
 def _final_kernel(in_ref, proj_ref, cls_ref, lab_ref, u_ref, v_ref, out_ref, loss_ref, lines, pyr):
     lines[...] = jnp.zeros_like(lines)
+    lane = lax.broadcasted_iota(jnp.int32, (1, 128), 1)
+    shifts = {}
+    for zl in range(2):
+        wholes = []
+        for xq in range(4):
+            terms = in_ref[zl * 4 + xq, 96:112].astype(F32)
+            wholes.append(terms[12:13] + terms[13:14] + terms[14:15])
+        for b in range(4):
+            line = jnp.zeros((1, 128), F32)
+            for xq in range(4):
+                whole = wholes[xq] if xq == b else pltpu.roll(wholes[xq], (xq - b) % 4 * 32, 1)
+                line = jnp.where((lane >= xq * 32) & (lane < xq * 32 + 32), whole, line)
+            shifts[zl, b] = line
     for h in range(2):
         for xq in range(4):
             r = h * 4 + xq
@@ -252,11 +249,11 @@
                 total = in_ref[(h * 2 + zl) * 4 + xq].astype(F32)
                 for q in range(1, 4):
                     total = total + in_ref[((q * 2 + h) * 2 + zl) * 4 + xq].astype(F32)
-                lines[r * 2 + zl, 0:ROWS] = jnp.maximum(total, 0.0)
+                lines[r * 2 + zl, 0:ROWS] = total
                 for b in range(4):
-                    pyr[r * 32 : (r + 1) * 32, b * 256 + zl * 128 : b * 256 + (zl + 1) * 128] = lines[
-                        r * 2 + zl, b * SPOTS : b * SPOTS + 32
-                    ].astype(BF)
+                    branch = lines[r * 2 + zl, b * SPOTS : b * SPOTS + 32] + shifts[zl, b]
+                    start = b * 256 + zl * 128
+                    pyr[r * 32 : (r + 1) * 32, start : start + 128] = jnp.maximum(branch, 0.0).astype(BF)
     mixed = jnp.dot(pyr[...], proj_ref[...], preferred_element_type=F32)
     projected = jnp.maximum(mixed, 0.0).astype(BF)
     for b in range(2):
@@ -275,16 +272,14 @@
 
 
 def body(features, atrous_weight, point_weight, branch_shift, proj_weight, class_weight, labels):
-    x, zh = lax.axis_index("x"), lax.axis_index("zh")
-    core, y = lax.axis_index("core"), lax.axis_index("y")
-    where = jnp.stack([x, core, y % 2, zh * 2 + y // 2]).astype(jnp.int32)
+    x, core, y = lax.axis_index("x"), lax.axis_index("core"), lax.axis_index("y")
+    where = jnp.stack([x, core, y % 2]).astype(jnp.int32)
 
     weights = pl.pallas_call(
         _weights_kernel,
-        out_shape=jax.ShapeDtypeStruct((29, 32, 128), BF),
-        scratch_shapes=[pltpu.VMEM((32, 128), F32)],
+        out_shape=jax.ShapeDtypeStruct((28, 32, 128), BF),
         name="weights",
-    )(atrous_weight.transpose(0, 1, 2, 4, 3).reshape(27, 32, 128), point_weight.T, branch_shift)
+    )(atrous_weight.transpose(0, 1, 2, 4, 3).reshape(27, 32, 128), point_weight.T)
     swapped = lax.ppermute(weights, "y", [(0, 1), (1, 0), (2, 3), (3, 2)])
 
     flat = features.transpose(1, 2, 0, 3).reshape(216, 2048)
@@ -320,13 +315,14 @@
     partial = pl.pallas_call(
         _conv_kernel,
         out_shape=jax.ShapeDtypeStruct((64, ROWS, 128), BF),
-        in_specs=[pl.BlockSpec(memory_space=pltpu.SMEM), pl.BlockSpec(memory_space=pltpu.VMEM)]
+        in_specs=[pl.BlockSpec(memory_space=pltpu.SMEM)]
+        + [pl.BlockSpec(memory_space=pltpu.VMEM)] * 2
         + [pl.BlockSpec(memory_space=pl.ANY)] * 6,
         out_specs=pl.BlockSpec(memory_space=pltpu.VMEM),
         scratch_shapes=CONV_SCRATCH,
         compiler_params=pltpu.CompilerParams(vmem_limit_bytes=24 * MIB),
         name="conv",
-    )(where, raw, *own, *other)
+    )(where, raw, branch_shift.reshape(1, 128), *own, *other)
 
     arrived = lax.all_to_all(partial, ("zh", "y", "zl", "x"), 0, 0, tiled=True)
     by_cols, by_samples = _unpack_matrices()

time: 104 us -> 103 us (level)
  waiting for transfers between devices: 49.8 us -> 48.6 us
    ppermute x1, waiting for transfers between devices: 18.3 us -> 17.3 us  [body(): lax.ppermute(picked, ('core', 'x'), [(c * 4 + i, c * 4 + (i - 1 + 2 * c)...]
    unnamed x16 -> x22, local copies, waits for them, and re-layouts: 1.28 us -> 2.22 us
where the time goes in v6:
time: 103 us; the launch traced here: 102 us
  waiting for transfers between devices  48.6 us (47%)
  starting transfers between devices  29.1 us (28%)
  Pallas kernels  17.8 us (17%)
  local copies, waits for them, and re-layouts  4.79 us (5%)
  other arithmetic  1.36 us (1%)
    all_to_all x1, waiting for transfers between devices, body(): arrived = lax.all_to_all(partial, ('zh', 'y', 'zl', 'x'), 0, 0, tiled=True)  27.6 us
    ppermute x1, waiting for transfers between devices, body(): lax.ppermute(picked, ('core', 'x'), [(c * 4 + i, c * 4 + (i - 1 + 2 * c)...  17.3 us
    pallas_call x1, Pallas kernels, body(): pl.pallas_call(_conv_kernel, out_shape=jax.ShapeDtypeStruct((64, ROWS, 12...  10.6 us
    all_to_all x1, starting transfers between devices, body(): raw = lax.all_to_all(messages, ('zh', 'y', 'zl', 'x'), 0, 0, tiled=True)  10.4 us
    all_to_all x1, starting transfers between devices, body(): arrived = lax.all_to_all(partial, ('zh', 'y', 'zl', 'x'), 0, 0, tiled=True)  9.13 us
    ppermute x1, starting transfers between devices, body(): lax.ppermute(picked, ('core', 'x'), [(c * 4 + i, c * 4 + (i - 1 + 2 * c)...  2.78 us
    reshape x1, local copies, waits for them, and re-layouts, body(): flat = features.transpose(1, 2, 0, 3).reshape(216, 2048)  2.4 us
    unnamed x22, local copies, waits for them, and re-layouts  2.22 us
  transfers between devices with their start and end apart: 9, of which 5 were waited for; matrix products, arithmetic and copies ran while one was open for 4% of the time, Pallas kernels for 4%

profile of v6, /device:TPU:0, one launch (start us, length us, event | category | flops | bytes accessed | tf_op | source)
XLA Modules:
  0.0 102.4 jit_solution(395654463913441988)
XLA Ops:
  0.6 0.0 copy-start.2
  0.6 1.7 %weights.1 = bf16[28,32,128]{2,1,0:T(8,128)(2,1)} custom-call(bf16[27,32,128]{2,1,0:T(8,128)(2,1)} %bitcast.23, bf16[32,128]{1,0:T(8,128)(2,1)} %bitcast.24), custom_call_target="tpu_custom_call" | custom-call | tf_op jit(solution)/shard_map/weights/pallas_call | solution.py:278
  2.3 1.7 %collective-permute-start = (bf16[28,32,128]{2,1,0:T(8,128)(2,1)}, bf16[28,32,128]{2,1,0:T(8,128)(2,1)S(1)}, u32[]{:S(2)}, u32[]{:S(2)}) collective-permute-start(bf16[28,32,128]{2,1,0:T(8,128)(2,1)} %weights.1), channel_id=1, source_target_pairs={{0,16},{16,0},{32,48},{48,32},{1,17},{17,1},{33,49},{49,33},{2,18}... | collective-permute-start | bytes 688136 | tf_op jit(solution)/shard_map/ppermute | solution.py:283
  4.0 2.4 %reshape.20.f_ref = bf16[216,2048]{1,0:T(8,128)(2,1)S(1)} reshape(bf16[6,18,2,2048]{3,2,1,0:T(2,128)(2,1)} %bitcast.19) | data formatting | bytes 1769472 | tf_op jit(solution)/shard_map/reshape | solution.py:285
  6.4 1.9 %pack.1 = bf16[64,112,128]{2,1,0:T(8,128)(2,1)} custom-call(bf16[256,216]{1,0:T(8,128)(2,1)S(1)} %copy-done.2, bf16[216,2048]{1,0:T(8,128)(2,1)S(1)} %reshape.20.f_ref), custom_call_target="tpu_custom_call" | custom-call | tf_op jit(solution)/shard_map/pack/pallas_call | solution.py:286
  8.3 1.5 %collective-permute-done = bf16[28,32,128]{2,1,0:T(8,128)(2,1)S(1)} collective-permute-done((bf16[28,32,128]{2,1,0:T(8,128)(2,1)}, bf16[28,32,128]{2,1,0:T(8,128)(2,1)S(1)}, u32[]{:S(2)}, u32[]{:S(2)}) %collective-permute-start) | collective-permute-done | bytes 229408 | tf_op jit(solution)/shard_map/ppermute | solution.py:283
  9.8 1.7 %collective-permute-start.2 = (bf16[2,28,32,128]{3,2,1,0:T(8,128)(2,1)S(1)}, bf16[2,28,32,128]{3,2,1,0:T(8,128)(2,1)S(1)}, u32[]{:S(2)}, u32[]{:S(2)}) collective-permute-start(bf16[2,28,32,128]{3,2,1,0:T(8,128)(2,1)S(1)} %pad_maximum_fusion.1.refs_0_), channel_id=1, source_target_pairs={{0,1},{1,2},{2,3},{3,0},{4,5},{5,6},{6,7},{7,4},{8,9},{9,10},{10,1... | collective-permute-start | bytes 1376264 | tf_op jit(solution)/shard_map/ppermute | solution.py:300
  11.6 1.6 %collective-permute-start.1 = (bf16[2,28,32,128]{3,2,1,0:T(8,128)(2,1)S(1)}, bf16[2,28,32,128]{3,2,1,0:T(8,128)(2,1)S(1)}, u32[]{:S(2)}, u32[]{:S(2)}) collective-permute-start(bf16[2,28,32,128]{3,2,1,0:T(8,128)(2,1)S(1)} %pad_maximum_fusion.1.refs_0_), channel_id=1, source_target_pairs={{0,3},{1,0},{2,1},{3,2},{4,7},{5,4},{6,5},{7,6},{8,11},{9,8},{10,9... | collective-permute-start | bytes 1376264 | tf_op jit(solution)/shard_map/ppermute | solution.py:299
  13.1 10.4 %all-to-all-start = ((bf16[64,112,128]{2,1,0:T(8,128)(2,1)}), bf16[64,112,128]{2,1,0:T(8,128)(2,1)S(1)}, u32[]{:S(2)}, u32[]{:S(2)}) async-start(bf16[64,112,128]{2,1,0:T(8,128)(2,1)} %pack.1), calls=%async_computation | async-start | bytes 3670016 | tf_op jit(solution)/shard_map/all_to_all | solution.py:314
  23.5 0.0 collective-permute-done.2.b_ref
  23.5 0.0 collective-permute-done.1.a_ref
  23.6 0.7 copy-done.6
  24.3 0.2 copy-done.7
  24.5 2.0 %pick.1 = bf16[2,28,32,128]{3,2,1,0:T(8,128)(2,1)} custom-call(s32[1]{0:T(128)} %bitcast.1.core_ref, bf16[2,28,32,128]{3,2,1,0:T(8,128)(2,1)} %copy-done.7, bf16[2,28,32,128]{3,2,1,0:T(8,128)(2,1)} %copy-done.6), custom_call_target="tpu_custom_call" | custom-call | flops 20000000000 | bytes 1400000 | tf_op jit(solution)/shard_map/pick/pallas_call | solution.py:301
  26.4 2.8 %collective-permute-start.3 = (bf16[2,28,32,128]{3,2,1,0:T(8,128)(2,1)}, bf16[2,28,32,128]{3,2,1,0:T(8,128)(2,1)}, u32[]{:S(2)}, u32[]{:S(2)}) collective-permute-start(bf16[2,28,32,128]{3,2,1,0:T(8,128)(2,1)} %pick.1), channel_id=1, source_target_pairs={{0,3},{1,0},{2,1},{3,2},{8,9},{9,10},{10,11},{11,8},{4,7},{5,4},{6... | collective-permute-start | bytes 1376264 | tf_op jit(solution)/shard_map/ppermute | solution.py:308
  29.2 1.2 %pad_maximum_fusion.refs_1_ = bf16[2,2,28,32,128]{4,3,2,1,0:T(8,128)(2,1)S(1)} fusion(bf16[1,2,28,32,128]{4,3,2,1,0:T(8,128)(2,1)} %bitcast.20, bf16[1,2,28,32,128]{4,3,2,1,0:T(8,128)(2,1)} %bitcast.21), kind=kLoop, calls=%fused_computation | loop fusion | flops 458752 | bytes 1835008 | tf_op jit(solution)/shard_map/stack | solution.py:311
  30.5 0.1 collective-permute-start.5
  30.6 0.5 collective-permute-start.4
  31.0 17.3 %collective-permute-done.3.refs_2_ = bf16[2,28,32,128]{3,2,1,0:T(8,128)(2,1)} collective-permute-done((bf16[2,28,32,128]{3,2,1,0:T(8,128)(2,1)}, bf16[2,28,32,128]{3,2,1,0:T(8,128)(2,1)}, u32[]{:S(2)}, u32[]{:S(2)}) %collective-permute-start.3) | collective-permute-done | bytes 458784 | tf_op jit(solution)/shard_map/ppermute | solution.py:308
  48.3 1.2 %collective-permute-start.6 = (bf16[2,28,32,128]{3,2,1,0:T(8,128)(2,1)}, bf16[2,28,32,128]{3,2,1,0:T(8,128)(2,1)}, u32[]{:S(2)}, u32[]{:S(2)}) collective-permute-start(bf16[2,28,32,128]{3,2,1,0:T(8,128)(2,1)} %collective-permute-done.3.refs_2_), channel_id=1, source_target_pairs={{0,8},{8,0},{1,9},{9,1},{2,10},{10,2},{3,11},{11,3},{4,12},{12,4},... | collective-permute-start | bytes 1376264 | tf_op jit(solution)/shard_map/ppermute | solution.py:297
  49.5 0.1 reshape.22.shift_ref
  49.6 0.1 pad_add_fusion.where_ref
  49.7 0.0 collective-permute-done.4.refs_3_
  49.7 1.6 %collective-permute-done.6.refs_5_ = bf16[2,28,32,128]{3,2,1,0:T(8,128)(2,1)} collective-permute-done((bf16[2,28,32,128]{3,2,1,0:T(8,128)(2,1)}, bf16[2,28,32,128]{3,2,1,0:T(8,128)(2,1)}, u32[]{:S(2)}, u32[]{:S(2)}) %collective-permute-start.6) | collective-permute-done | bytes 458784 | tf_op jit(solution)/shard_map/ppermute | solution.py:297
  51.3 0.6 all-to-all-done.raw_ref
  51.9 10.6 %conv.1 = bf16[64,112,128]{2,1,0:T(8,128)(2,1)S(1)} custom-call(s32[3]{0:T(128)S(1)} %pad_add_fusion.where_ref, bf16[64,112,128]{2,1,0:T(8,128)(2,1)S(1)} %all-to-all-done.raw_ref, f32[1,128]{1,0:T(1,128)S(1)} %reshape.22.shift_ref, bf16[2,28,32,128]{3,2,1,0:T(8,128)(2,1)S(1)} %pad_maximum_fusion.1.refs_0_, ...), custom_call_target="tpu_custom_call" | custom-call | tf_op jit(solution)/shard_map/conv/pallas_call | solution.py:315
  62.5 1.3 %copy-done = bf16[64,112,128]{2,1,0:T(8,128)(2,1)} copy-done((bf16[64,112,128]{2,1,0:T(8,128)(2,1)}, bf16[64,112,128]{2,1,0:T(8,128)(2,1)S(1)}, u32[]{:S(2)}) %copy-start) | copy-done | bytes 1835032
  63.8 0.0 copy-start.4
  63.8 9.1 %all-to-all-start.1 = ((bf16[64,112,128]{2,1,0:T(8,128)(2,1)}), bf16[64,112,128]{2,1,0:T(8,128)(2,1)S(1)}, u32[]{:S(2)}, u32[]{:S(2)}) async-start(bf16[64,112,128]{2,1,0:T(8,128)(2,1)} %copy-done), calls=%async_computation.1 | async-start | bytes 3670016 | tf_op jit(solution)/shard_map/all_to_all | solution.py:327
  72.9 0.1 reshape.23.lab_ref
  73.0 27.6 %all-to-all-done.1.in_ref = bf16[64,112,128]{2,1,0:T(8,128)(2,1)S(1)} async-done(((bf16[64,112,128]{2,1,0:T(8,128)(2,1)}), bf16[64,112,128]{2,1,0:T(8,128)(2,1)S(1)}, u32[]{:S(2)}, u32[]{:S(2)}) %all-to-all-start.1) | async-done | bytes 1835040 | tf_op jit(solution)/shard_map/all_to_all | solution.py:327
  100.7 1.7 %final.1 = (bf16[108,2,256]{2,1,0:T(2,128)(2,1)}, f32[6,2,18]{2,1,0:T(2,128)}) custom-call(bf16[64,112,128]{2,1,0:T(8,128)(2,1)S(1)} %all-to-all-done.1.in_ref, bf16[1024,256]{1,0:T(8,128)(2,1)S(1)} %copy-done.1, bf16[8,256]{1,0:T(8,128)(2,1)S(1)} %concatenate.3.cls_ref, s32[1,216]{1,0:T(1,128)S(1)} %reshape.23.lab_ref, bf16[2,108,256]{2,1,0:T(8,128)(2,1)S(1)} %copy-done.3, ...), custom_call_target="tpu_custom_call" | custom-call | tf_op jit(solution)/shard_map/final/pallas_call | solution.py:330
  (20 shorter events, 0.1 us)
Async XLA Ops:
  0.6 5.8 %copy-start.2 = (bf16[256,216]{1,0:T(8,128)(2,1)S(1)}, bf16[256,216]{1,0:T(8,128)(2,1)}, u32[]{:S(2)}) copy-start(bf16[256,216]{1,0:T(8,128)(2,1)} %constant.34.clone.p_ref) | copy-start | bytes 331780
  2.3 7.5 %collective-permute-start = (bf16[28,32,128]{2,1,0:T(8,128)(2,1)}, bf16[28,32,128]{2,1,0:T(8,128)(2,1)S(1)}, u32[]{:S(2)}, u32[]{:S(2)}) collective-permute-start(bf16[28,32,128]{2,1,0:T(8,128)(2,1)} %weights.1), channel_id=1, source_target_pairs={{0,16},{16,0},{32,48},{48,32},{1,17},{17,1},{33,49},{49,33},{2,18}... | collective-permute-start | bytes 688136 | tf_op jit(solution)/shard_map/ppermute | solution.py:283
  6.4 3.4 %copy-start.5 = (bf16[28,32,128]{2,1,0:T(8,128)(2,1)S(1)}, bf16[28,32,128]{2,1,0:T(8,128)(2,1)}, u32[]{:S(2)}) copy-start(bf16[28,32,128]{2,1,0:T(8,128)(2,1)} %weights.1) | copy-start | bytes 688132
  9.8 13.7 %collective-permute-start.2 = (bf16[2,28,32,128]{3,2,1,0:T(8,128)(2,1)S(1)}, bf16[2,28,32,128]{3,2,1,0:T(8,128)(2,1)S(1)}, u32[]{:S(2)}, u32[]{:S(2)}) collective-permute-start(bf16[2,28,32,128]{3,2,1,0:T(8,128)(2,1)S(1)} %pad_maximum_fusion.1.refs_0_), channel_id=1, source_target_pairs={{0,1},{1,2},{2,3},{3,0},{4,5},{5,6},{6,7},{7,4},{8,9},{9,10},{10,1... | collective-permute-start | bytes 1376264 | tf_op jit(solution)/shard_map/ppermute | solution.py:300
  11.6 12.0 %collective-permute-start.1 = (bf16[2,28,32,128]{3,2,1,0:T(8,128)(2,1)S(1)}, bf16[2,28,32,128]{3,2,1,0:T(8,128)(2,1)S(1)}, u32[]{:S(2)}, u32[]{:S(2)}) collective-permute-start(bf16[2,28,32,128]{3,2,1,0:T(8,128)(2,1)S(1)} %pad_maximum_fusion.1.refs_0_), channel_id=1, source_target_pairs={{0,3},{1,0},{2,1},{3,2},{4,7},{5,4},{6,5},{7,6},{8,11},{9,8},{10,9... | collective-permute-start | bytes 1376264 | tf_op jit(solution)/shard_map/ppermute | solution.py:299
  13.1 38.7 %all-to-all-start = ((bf16[64,112,128]{2,1,0:T(8,128)(2,1)}), bf16[64,112,128]{2,1,0:T(8,128)(2,1)S(1)}, u32[]{:S(2)}, u32[]{:S(2)}) async-start(bf16[64,112,128]{2,1,0:T(8,128)(2,1)} %pack.1), calls=%async_computation | async-start | bytes 3670016 | tf_op jit(solution)/shard_map/all_to_all | solution.py:314
  23.5 0.8 copy-start.6
  23.6 0.9 copy-start.7
  26.4 23.1 %copy-start.9 = (f32[4,32]{1,0:T(4,128)S(1)}, f32[4,32]{1,0:T(4,128)}, u32[]{:S(2)}) copy-start(f32[4,32]{1,0:T(4,128)} %param.13) | copy-start | bytes 1540
  26.4 21.9 %collective-permute-start.3 = (bf16[2,28,32,128]{3,2,1,0:T(8,128)(2,1)}, bf16[2,28,32,128]{3,2,1,0:T(8,128)(2,1)}, u32[]{:S(2)}, u32[]{:S(2)}) collective-permute-start(bf16[2,28,32,128]{3,2,1,0:T(8,128)(2,1)} %pick.1), channel_id=1, source_target_pairs={{0,3},{1,0},{2,1},{3,2},{8,9},{9,10},{10,11},{11,8},{4,7},{5,4},{6... | collective-permute-start | bytes 1376264 | tf_op jit(solution)/shard_map/ppermute | solution.py:308
  30.5 19.2 %collective-permute-start.5 = (bf16[2,2,28,32,128]{4,3,2,1,0:T(8,128)(2,1)S(1)}, bf16[2,2,28,32,128]{4,3,2,1,0:T(8,128)(2,1)}, u32[]{:S(2)}, u32[]{:S(2)}) collective-permute-start(bf16[2,2,28,32,128]{4,3,2,1,0:T(8,128)(2,1)S(1)} %pad_maximum_fusion.refs_1_), channel_id=1, source_target_pairs={{0,8},{8,0},{1,9},{9,1},{2,10},{10,2},{3,11},{11,3},{4,12},{12,4},... | collective-permute-start | bytes 2752520 | tf_op jit(solution)/shard_map/ppermute | solution.py:297
  30.6 19.1 %collective-permute-start.4 = (bf16[2,28,32,128]{3,2,1,0:T(8,128)(2,1)S(1)}, bf16[2,28,32,128]{3,2,1,0:T(8,128)(2,1)}, u32[]{:S(2)}, u32[]{:S(2)}) collective-permute-start(bf16[2,28,32,128]{3,2,1,0:T(8,128)(2,1)S(1)} %pad_maximum_fusion.1.refs_0_), channel_id=1, source_target_pairs={{0,8},{8,0},{1,9},{9,1},{2,10},{10,2},{3,11},{11,3},{4,12},{12,4},... | collective-permute-start | bytes 1376264 | tf_op jit(solution)/shard_map/ppermute | solution.py:297
  48.3 3.0 %collective-permute-start.6 = (bf16[2,28,32,128]{3,2,1,0:T(8,128)(2,1)}, bf16[2,28,32,128]{3,2,1,0:T(8,128)(2,1)}, u32[]{:S(2)}, u32[]{:S(2)}) collective-permute-start(bf16[2,28,32,128]{3,2,1,0:T(8,128)(2,1)} %collective-permute-done.3.refs_2_), channel_id=1, source_target_pairs={{0,8},{8,0},{1,9},{9,1},{2,10},{10,2},{3,11},{11,3},{4,12},{12,4},... | collective-permute-start | bytes 1376264 | tf_op jit(solution)/shard_map/ppermute | solution.py:297
  62.5 1.3 %copy-start = (bf16[64,112,128]{2,1,0:T(8,128)(2,1)}, bf16[64,112,128]{2,1,0:T(8,128)(2,1)S(1)}, u32[]{:S(2)}) copy-start(bf16[64,112,128]{2,1,0:T(8,128)(2,1)S(1)} %conv.1) | copy-start | bytes 5505028
  63.7 9.2 %copy-start.8 = (s32[2,6,18]{2,0,1:T(2,128)S(1)}, s32[2,6,18]{2,0,1:T(2,128)}, u32[]{:S(2)}) copy-start(s32[2,6,18]{2,0,1:T(2,128)} %param.16) | copy-start | bytes 2596
  63.7 9.3 %copy-start.10 = (bf16[256,3]{0,1:T(4,128)(2,1)S(1)}, bf16[256,3]{0,1:T(4,128)(2,1)}, u32[]{:S(2)}) copy-start(bf16[256,3]{0,1:T(4,128)(2,1)} %param.15) | copy-start | bytes 4612
  63.8 36.9 %copy-start.1 = (bf16[1024,256]{1,0:T(8,128)(2,1)S(1)}, bf16[1024,256]{1,0:T(8,128)(2,1)}, u32[]{:S(2)}) copy-start(bf16[1024,256]{1,0:T(8,128)(2,1)} %proj_ref.1) | copy-start | bytes 1572868
  63.8 36.9 %copy-start.3 = (bf16[2,108,256]{2,1,0:T(8,128)(2,1)S(1)}, bf16[2,108,256]{2,1,0:T(8,128)(2,1)}, u32[]{:S(2)}) copy-start(bf16[2,108,256]{2,1,0:T(8,128)(2,1)} %constant.35.clone.u_ref) | copy-start | bytes 331780
  63.8 36.9 %copy-start.4 = (bf16[216,256]{1,0:T(8,128)(2,1)S(1)}, bf16[216,256]{1,0:T(8,128)(2,1)}, u32[]{:S(2)}) copy-start(bf16[216,256]{1,0:T(8,128)(2,1)} %constant.36.clone.v_ref) | copy-start | bytes 331780
  63.8 36.9 %all-to-all-start.1 = ((bf16[64,112,128]{2,1,0:T(8,128)(2,1)}), bf16[64,112,128]{2,1,0:T(8,128)(2,1)S(1)}, u32[]{:S(2)}, u32[]{:S(2)}) async-start(bf16[64,112,128]{2,1,0:T(8,128)(2,1)} %copy-done), calls=%async_computation.1 | async-start | bytes 3670016 | tf_op jit(solution)/shard_map/all_to_all | solution.py:327

commit v7 on v6

--- a/solution.py
+++ b/solution.py
@@ -228,7 +228,7 @@
 
 
 def _final_kernel(in_ref, proj_ref, cls_ref, lab_ref, u_ref, v_ref, out_ref, loss_ref, lines, pyr):
-    lines[...] = jnp.zeros_like(lines)
+    lines[:, ROWS:] = jnp.zeros((16, 8, 128), F32)
     lane = lax.broadcasted_iota(jnp.int32, (1, 128), 1)
     shifts = {}
     for zl in range(2):
@@ -320,7 +320,7 @@
         + [pl.BlockSpec(memory_space=pl.ANY)] * 6,
         out_specs=pl.BlockSpec(memory_space=pltpu.VMEM),
         scratch_shapes=CONV_SCRATCH,
-        compiler_params=pltpu.CompilerParams(vmem_limit_bytes=24 * MIB),
+        compiler_params=pltpu.CompilerParams(vmem_limit_bytes=44 * MIB),
         name="conv",
     )(where, raw, branch_shift.reshape(1, 128), *own, *other)
 

time: 103 us -> 103 us (level)
  no operation moved by 1% of the time
where the time goes in v7:
time: 103 us; the launch traced here: 102 us
  waiting for transfers between devices  48.6 us (47%)
  starting transfers between devices  29.1 us (28%)
  Pallas kernels  17.8 us (17%)
  local copies, waits for them, and re-layouts  4.79 us (5%)
  other arithmetic  1.36 us (1%)
    all_to_all x1, waiting for transfers between devices, body(): arrived = lax.all_to_all(partial, ('zh', 'y', 'zl', 'x'), 0, 0, tiled=True)  27.6 us
    ppermute x1, waiting for transfers between devices, body(): lax.ppermute(picked, ('core', 'x'), [(c * 4 + i, c * 4 + (i - 1 + 2 * c)...  17.3 us
    pallas_call x1, Pallas kernels, body(): pl.pallas_call(_conv_kernel, out_shape=jax.ShapeDtypeStruct((64, ROWS, 12...  10.6 us
    all_to_all x1, starting transfers between devices, body(): raw = lax.all_to_all(messages, ('zh', 'y', 'zl', 'x'), 0, 0, tiled=True)  10.4 us
    all_to_all x1, starting transfers between devices, body(): arrived = lax.all_to_all(partial, ('zh', 'y', 'zl', 'x'), 0, 0, tiled=True)  9.13 us
    ppermute x1, starting transfers between devices, body(): lax.ppermute(picked, ('core', 'x'), [(c * 4 + i, c * 4 + (i - 1 + 2 * c)...  2.78 us
    reshape x1, local copies, waits for them, and re-layouts, body(): flat = features.transpose(1, 2, 0, 3).reshape(216, 2048)  2.4 us
    unnamed x22, local copies, waits for them, and re-layouts  2.22 us
  transfers between devices with their start and end apart: 9, of which 5 were waited for; matrix products, arithmetic and copies ran while one was open for 4% of the time, Pallas kernels for 4%

profile of v7, /device:TPU:0, one launch (start us, length us, event | category | flops | bytes accessed | tf_op | source)
XLA Modules:
  0.0 102.4 jit_solution(17069098813313640009)
XLA Ops:
  0.6 0.0 copy-start.2
  0.6 1.7 %weights.1 = bf16[28,32,128]{2,1,0:T(8,128)(2,1)} custom-call(bf16[27,32,128]{2,1,0:T(8,128)(2,1)} %bitcast.23, bf16[32,128]{1,0:T(8,128)(2,1)} %bitcast.24), custom_call_target="tpu_custom_call" | custom-call | tf_op jit(solution)/shard_map/weights/pallas_call | solution.py:278
  2.3 1.7 %collective-permute-start = (bf16[28,32,128]{2,1,0:T(8,128)(2,1)}, bf16[28,32,128]{2,1,0:T(8,128)(2,1)S(1)}, u32[]{:S(2)}, u32[]{:S(2)}) collective-permute-start(bf16[28,32,128]{2,1,0:T(8,128)(2,1)} %weights.1), channel_id=1, source_target_pairs={{0,16},{16,0},{32,48},{48,32},{1,17},{17,1},{33,49},{49,33},{2,18}... | collective-permute-start | bytes 688136 | tf_op jit(solution)/shard_map/ppermute | solution.py:283
  4.0 2.4 %reshape.20.f_ref = bf16[216,2048]{1,0:T(8,128)(2,1)S(1)} reshape(bf16[6,18,2,2048]{3,2,1,0:T(2,128)(2,1)} %bitcast.19) | data formatting | bytes 1769472 | tf_op jit(solution)/shard_map/reshape | solution.py:285
  6.4 1.9 %pack.1 = bf16[64,112,128]{2,1,0:T(8,128)(2,1)} custom-call(bf16[256,216]{1,0:T(8,128)(2,1)S(1)} %copy-done.2, bf16[216,2048]{1,0:T(8,128)(2,1)S(1)} %reshape.20.f_ref), custom_call_target="tpu_custom_call" | custom-call | tf_op jit(solution)/shard_map/pack/pallas_call | solution.py:286
  8.3 1.5 %collective-permute-done = bf16[28,32,128]{2,1,0:T(8,128)(2,1)S(1)} collective-permute-done((bf16[28,32,128]{2,1,0:T(8,128)(2,1)}, bf16[28,32,128]{2,1,0:T(8,128)(2,1)S(1)}, u32[]{:S(2)}, u32[]{:S(2)}) %collective-permute-start) | collective-permute-done | bytes 229408 | tf_op jit(solution)/shard_map/ppermute | solution.py:283
  9.8 1.7 %collective-permute-start.2 = (bf16[2,28,32,128]{3,2,1,0:T(8,128)(2,1)S(1)}, bf16[2,28,32,128]{3,2,1,0:T(8,128)(2,1)S(1)}, u32[]{:S(2)}, u32[]{:S(2)}) collective-permute-start(bf16[2,28,32,128]{3,2,1,0:T(8,128)(2,1)S(1)} %pad_maximum_fusion.1.refs_0_), channel_id=1, source_target_pairs={{0,1},{1,2},{2,3},{3,0},{4,5},{5,6},{6,7},{7,4},{8,9},{9,10},{10,1... | collective-permute-start | bytes 1376264 | tf_op jit(solution)/shard_map/ppermute | solution.py:300
  11.6 1.6 %collective-permute-start.1 = (bf16[2,28,32,128]{3,2,1,0:T(8,128)(2,1)S(1)}, bf16[2,28,32,128]{3,2,1,0:T(8,128)(2,1)S(1)}, u32[]{:S(2)}, u32[]{:S(2)}) collective-permute-start(bf16[2,28,32,128]{3,2,1,0:T(8,128)(2,1)S(1)} %pad_maximum_fusion.1.refs_0_), channel_id=1, source_target_pairs={{0,3},{1,0},{2,1},{3,2},{4,7},{5,4},{6,5},{7,6},{8,11},{9,8},{10,9... | collective-permute-start | bytes 1376264 | tf_op jit(solution)/shard_map/ppermute | solution.py:299
  13.1 10.4 %all-to-all-start = ((bf16[64,112,128]{2,1,0:T(8,128)(2,1)}), bf16[64,112,128]{2,1,0:T(8,128)(2,1)S(1)}, u32[]{:S(2)}, u32[]{:S(2)}) async-start(bf16[64,112,128]{2,1,0:T(8,128)(2,1)} %pack.1), calls=%async_computation | async-start | bytes 3670016 | tf_op jit(solution)/shard_map/all_to_all | solution.py:314
  23.5 0.0 collective-permute-done.2.b_ref
  23.5 0.0 collective-permute-done.1.a_ref
  23.6 0.7 copy-done.6
  24.3 0.2 copy-done.7
  24.5 2.0 %pick.1 = bf16[2,28,32,128]{3,2,1,0:T(8,128)(2,1)} custom-call(s32[1]{0:T(128)} %bitcast.1.core_ref, bf16[2,28,32,128]{3,2,1,0:T(8,128)(2,1)} %copy-done.7, bf16[2,28,32,128]{3,2,1,0:T(8,128)(2,1)} %copy-done.6), custom_call_target="tpu_custom_call" | custom-call | flops 20000000000 | bytes 1400000 | tf_op jit(solution)/shard_map/pick/pallas_call | solution.py:301
  26.4 2.8 %collective-permute-start.3 = (bf16[2,28,32,128]{3,2,1,0:T(8,128)(2,1)}, bf16[2,28,32,128]{3,2,1,0:T(8,128)(2,1)}, u32[]{:S(2)}, u32[]{:S(2)}) collective-permute-start(bf16[2,28,32,128]{3,2,1,0:T(8,128)(2,1)} %pick.1), channel_id=1, source_target_pairs={{0,3},{1,0},{2,1},{3,2},{8,9},{9,10},{10,11},{11,8},{4,7},{5,4},{6... | collective-permute-start | bytes 1376264 | tf_op jit(solution)/shard_map/ppermute | solution.py:308
  29.2 1.2 %pad_maximum_fusion.refs_1_ = bf16[2,2,28,32,128]{4,3,2,1,0:T(8,128)(2,1)S(1)} fusion(bf16[1,2,28,32,128]{4,3,2,1,0:T(8,128)(2,1)} %bitcast.20, bf16[1,2,28,32,128]{4,3,2,1,0:T(8,128)(2,1)} %bitcast.21), kind=kLoop, calls=%fused_computation | loop fusion | flops 458752 | bytes 1835008 | tf_op jit(solution)/shard_map/stack | solution.py:311
  30.5 0.1 collective-permute-start.5
  30.6 0.5 collective-permute-start.4
  31.0 17.3 %collective-permute-done.3.refs_2_ = bf16[2,28,32,128]{3,2,1,0:T(8,128)(2,1)} collective-permute-done((bf16[2,28,32,128]{3,2,1,0:T(8,128)(2,1)}, bf16[2,28,32,128]{3,2,1,0:T(8,128)(2,1)}, u32[]{:S(2)}, u32[]{:S(2)}) %collective-permute-start.3) | collective-permute-done | bytes 458784 | tf_op jit(solution)/shard_map/ppermute | solution.py:308
  48.3 1.2 %collective-permute-start.6 = (bf16[2,28,32,128]{3,2,1,0:T(8,128)(2,1)}, bf16[2,28,32,128]{3,2,1,0:T(8,128)(2,1)}, u32[]{:S(2)}, u32[]{:S(2)}) collective-permute-start(bf16[2,28,32,128]{3,2,1,0:T(8,128)(2,1)} %collective-permute-done.3.refs_2_), channel_id=1, source_target_pairs={{0,8},{8,0},{1,9},{9,1},{2,10},{10,2},{3,11},{11,3},{4,12},{12,4},... | collective-permute-start | bytes 1376264 | tf_op jit(solution)/shard_map/ppermute | solution.py:297
  49.5 0.1 reshape.22.shift_ref
  49.6 0.1 pad_add_fusion.where_ref
  49.7 0.0 collective-permute-done.4.refs_3_
  49.7 1.6 %collective-permute-done.6.refs_5_ = bf16[2,28,32,128]{3,2,1,0:T(8,128)(2,1)} collective-permute-done((bf16[2,28,32,128]{3,2,1,0:T(8,128)(2,1)}, bf16[2,28,32,128]{3,2,1,0:T(8,128)(2,1)}, u32[]{:S(2)}, u32[]{:S(2)}) %collective-permute-start.6) | collective-permute-done | bytes 458784 | tf_op jit(solution)/shard_map/ppermute | solution.py:297
  51.3 0.6 all-to-all-done.raw_ref
  51.9 10.6 %conv.1 = bf16[64,112,128]{2,1,0:T(8,128)(2,1)S(1)} custom-call(s32[3]{0:T(128)S(1)} %pad_add_fusion.where_ref, bf16[64,112,128]{2,1,0:T(8,128)(2,1)S(1)} %all-to-all-done.raw_ref, f32[1,128]{1,0:T(1,128)S(1)} %reshape.22.shift_ref, bf16[2,28,32,128]{3,2,1,0:T(8,128)(2,1)S(1)} %pad_maximum_fusion.1.refs_0_, ...), custom_call_target="tpu_custom_call" | custom-call | tf_op jit(solution)/shard_map/conv/pallas_call | solution.py:315
  62.5 1.3 %copy-done = bf16[64,112,128]{2,1,0:T(8,128)(2,1)} copy-done((bf16[64,112,128]{2,1,0:T(8,128)(2,1)}, bf16[64,112,128]{2,1,0:T(8,128)(2,1)S(1)}, u32[]{:S(2)}) %copy-start) | copy-done | bytes 1835032
  63.8 0.0 copy-start.4
  63.8 9.1 %all-to-all-start.1 = ((bf16[64,112,128]{2,1,0:T(8,128)(2,1)}), bf16[64,112,128]{2,1,0:T(8,128)(2,1)S(1)}, u32[]{:S(2)}, u32[]{:S(2)}) async-start(bf16[64,112,128]{2,1,0:T(8,128)(2,1)} %copy-done), calls=%async_computation.1 | async-start | bytes 3670016 | tf_op jit(solution)/shard_map/all_to_all | solution.py:327
  72.9 0.1 reshape.23.lab_ref
  73.0 27.6 %all-to-all-done.1.in_ref = bf16[64,112,128]{2,1,0:T(8,128)(2,1)S(1)} async-done(((bf16[64,112,128]{2,1,0:T(8,128)(2,1)}), bf16[64,112,128]{2,1,0:T(8,128)(2,1)S(1)}, u32[]{:S(2)}, u32[]{:S(2)}) %all-to-all-start.1) | async-done | bytes 1835040 | tf_op jit(solution)/shard_map/all_to_all | solution.py:327
  100.7 1.7 %final.1 = (bf16[108,2,256]{2,1,0:T(2,128)(2,1)}, f32[6,2,18]{2,1,0:T(2,128)}) custom-call(bf16[64,112,128]{2,1,0:T(8,128)(2,1)S(1)} %all-to-all-done.1.in_ref, bf16[1024,256]{1,0:T(8,128)(2,1)S(1)} %copy-done.1, bf16[8,256]{1,0:T(8,128)(2,1)S(1)} %concatenate.3.cls_ref, s32[1,216]{1,0:T(1,128)S(1)} %reshape.23.lab_ref, bf16[2,108,256]{2,1,0:T(8,128)(2,1)S(1)} %copy-done.3, ...), custom_call_target="tpu_custom_call" | custom-call | tf_op jit(solution)/shard_map/final/pallas_call | solution.py:330
  (20 shorter events, 0.1 us)
Async XLA Ops:
  0.6 5.8 %copy-start.2 = (bf16[256,216]{1,0:T(8,128)(2,1)S(1)}, bf16[256,216]{1,0:T(8,128)(2,1)}, u32[]{:S(2)}) copy-start(bf16[256,216]{1,0:T(8,128)(2,1)} %constant.34.clone.p_ref) | copy-start | bytes 331780
  2.3 7.5 %collective-permute-start = (bf16[28,32,128]{2,1,0:T(8,128)(2,1)}, bf16[28,32,128]{2,1,0:T(8,128)(2,1)S(1)}, u32[]{:S(2)}, u32[]{:S(2)}) collective-permute-start(bf16[28,32,128]{2,1,0:T(8,128)(2,1)} %weights.1), channel_id=1, source_target_pairs={{0,16},{16,0},{32,48},{48,32},{1,17},{17,1},{33,49},{49,33},{2,18}... | collective-permute-start | bytes 688136 | tf_op jit(solution)/shard_map/ppermute | solution.py:283
  6.4 3.4 %copy-start.5 = (bf16[28,32,128]{2,1,0:T(8,128)(2,1)S(1)}, bf16[28,32,128]{2,1,0:T(8,128)(2,1)}, u32[]{:S(2)}) copy-start(bf16[28,32,128]{2,1,0:T(8,128)(2,1)} %weights.1) | copy-start | bytes 688132
  9.8 13.7 %collective-permute-start.2 = (bf16[2,28,32,128]{3,2,1,0:T(8,128)(2,1)S(1)}, bf16[2,28,32,128]{3,2,1,0:T(8,128)(2,1)S(1)}, u32[]{:S(2)}, u32[]{:S(2)}) collective-permute-start(bf16[2,28,32,128]{3,2,1,0:T(8,128)(2,1)S(1)} %pad_maximum_fusion.1.refs_0_), channel_id=1, source_target_pairs={{0,1},{1,2},{2,3},{3,0},{4,5},{5,6},{6,7},{7,4},{8,9},{9,10},{10,1... | collective-permute-start | bytes 1376264 | tf_op jit(solution)/shard_map/ppermute | solution.py:300
  11.6 12.0 %collective-permute-start.1 = (bf16[2,28,32,128]{3,2,1,0:T(8,128)(2,1)S(1)}, bf16[2,28,32,128]{3,2,1,0:T(8,128)(2,1)S(1)}, u32[]{:S(2)}, u32[]{:S(2)}) collective-permute-start(bf16[2,28,32,128]{3,2,1,0:T(8,128)(2,1)S(1)} %pad_maximum_fusion.1.refs_0_), channel_id=1, source_target_pairs={{0,3},{1,0},{2,1},{3,2},{4,7},{5,4},{6,5},{7,6},{8,11},{9,8},{10,9... | collective-permute-start | bytes 1376264 | tf_op jit(solution)/shard_map/ppermute | solution.py:299
  13.1 38.7 %all-to-all-start = ((bf16[64,112,128]{2,1,0:T(8,128)(2,1)}), bf16[64,112,128]{2,1,0:T(8,128)(2,1)S(1)}, u32[]{:S(2)}, u32[]{:S(2)}) async-start(bf16[64,112,128]{2,1,0:T(8,128)(2,1)} %pack.1), calls=%async_computation | async-start | bytes 3670016 | tf_op jit(solution)/shard_map/all_to_all | solution.py:314
  23.5 0.8 copy-start.6
  23.6 0.9 copy-start.7
  26.4 23.1 %copy-start.9 = (f32[4,32]{1,0:T(4,128)S(1)}, f32[4,32]{1,0:T(4,128)}, u32[]{:S(2)}) copy-start(f32[4,32]{1,0:T(4,128)} %param.13) | copy-start | bytes 1540
  26.4 21.9 %collective-permute-start.3 = (bf16[2,28,32,128]{3,2,1,0:T(8,128)(2,1)}, bf16[2,28,32,128]{3,2,1,0:T(8,128)(2,1)}, u32[]{:S(2)}, u32[]{:S(2)}) collective-permute-start(bf16[2,28,32,128]{3,2,1,0:T(8,128)(2,1)} %pick.1), channel_id=1, source_target_pairs={{0,3},{1,0},{2,1},{3,2},{8,9},{9,10},{10,11},{11,8},{4,7},{5,4},{6... | collective-permute-start | bytes 1376264 | tf_op jit(solution)/shard_map/ppermute | solution.py:308
  30.5 19.2 %collective-permute-start.5 = (bf16[2,2,28,32,128]{4,3,2,1,0:T(8,128)(2,1)S(1)}, bf16[2,2,28,32,128]{4,3,2,1,0:T(8,128)(2,1)}, u32[]{:S(2)}, u32[]{:S(2)}) collective-permute-start(bf16[2,2,28,32,128]{4,3,2,1,0:T(8,128)(2,1)S(1)} %pad_maximum_fusion.refs_1_), channel_id=1, source_target_pairs={{0,8},{8,0},{1,9},{9,1},{2,10},{10,2},{3,11},{11,3},{4,12},{12,4},... | collective-permute-start | bytes 2752520 | tf_op jit(solution)/shard_map/ppermute | solution.py:297
  30.6 19.1 %collective-permute-start.4 = (bf16[2,28,32,128]{3,2,1,0:T(8,128)(2,1)S(1)}, bf16[2,28,32,128]{3,2,1,0:T(8,128)(2,1)}, u32[]{:S(2)}, u32[]{:S(2)}) collective-permute-start(bf16[2,28,32,128]{3,2,1,0:T(8,128)(2,1)S(1)} %pad_maximum_fusion.1.refs_0_), channel_id=1, source_target_pairs={{0,8},{8,0},{1,9},{9,1},{2,10},{10,2},{3,11},{11,3},{4,12},{12,4},... | collective-permute-start | bytes 1376264 | tf_op jit(solution)/shard_map/ppermute | solution.py:297
  48.3 3.0 %collective-permute-start.6 = (bf16[2,28,32,128]{3,2,1,0:T(8,128)(2,1)}, bf16[2,28,32,128]{3,2,1,0:T(8,128)(2,1)}, u32[]{:S(2)}, u32[]{:S(2)}) collective-permute-start(bf16[2,28,32,128]{3,2,1,0:T(8,128)(2,1)} %collective-permute-done.3.refs_2_), channel_id=1, source_target_pairs={{0,8},{8,0},{1,9},{9,1},{2,10},{10,2},{3,11},{11,3},{4,12},{12,4},... | collective-permute-start | bytes 1376264 | tf_op jit(solution)/shard_map/ppermute | solution.py:297
  62.5 1.3 %copy-start = (bf16[64,112,128]{2,1,0:T(8,128)(2,1)}, bf16[64,112,128]{2,1,0:T(8,128)(2,1)S(1)}, u32[]{:S(2)}) copy-start(bf16[64,112,128]{2,1,0:T(8,128)(2,1)S(1)} %conv.1) | copy-start | bytes 5505028
  63.7 9.2 %copy-start.8 = (s32[2,6,18]{2,0,1:T(2,128)S(1)}, s32[2,6,18]{2,0,1:T(2,128)}, u32[]{:S(2)}) copy-start(s32[2,6,18]{2,0,1:T(2,128)} %param.16) | copy-start | bytes 2596
  63.7 9.3 %copy-start.10 = (bf16[256,3]{0,1:T(4,128)(2,1)S(1)}, bf16[256,3]{0,1:T(4,128)(2,1)}, u32[]{:S(2)}) copy-start(bf16[256,3]{0,1:T(4,128)(2,1)} %param.15) | copy-start | bytes 4612
  63.8 36.9 %copy-start.1 = (bf16[1024,256]{1,0:T(8,128)(2,1)S(1)}, bf16[1024,256]{1,0:T(8,128)(2,1)}, u32[]{:S(2)}) copy-start(bf16[1024,256]{1,0:T(8,128)(2,1)} %proj_ref.1) | copy-start | bytes 1572868
  63.8 36.9 %copy-start.3 = (bf16[2,108,256]{2,1,0:T(8,128)(2,1)S(1)}, bf16[2,108,256]{2,1,0:T(8,128)(2,1)}, u32[]{:S(2)}) copy-start(bf16[2,108,256]{2,1,0:T(8,128)(2,1)} %constant.35.clone.u_ref) | copy-start | bytes 331780
  63.8 36.9 %copy-start.4 = (bf16[216,256]{1,0:T(8,128)(2,1)S(1)}, bf16[216,256]{1,0:T(8,128)(2,1)}, u32[]{:S(2)}) copy-start(bf16[216,256]{1,0:T(8,128)(2,1)} %constant.36.clone.v_ref) | copy-start | bytes 331780
  63.8 36.9 %all-to-all-start.1 = ((bf16[64,112,128]{2,1,0:T(8,128)(2,1)}), bf16[64,112,128]{2,1,0:T(8,128)(2,1)S(1)}, u32[]{:S(2)}, u32[]{:S(2)}) async-start(bf16[64,112,128]{2,1,0:T(8,128)(2,1)} %copy-done), calls=%async_computation.1 | async-start | bytes 3670016 | tf_op jit(solution)/shard_map/all_to_all | solution.py:327
